TPU v7x, 32 devices: a whole 2x2x4 slice. The times are simulated.
32 devices in a mesh: dp: 4 (over x, core), seq: 8 (over z, y).
Axes of the slice: x: 2, y: 2, z: 4, core: 2. Of those that a mesh axis runs over, the one named last changes fastest.
Arguments:
- tokens: bfloat16 [12, 1024, 1536], P('dp', 'seq'), may hold values from -6 to 6
- cotangent: bfloat16 [12, 1024, 1536], P('dp', 'seq'), may hold values from -6 to 6
- lengths: int32 [12], P('dp'), may hold values from 256 to 1024, as said below
- in_weight: bfloat16 [1536, 4608], P(('dp', 'seq')), may hold values from -0.15625 to 0.15625
- conv_weight: bfloat16 [3, 1536], P(None, ('dp', 'seq')), may hold values from -3 to 3
- out_weight: bfloat16 [1536, 1536], P(('dp', 'seq')), may hold values from -0.15625 to 0.15625
- gain_one: bfloat16 [1536], P(('dp', 'seq')), may hold values from 0.099609375 to 1.8984375
- gain_two: bfloat16 [1536], P(('dp', 'seq')), may hold values from 0.099609375 to 1.8984375
- gate_weight: bfloat16 [1536, 6912], P(('dp', 'seq')), may hold values from -0.15625 to 0.15625
- up_weight: bfloat16 [1536, 6912], P(('dp', 'seq')), may hold values from -0.15625 to 0.15625
- down_weight: bfloat16 [6912, 1536], P(('dp', 'seq')), may hold values from -0.15625 to 0.15625
Outputs:
- mixed: bfloat16 [12, 1024, 1536], P('dp', 'seq')
- input_grad: float32 [12, 1024, 1536], P('dp', 'seq')
- in_grad: float32 [1536, 4608], P(('dp', 'seq'))
- conv_grad: float32 [3, 1536], P(None, ('dp', 'seq'))
- out_grad: float32 [1536, 1536], P(('dp', 'seq'))
- gain_one_grad: float32 [1536], P(('dp', 'seq'))
- gain_two_grad: float32 [1536], P(('dp', 'seq'))
- gate_grad: float32 [1536, 6912], P(('dp', 'seq'))
- up_grad: float32 [1536, 6912], P(('dp', 'seq'))
- down_grad: float32 [6912, 1536], P(('dp', 'seq'))
Inputs may be any that keep to these rules, and one draw needn't show every extreme that they name: `lengths`: each slot's length is between 256 and 1024; in each aligned block of 3 slots one slot has length 1024.
All inputs are finite; a program needn't handle non-finite values.
Results may differ from a plain program's by a relative error of at most 0.0098.
Values may be sent and summed in bfloat16 or wider, within the bound.
No kernel may reach another device: no remote copies, remote signals or barrier semaphores. Data moves between devices by JAX's collectives and lax.ppermute only.
A program may use at most 512 MiB of HBM per device.

v0:
```python
import jax
import jax.numpy as jnp
from jax import lax
from jax.sharding import PartitionSpec as P

MICRO = 3


def shifted(block, axis, distance):
    devices = range(lax.axis_size(axis))
    route = [(i - distance, i) for i in devices if i - distance in devices]
    return lax.ppermute(block, axis, route)


def rms_scale(values):
    return lax.rsqrt(jnp.mean(values * values, axis=-1, keepdims=True) + 1e-05)


def norm_back(input_weight_gradient, values, scale, gain):
    scaled = input_weight_gradient * gain
    mean_term = jnp.mean(scaled * values, axis=-1, keepdims=True)
    gain_term = jnp.sum(input_weight_gradient * values * scale, axis=(0, 1))
    return (scale * scaled - values * scale * scale * scale * mean_term, gain_term)


def fetch_weights(shards):
    return (
        lax.all_gather(shards[0], ("dp", "seq"), axis=0, tiled=True),
        lax.all_gather(shards[1], ("dp", "seq"), axis=1, tiled=True),
        lax.all_gather(shards[2], ("dp", "seq"), axis=0, tiled=True),
        lax.all_gather(shards[3], ("dp", "seq"), axis=0, tiled=True),
        lax.all_gather(shards[4], ("dp", "seq"), axis=0, tiled=True),
        lax.all_gather(shards[5], ("dp", "seq"), axis=0, tiled=True),
        lax.all_gather(shards[6], ("dp", "seq"), axis=0, tiled=True),
        lax.all_gather(shards[7], ("dp", "seq"), axis=0, tiled=True),
    )


def on_device(
    tokens,
    cotangent,
    lengths,
    in_weight,
    conv_weight,
    out_weight,
    gain_one,
    gain_two,
    gate_weight,
    up_weight,
    down_weight,
):
    slots_here, seq_dev, width = tokens.shape
    hidden = gate_weight.shape[1]
    per_batch = slots_here // MICRO
    first = lax.axis_index("seq") * seq_dev
    positions = first + jnp.arange(seq_dev, dtype=jnp.int32)
    shards = (
        in_weight,
        conv_weight,
        out_weight,
        gain_one,
        gain_two,
        gate_weight,
        up_weight,
        down_weight,
    )
    small_totals = (
        jnp.zeros((width,), jnp.float32),
        jnp.zeros((width,), jnp.float32),
        jnp.zeros((3, width), jnp.float32),
    )
    outputs = []
    grads_in = []
    kept_first = []
    kept_triple = []
    kept_branch = []
    kept_mixer = []
    kept_second = []
    kept_gate = []
    kept_upward = []
    kept_inner = []
    kept_seed = []
    for batch in range(MICRO):
        low_row = batch * per_batch
        inputs = tokens[low_row : low_row + per_batch].astype(jnp.float32)
        seeds = cotangent[low_row : low_row + per_batch].astype(jnp.float32)
        slot_len = lengths[low_row : low_row + per_batch]
        mask = (positions[None, :] < slot_len[:, None]).astype(jnp.float32)[:, :, None]
        full = fetch_weights(shards)
        (
            input_matrix,
            w_conv,
            output_matrix,
            g_one,
            g_two,
            gate_matrix,
            upward_matrix,
            down_matrix,
        ) = full
        taps = w_conv.astype(jnp.float32)
        gain_a = g_one.astype(jnp.float32)
        gain_b = g_two.astype(jnp.float32)
        scale_one = rms_scale(inputs)
        first_normalized = (inputs * scale_one * gain_a).astype(jnp.bfloat16)
        projected_triple = jnp.einsum(
            "puy,yw->puw", first_normalized, input_matrix, preferred_element_type=jnp.float32
        )
        b_part = projected_triple[:, :, :width]
        c_part = projected_triple[:, :, width : 2 * width]
        x_part = projected_triple[:, :, 2 * width :]
        mixed_bx = b_part * x_part
        before = shifted(mixed_bx[:, -2:, :], "seq", 1)
        padded = jnp.concatenate([before, mixed_bx], axis=1)
        conv = taps[0] * padded[:, :-2] + taps[1] * padded[:, 1:-1] + taps[2] * padded[:, 2:]
        residual_branch = (c_part * conv).astype(jnp.bfloat16)
        mixer_output = jnp.einsum(
            "puy,yw->puw", residual_branch, output_matrix, preferred_element_type=jnp.float32
        )
        hidden_one = inputs + mixer_output
        scale_two = rms_scale(hidden_one)
        second_normalized = (hidden_one * scale_two * gain_b).astype(jnp.bfloat16)
        gate_activation = jnp.einsum(
            "rev,vw->rew", second_normalized, gate_matrix, preferred_element_type=jnp.float32
        )
        upward_activation = jnp.einsum(
            "rev,vw->rew", second_normalized, upward_matrix, preferred_element_type=jnp.float32
        )
        sigma = jax.nn.sigmoid(gate_activation)
        activ = gate_activation * sigma
        inner_product = (activ * upward_activation).astype(jnp.bfloat16)
        feedforward_output = jnp.einsum(
            "njc,cx->njx", inner_product, down_matrix, preferred_element_type=jnp.float32
        )
        outputs.append((mask * (hidden_one + feedforward_output)).astype(jnp.bfloat16))
        back = (
            lax.all_gather(in_weight, ("dp", "seq"), axis=0, tiled=True),
            lax.all_gather(conv_weight, ("dp", "seq"), axis=1, tiled=True),
            lax.all_gather(out_weight, ("dp", "seq"), axis=0, tiled=True),
            lax.all_gather(gain_one, ("dp", "seq"), axis=0, tiled=True),
            lax.all_gather(gain_two, ("dp", "seq"), axis=0, tiled=True),
            lax.all_gather(gate_weight, ("dp", "seq"), axis=0, tiled=True),
            lax.all_gather(up_weight, ("dp", "seq"), axis=0, tiled=True),
            lax.all_gather(down_weight, ("dp", "seq"), axis=0, tiled=True),
        )
        input_bias, b_conv, output_bias, b_one, b_two, gate_bias, upward_bias, down_bias = back
        taps_back = b_conv.astype(jnp.float32)
        d_out = mask * seeds
        feedforward_grad = d_out.astype(jnp.bfloat16)
        inner_product_grad = jnp.einsum(
            "izo,yo->izy", feedforward_grad, down_bias, preferred_element_type=jnp.float32
        )
        gate_activation_grad = (
            inner_product_grad * upward_activation * sigma * (1.0 + gate_activation * (1.0 - sigma))
        ).astype(jnp.bfloat16)
        upward_grad = (inner_product_grad * activ).astype(jnp.bfloat16)
        second_norm_grad = jnp.einsum(
            "gao,eo->gae", gate_activation_grad, gate_bias, preferred_element_type=jnp.float32
        )
        second_norm_grad = second_norm_grad + jnp.einsum(
            "gao,eo->gae", upward_grad, upward_bias, preferred_element_type=jnp.float32
        )
        through_two, grad_gain_two = norm_back(
            second_norm_grad, hidden_one, scale_two, b_two.astype(jnp.float32)
        )
        d_hidden = d_out + through_two
        mixer_output_grad = d_hidden.astype(jnp.bfloat16)
        residual_branch_grad = jnp.einsum(
            "bgt,pt->bgp", mixer_output_grad, output_bias, preferred_element_type=jnp.float32
        )
        d_c = residual_branch_grad * conv
        d_conv = residual_branch_grad * c_part
        after = shifted(d_conv[:, :2, :], "seq", -1)
        padded_grad = jnp.concatenate([d_conv, after], axis=1)
        d_bx = (
            taps_back[2] * padded_grad[:, :-2]
            + taps_back[1] * padded_grad[:, 1:-1]
            + taps_back[0] * padded_grad[:, 2:]
        )
        grad_conv = jnp.stack(
            [
                jnp.sum(d_conv * padded[:, :-2], axis=(0, 1)),
                jnp.sum(d_conv * padded[:, 1:-1], axis=(0, 1)),
                jnp.sum(d_conv * padded[:, 2:], axis=(0, 1)),
            ],
            axis=0,
        )
        projected_triple_grad = jnp.concatenate(
            [d_bx * x_part, d_c, d_bx * b_part], axis=-1
        ).astype(jnp.bfloat16)
        first_norm_grad = jnp.einsum(
            "bgt,pt->bgp", projected_triple_grad, input_bias, preferred_element_type=jnp.float32
        )
        through_one, grad_gain_one = norm_back(
            first_norm_grad, inputs, scale_one, b_one.astype(jnp.float32)
        )
        grads_in.append(d_hidden + through_one)
        small_totals = (
            small_totals[0] + grad_gain_one,
            small_totals[1] + grad_gain_two,
            small_totals[2] + grad_conv,
        )
        kept_first.append(first_normalized)
        kept_triple.append(projected_triple_grad)
        kept_branch.append(residual_branch)
        kept_mixer.append(mixer_output_grad)
        kept_second.append(second_normalized)
        kept_gate.append(gate_activation_grad)
        kept_upward.append(upward_grad)
        kept_inner.append(inner_product)
        kept_seed.append(feedforward_grad)
    first_all = jnp.concatenate(kept_first, axis=0)
    triple_all = jnp.concatenate(kept_triple, axis=0)
    branch_all = jnp.concatenate(kept_branch, axis=0)
    mixer_all = jnp.concatenate(kept_mixer, axis=0)
    second_all = jnp.concatenate(kept_second, axis=0)
    gate_all = jnp.concatenate(kept_gate, axis=0)
    upward_all = jnp.concatenate(kept_upward, axis=0)
    inner_all = jnp.concatenate(kept_inner, axis=0)
    seed_all = jnp.concatenate(kept_seed, axis=0)
    joined = lax.psum_scatter(
        jnp.concatenate(
            [
                jnp.einsum(
                    "stc,stw->cw", first_all, triple_all, preferred_element_type=jnp.float32
                ),
                jnp.einsum(
                    "stc,stw->cw", branch_all, mixer_all, preferred_element_type=jnp.float32
                ),
                jnp.einsum("stc,stw->cw", second_all, gate_all, preferred_element_type=jnp.float32),
                jnp.einsum(
                    "stc,stw->cw", second_all, upward_all, preferred_element_type=jnp.float32
                ),
            ],
            axis=1,
        ),
        ("dp", "seq"),
        scatter_dimension=0,
        tiled=True,
    )
    down_part = lax.psum_scatter(
        jnp.einsum("stc,stw->cw", inner_all, seed_all, preferred_element_type=jnp.float32),
        ("dp", "seq"),
        scatter_dimension=0,
        tiled=True,
    )
    small = (
        lax.psum_scatter(small_totals[0], ("dp", "seq"), scatter_dimension=0, tiled=True),
        lax.psum_scatter(small_totals[1], ("dp", "seq"), scatter_dimension=0, tiled=True),
        lax.psum_scatter(small_totals[2], ("dp", "seq"), scatter_dimension=1, tiled=True),
    )
    in_part = joined[:, : 3 * width]
    out_part = joined[:, 3 * width : 4 * width]
    gate_part = joined[:, 4 * width : 4 * width + hidden]
    upward_part = joined[:, 4 * width + hidden :]
    mixed = jnp.concatenate(outputs, axis=0)
    input_grad = jnp.concatenate(grads_in, axis=0)
    return (
        mixed,
        input_grad,
        in_part,
        small[2],
        out_part,
        small[0],
        small[1],
        gate_part,
        upward_part,
        down_part,
    )


def solution(mesh):
    in_specs = (
        P("dp", "seq", None),
        P("dp", "seq", None),
        P("dp"),
        P(("dp", "seq"), None),
        P(None, ("dp", "seq")),
        P(("dp", "seq"), None),
        P(("dp", "seq")),
        P(("dp", "seq")),
        P(("dp", "seq"), None),
        P(("dp", "seq"), None),
        P(("dp", "seq"), None),
    )
    out_specs = (
        P("dp", "seq", None),
        P("dp", "seq", None),
        P(("dp", "seq"), None),
        P(None, ("dp", "seq")),
        P(("dp", "seq"), None),
        P(("dp", "seq")),
        P(("dp", "seq")),
        P(("dp", "seq"), None),
        P(("dp", "seq"), None),
        P(("dp", "seq"), None),
    )
    return jax.shard_map(
        on_device, mesh=mesh, in_specs=in_specs, out_specs=out_specs, check_vma=False
    )
```

profile of v0, /device:TPU:0, one launch (start us, length us, event | category | flops | bytes accessed | tf_op | source)
XLA Modules:
  0.0 2294.1 jit_solution(424298632156989457)
XLA Ops:
  12.3 43.3 %all-reduce.5 = (bf16[1536]{0:T(1024)(128)(2,1)S(1)}, bf16[1536]{0:T(1024)(128)(2,1)S(1)}) all-reduce(bf16[1536]{0:T(1024)(128)(2,1)S(1)} %dynamic-update-slice, bf16[1536]{0:T(1024)(128)(2,1)S(1)} %dynamic-update-slice.1), channel_id=1, replica_groups=mesh['dp'=4,'seq'=8] {'dp','seq'}, use_global_device_ids=true, to_apply=%add | all-reduce | flops 3072 | bytes 12288
  56.3 66.5 %all-gather = bf16[32,48,3]{1,2,0:T(4,128)(2,1)S(1)} all-gather(bf16[1,48,3]{1,2,0:T(4,128)(2,1)} %bitcast.281), channel_id=1, replica_groups=mesh['dp'=4,'seq'=8] {'dp','seq'}, dimensions={0}, use_global_device_ids=true | all-gather | bytes 9504 | tf_op jit(solution)/shard_map/all_gather | solution.py:29
  153.0 29.8 %all-gather.9.cloned.1.call-done = bf16[1536,1536]{1,0:T(8,128)(2,1)} async-done(((bf16[48,1536]{1,0:T(8,128)(2,1)}), bf16[1536,1536]{1,0:T(8,128)(2,1)}) %all-gather.9.cloned.1.call-update) | async-done | bytes 4718608 | tf_op jit(solution)/shard_map/all_gather | solution.py:30
  192.4 128.0 %all-gather.13.cloned.1.call-done = bf16[1536,6912]{1,0:T(8,128)(2,1)} async-done(((bf16[48,6912]{1,0:T(8,128)(2,1)}), bf16[1536,6912]{1,0:T(8,128)(2,1)}) %all-gather.13.cloned.1.call-update) | async-done | bytes 21233680 | tf_op jit(solution)/shard_map/all_gather | solution.py:34
  320.4 11.8 fusion.172
  332.2 125.0 %all-gather.11.cloned.1.call-done = bf16[1536,6912]{1,0:T(8,128)(2,1)} async-done(((bf16[48,6912]{1,0:T(8,128)(2,1)}), bf16[1536,6912]{1,0:T(8,128)(2,1)}) %all-gather.11.cloned.1.call-update) | async-done | bytes 21233680 | tf_op jit(solution)/shard_map/all_gather | solution.py:33
  457.2 11.7 fusion.174
  468.9 125.1 %all-gather.15.cloned.1.call-done = bf16[6912,1536]{1,0:T(8,128)(2,1)} async-done(((bf16[216,1536]{1,0:T(8,128)(2,1)}), bf16[6912,1536]{1,0:T(8,128)(2,1)}) %all-gather.15.cloned.1.call-update) | async-done | bytes 21233680 | tf_op jit(solution)/shard_map/all_gather | solution.py:35
  594.0 14.1 multiply_convert_fusion.4
  608.2 11.6 fusion.198
  619.9 13.3 fusion.141
  633.7 11.7 fusion.166
  645.4 12.0 fusion.168
  657.4 12.0 fusion.160
  674.1 14.4 multiply_convert_fusion.2
  688.5 12.3 fusion.199
  700.8 14.1 multiply_convert_fusion
  726.5 11.7 convolution_add_fusion
  738.2 13.5 fusion.139
  781.8 20.7 convolution_bitcast_fusion.1
  802.5 20.4 convolution_bitcast_fusion
  830.6 13.8 convolution_bitcast_fusion.3
  844.4 81.1 %pad_maximum_fusion = f32[1536,19968]{1,0:T(8,128)} fusion(f32[1536,6912]{1,0:T(8,128)} %convolution_bitcast_fusion, f32[1536,6912]{1,0:T(8,128)} %convolution_bitcast_fusion.1, f32[1536,1536]{1,0:T(8,128)} %convolution_bitcast_fusion.4, f32[1536,4608]{1,0:T(8,128)} %convolution_bitcast_fusion.3), kind=kLoop, calls=%fused_computation | loop fusion | flops 92012544 | bytes 245366784 | tf_op jit(solution)/shard_map/concatenate | solution.py:221
  927.2 29.5 %convolution_bitcast_fusion.2 = f32[6912,1536]{1,0:T(8,128)} fusion(bf16[1,128,6912]{2,1,0:T(8,128)(2,1)} %bitcast.268, bf16[1,128,6912]{2,1,0:T(8,128)(2,1)} %bitcast.267, bf16[1,128,6912]{2,1,0:T(8,128)(2,1)S(1)} %bitcast.266, bf16[1,128,1536]{2,1,0:T(8,128)(2,1)S(1)} %copy-done.56, bf16[1,128,1536]{2,1,0:T(8,128)(2,1)S(1)} %copy-done.58, ...), kind=kOutput, calls=%fused_computation.3 | convolution fusion | flops 8160215040 | bytes 48955392 | tf_op jit(solution)/shard_map/stc,stw->cw/dot_general | solution.py:241
  958.0 15.9 fusion.46
  974.0 18.3 fusion.45
  999.4 13.4 fusion.53
  1012.9 14.3 fusion.47
  1027.3 15.0 fusion.132
  1042.9 46.0 %all-reduce.4 = (f32[1536]{0:T(1024)}, f32[1536]{0:T(1024)}) all-reduce(f32[1536]{0:T(1024)} %add_add_fusion.1, f32[1536]{0:T(1024)S(1)} %add_add_fusion), channel_id=4, replica_groups=mesh['dp'=4,'seq'=8] {'dp','seq'}, use_global_device_ids=true, to_apply=%region_26.0.clone | all-reduce | flops 3072 | bytes 24576
  1098.8 802.0 %reduce-scatter.6.cloned.1.call-done = f32[48,19968]{1,0:T(8,128)} async-done(((f32[1536,19968]{1,0:T(8,128)}), f32[48,19968]{1,0:T(8,128)}) %reduce-scatter.6.cloned.1.call-update) | async-done | bytes 3833872 | tf_op jit(solution)/shard_map/reduce_scatter | solution.py:220
  1908.0 379.1 %reduce-scatter.8.cloned.1.call-done = f32[216,1536]{1,0:T(8,128)} async-done(((f32[6912,1536]{1,0:T(8,128)}), f32[216,1536]{1,0:T(8,128)}) %reduce-scatter.8.cloned.1.call-update) | async-done | bytes 1327120 | tf_op jit(solution)/shard_map/reduce_scatter | solution.py:240
  (372 shorter events, 126.9 us)
Async XLA Ops:
  7.2 119.7 %copy-start.13 = (bf16[3,128,1536]{2,1,0:T(8,128)(2,1)S(1)}, bf16[3,128,1536]{2,1,0:T(8,128)(2,1)}, u32[]{:S(2)}) copy-start(bf16[3,128,1536]{2,1,0:T(8,128)(2,1)} %param.11) | copy-start | bytes 3538948
  7.2 120.1 %copy-start.31 = (bf16[3,128,1536]{2,1,0:T(8,128)(2,1)S(1)}, bf16[3,128,1536]{2,1,0:T(8,128)(2,1)}, u32[]{:S(2)}) copy-start(bf16[3,128,1536]{2,1,0:T(8,128)(2,1)} %param.12) | copy-start | bytes 3538948
  7.2 121.8 %all-gather.7.cloned.1.call-start = ((), (), s32[]{:S(2)}) async-start(), calls=%async_computation.3 | async-start | bytes 14598144 | tf_op jit(solution)/shard_map/all_gather | solution.py:28
  7.9 174.9 %all-gather.9.cloned.1.call-start = ((), (), s32[]{:S(2)}) async-start(), calls=%async_computation.4 | async-start | bytes 4866048 | tf_op jit(solution)/shard_map/all_gather | solution.py:30
  8.7 311.7 %all-gather.13.cloned.1.call-start = ((), (), s32[]{:S(2)}) async-start(), calls=%async_computation.6 | async-start | bytes 21897216 | tf_op jit(solution)/shard_map/all_gather | solution.py:34
  9.4 447.8 %all-gather.11.cloned.1.call-start = ((), (), s32[]{:S(2)}) async-start(), calls=%async_computation.5 | async-start | bytes 21897216 | tf_op jit(solution)/shard_map/all_gather | solution.py:33
  10.0 584.0 %all-gather.15.cloned.1.call-start = ((), (), s32[]{:S(2)}) async-start(), calls=%async_computation.7 | async-start | bytes 21897216 | tf_op jit(solution)/shard_map/all_gather | solution.py:35
  10.6 1086.8 %reduce-scatter.10.cloned.1.call-start = ((), (), s32[]{:S(2)}) async-start(), calls=%async_computation.10 | async-start | bytes 811008
  126.9 59.9 %copy-start.78 = (f32[1536]{0:T(1024)}, f32[1536]{0:T(1024)S(1)}, u32[]{:S(2)}) copy-start(f32[1536]{0:T(1024)S(1)} %get-tuple-element.38) | copy-start | bytes 18436
  136.5 50.4 %copy-start.3 = (f32[1,128,4608]{2,1,0:T(8,128)}, f32[1,128,4608]{2,1,0:T(8,128)S(1)}, u32[]{:S(2)}) copy-start(f32[1,128,4608]{2,1,0:T(8,128)S(1)} %convolution_bitcast_fusion.7) | copy-start | bytes 7077892
  137.2 49.7 %collective-permute-start = (f32[1,2,1536]{2,1,0:T(2,128)}, f32[1,2,1536]{2,1,0:T(2,128)}, u32[]{:S(2)}, u32[]{:S(2)}) collective-permute-start(f32[1,2,1536]{2,1,0:T(2,128)} %slice.197), channel_id=1, source_target_pairs={{0,1},{1,2},{2,3},{3,4},{4,5},{5,6},{6,7},{8,9},{9,10},{10,11},{11... | collective-permute-start | bytes 36872 | tf_op jit(solution)/shard_map/ppermute | solution.py:12
  142.3 9.4 collective-permute-start.2
  149.0 37.9 %collective-permute-start.1 = (f32[1,2,1536]{2,1,0:T(2,128)}, f32[1,2,1536]{2,1,0:T(2,128)}, u32[]{:S(2)}, u32[]{:S(2)}) collective-permute-start(f32[1,2,1536]{2,1,0:T(2,128)} %slice.205), channel_id=1, source_target_pairs={{0,1},{1,2},{2,3},{3,4},{4,5},{5,6},{6,7},{8,9},{9,10},{10,11},{11... | collective-permute-start | bytes 36872 | tf_op jit(solution)/shard_map/ppermute | solution.py:12
  151.8 31.0 %copy-start.88 = (f32[1,2,1536]{2,1,0:T(2,128)}, f32[1,2,1536]{2,1,0:T(2,128)S(1)}, u32[]{:S(2)}) copy-start(f32[1,2,1536]{2,1,0:T(2,128)S(1)} %collective-permute-done.2) | copy-start | bytes 36868
  153.0 36.9 %copy-start.38 = (bf16[1,128,1536]{2,1,0:T(8,128)(2,1)}, bf16[1,128,1536]{2,1,0:T(8,128)(2,1)S(1)}, u32[]{:S(2)}) copy-start(bf16[1,128,1536]{2,1,0:T(8,128)(2,1)S(1)} %get-tuple-element.64) | copy-start | bytes 1179652
  186.3 565.4 %copy-start.9 = (f32[1,128,1536]{2,1,0:T(8,128)}, f32[1,128,1536]{2,1,0:T(8,128)S(1)}, u32[]{:S(2)}) copy-start(f32[1,128,1536]{2,1,0:T(8,128)S(1)} %get-tuple-element.109) | copy-start | bytes 2359300
  190.8 561.0 %copy-start.7 = (f32[1,128,1536]{2,1,0:T(8,128)}, f32[1,128,1536]{2,1,0:T(8,128)S(1)}, u32[]{:S(2)}) copy-start(f32[1,128,1536]{2,1,0:T(8,128)S(1)} %get-tuple-element.105) | copy-start | bytes 2359300
  191.7 560.1 %copy-start.11 = (f32[1,128,1536]{2,1,0:T(8,128)}, f32[1,128,1536]{2,1,0:T(8,128)S(1)}, u32[]{:S(2)}) copy-start(f32[1,128,1536]{2,1,0:T(8,128)S(1)} %get-tuple-element.107) | copy-start | bytes 2359300
  192.4 264.8 %copy-start.19 = (bf16[1,128,1536]{2,1,0:T(8,128)(2,1)}, bf16[1,128,1536]{2,1,0:T(8,128)(2,1)S(1)}, u32[]{:S(2)}) copy-start(bf16[1,128,1536]{2,1,0:T(8,128)(2,1)S(1)} %multiply_convert_fusion.22) | copy-start | bytes 1179652
  332.2 261.8 %copy-start.53 = (bf16[1,128,1536]{2,1,0:T(8,128)(2,1)S(1)}, bf16[1,128,1536]{2,1,0:T(8,128)(2,1)}, u32[]{:S(2)}) copy-start(bf16[1,128,1536]{2,1,0:T(8,128)(2,1)} %get-tuple-element.87) | copy-start | bytes 1179652
  633.2 36.2 %copy-start.17 = (bf16[1,128,1536]{2,1,0:T(8,128)(2,1)}, bf16[1,128,1536]{2,1,0:T(8,128)(2,1)S(1)}, u32[]{:S(2)}) copy-start(bf16[1,128,1536]{2,1,0:T(8,128)(2,1)S(1)} %get-tuple-element.98) | copy-start | bytes 1179652
  760.5 64.6 %collective-permute-start.3 = (f32[1,2,1536]{2,1,0:T(2,128)}, f32[1,2,1536]{2,1,0:T(2,128)}, u32[]{:S(2)}, u32[]{:S(2)}) collective-permute-start(f32[1,2,1536]{2,1,0:T(2,128)} %slice.214), channel_id=1, source_target_pairs={{1,0},{2,1},{3,2},{4,3},{5,4},{6,5},{7,6},{9,8},{10,9},{11,10},{12... | collective-permute-start | bytes 36872 | tf_op jit(solution)/shard_map/ppermute | solution.py:12
  776.5 48.7 %collective-permute-start.4 = (f32[1,2,1536]{2,1,0:T(2,128)}, f32[1,2,1536]{2,1,0:T(2,128)}, u32[]{:S(2)}, u32[]{:S(2)}) collective-permute-start(f32[1,2,1536]{2,1,0:T(2,128)} %slice.217), channel_id=1, source_target_pairs={{1,0},{2,1},{3,2},{4,3},{5,4},{6,5},{7,6},{9,8},{10,9},{11,10},{12... | collective-permute-start | bytes 36872 | tf_op jit(solution)/shard_map/ppermute | solution.py:12
  777.8 45.0 %collective-permute-start.5 = (f32[1,2,1536]{2,1,0:T(2,128)}, f32[1,2,1536]{2,1,0:T(2,128)}, u32[]{:S(2)}, u32[]{:S(2)}) collective-permute-start(f32[1,2,1536]{2,1,0:T(2,128)} %slice.220), channel_id=1, source_target_pairs={{1,0},{2,1},{3,2},{4,3},{5,4},{6,5},{7,6},{9,8},{10,9},{11,10},{12... | collective-permute-start | bytes 36872 | tf_op jit(solution)/shard_map/ppermute | solution.py:12
  781.7 1119.0 %reduce-scatter.6.cloned.1.call-start = ((), (), s32[]{:S(2)}) async-start(), calls=%async_computation.8 | async-start | bytes 126517248 | tf_op jit(solution)/shard_map/reduce_scatter | solution.py:220
  925.5 1361.6 %reduce-scatter.8.cloned.1.call-start = ((), (), s32[]{:S(2)}) async-start(), calls=%async_computation.9 | async-start | bytes 43794432 | tf_op jit(solution)/shard_map/reduce_scatter | solution.py:240
  958.0 34.3 %slice-start.6 = ((s8[21233664]{0:T(1024)(128)(4,1)}), s8[4194304]{0:T(1024)(128)(4,1)S(1)}, s32[]{:S(2)}) async-start(s8[21233664]{0:T(1024)(128)(4,1)} %bitcast.254), calls=%async_computation.17 | async-start | bytes 8388608
  958.0 34.3 %slice-start.7 = ((s8[21233664]{0:T(1024)(128)(4,1)}), s8[4194304]{0:T(1024)(128)(4,1)S(1)}, s32[]{:S(2)}) async-start(s8[21233664]{0:T(1024)(128)(4,1)} %bitcast.254), calls=%async_computation.18 | async-start | bytes 8388608
  958.0 34.3 %slice-start.8 = ((s8[21233664]{0:T(1024)(128)(4,1)}), s8[4194304]{0:T(1024)(128)(4,1)S(1)}, s32[]{:S(2)}) async-start(s8[21233664]{0:T(1024)(128)(4,1)} %bitcast.254), calls=%async_computation.19 | async-start | bytes 8388608
  1027.3 66.1 %copy-start.50 = (f32[1,128,1536]{2,1,0:T(8,128)S(1)}, f32[1,128,1536]{2,1,0:T(8,128)}, u32[]{:S(2)}) copy-start(f32[1,128,1536]{2,1,0:T(8,128)} %get-tuple-element.51) | copy-start | bytes 2359300
  1027.3 66.1 %copy-start.51 = (f32[1,128,1536]{2,1,0:T(8,128)S(1)}, f32[1,128,1536]{2,1,0:T(8,128)}, u32[]{:S(2)}) copy-start(f32[1,128,1536]{2,1,0:T(8,128)} %get-tuple-element.81) | copy-start | bytes 2359300
  1027.3 66.1 %copy-start.52 = (f32[1,128,1536]{2,1,0:T(8,128)S(1)}, f32[1,128,1536]{2,1,0:T(8,128)}, u32[]{:S(2)}) copy-start(f32[1,128,1536]{2,1,0:T(8,128)} %get-tuple-element.83) | copy-start | bytes 2359300
  (110 other events, 909.2 us)
Sparse Core Ops, SparseCore 0:
  10.9 107.0 all-gather.6
  121.0 61.7 all-gather.8
  185.7 134.6 all-gather.12
  323.2 134.0 all-gather.10
  460.0 133.9 all-gather.14
  781.8 100.3 reduce-scatter.9
  925.6 975.1 reduce-scatter.5
  1908.9 378.0 reduce-scatter.7
where the time goes:
time: 2300 us; the launch traced here: 2290 us
  waiting for transfers between devices  1590 us (69%)
  matrix products  371 us (16%)
  blocking collectives  156 us (7%)
  other arithmetic  116 us (5%)
  local copies, waits for them, and re-layouts  31.6 us (1%)
    reduce_scatter x1, waiting for transfers between devices, on_device(): lax.psum_scatter(jnp.concatenate([jnp.einsum('stc,stw->cw', first_all, tr...  802 us
    reduce_scatter x1, waiting for transfers between devices, on_device(): lax.psum_scatter(jnp.einsum('stc,stw->cw', inner_all, seed_all, preferred...  379 us
    all_gather x1, waiting for transfers between devices, fetch_weights(): lax.all_gather(shards[6], ('dp', 'seq'), axis=0, tiled=True)  128 us
    all_gather x1, waiting for transfers between devices, fetch_weights(): lax.all_gather(shards[7], ('dp', 'seq'), axis=0, tiled=True)  125 us
    all_gather x1, waiting for transfers between devices, fetch_weights(): lax.all_gather(shards[5], ('dp', 'seq'), axis=0, tiled=True)  125 us
    unnamed x2, blocking collectives  89.3 us
    concatenate x1, other arithmetic, on_device(): jnp.concatenate([jnp.einsum('stc,stw->cw', first_all, triple_all, preferr...  81.1 us
    all_gather x1, blocking collectives, fetch_weights(): lax.all_gather(shards[1], ('dp', 'seq'), axis=1, tiled=True)  66.5 us
  transfers between devices with their start and end apart: 14, of which 6 were waited for; matrix products, arithmetic and copies ran while one was open for 15% of the time, Pallas kernels for 0%

commit v1 on v0

v1 whole, which is shorter than its diff:
```python
import jax
import jax.numpy as jnp
from jax import lax
from jax.sharding import Mesh
from jax.sharding import PartitionSpec as P

BF = jnp.bfloat16
F32 = jnp.float32
GROUP = ("x", "c", "y")


def ring_of(count):
    return [0] + list(range(1, count, 2)) + list(range(count - 2 + count % 2, 0, -2))


def send(block, hop, sizes):
    nx, nc, ny = sizes
    dx, dc, dy = hop
    route = []
    for i in range(nx):
        for j in range(nc):
            for k in range(ny):
                source = (i * nc + j) * ny + k
                target = (((i + dx) % nx) * nc + (j + dc) % nc) * ny + (k + dy) % ny
                route.append((source, target))
    return lax.ppermute(block, GROUP, route)


def mirror(hop, sizes):
    return tuple((-h) % n for h, n in zip(hop, sizes))


def fetch(block, hop, sizes):
    return send(block, mirror(hop, sizes), sizes)


def group_gather(block, sizes):
    nx, nc, ny = sizes
    half = block.shape[0] // 2
    got = {(0, 0): block}
    for dx in range(1, nx):
        got[dx, 0] = fetch(block, (dx, 0, 0), sizes)
    for dy in range(1, ny):
        got[0, dy] = fetch(block, (0, 0, dy), sizes)
    for dx in range(1, nx):
        for dy in range(1, ny):
            one = fetch(got[dx, 0][:half], (0, 0, dy), sizes)
            two = fetch(got[0, dy][half:], (dx, 0, 0), sizes)
            got[dx, dy] = jnp.concatenate([one, two], axis=0)
    full = {}
    for (dx, dy), value in got.items():
        full[dx, 0, dy] = value
        for dc in range(1, nc):
            full[dx, dc, dy] = fetch(value, (0, dc, 0), sizes)
    return full


def group_reduce(parts, sizes):
    nx, nc, ny = sizes
    chip = {}
    for dx in range(nx):
        for dy in range(ny):
            total = parts[dx, 0, dy].astype(F32)
            for dc in range(1, nc):
                total = total + send(parts[dx, dc, dy].astype(BF), (0, dc, 0), sizes).astype(F32)
            chip[dx, dy] = total
    half = chip[0, 0].shape[0] // 2
    for dx in range(1, nx):
        for dy in range(1, ny):
            far = chip[dx, dy].astype(BF)
            one = send(far[:half], (dx, 0, 0), sizes).astype(F32)
            two = send(far[half:], (0, 0, dy), sizes).astype(F32)
            side = chip[0, dy]
            chip[0, dy] = jnp.concatenate([side[:half] + one, side[half:]], axis=0)
            side = chip[dx, 0]
            chip[dx, 0] = jnp.concatenate([side[:half], side[half:] + two], axis=0)
    total = chip[0, 0]
    for dx in range(1, nx):
        total = total + send(chip[dx, 0].astype(BF), (dx, 0, 0), sizes).astype(F32)
    for dy in range(1, ny):
        total = total + send(chip[0, dy].astype(BF), (0, 0, dy), sizes).astype(F32)
    return total


def group_exchange(parts, sizes):
    return {mirror(hop, sizes): send(value, hop, sizes) if any(hop) else value for hop, value in parts.items()}


class Line:
    def __init__(self, count):
        self.count = count
        self.ring = ring_of(count)
        self.route = [(self.ring[i], self.ring[(i + 1) % count]) for i in range(count)]
        place = {z: i for i, z in enumerate(self.ring)}
        table = [[self.ring[(place[z] - s) % count] for z in range(count)] for s in range(count + 1)]
        here = lax.axis_index("z")
        self.source = [here]
        for s in range(1, count + 1):
            at = jnp.int32(table[s][0])
            for z in range(1, count):
                at = jnp.where(here == z, jnp.int32(table[s][z]), at)
            self.source.append(at)

    def gather(self, block, axis):
        shape = list(block.shape)
        shape.insert(axis, self.count)
        full = jnp.zeros(shape, block.dtype)
        for s in range(self.count):
            if s > 0:
                block = lax.ppermute(block, "z", self.route)
            full = lax.dynamic_update_slice_in_dim(full, jnp.expand_dims(block, axis), self.source[s], axis)
        return full

    def reduce(self, parts, axis):
        total = None
        for s in range(1, self.count + 1):
            own = lax.dynamic_index_in_dim(parts, self.source[s], axis, keepdims=False).astype(F32)
            if total is None:
                total = own
            else:
                total = own + lax.ppermute(total.astype(BF), "z", self.route).astype(F32)
        return total


def dot(left, right):
    return jnp.dot(left, right, preferred_element_type=F32)


def dot_nt(left, right):
    return lax.dot_general(left, right, (((1,), (1,)), ((), ())), preferred_element_type=F32)


def dot_tn(left, right):
    return lax.dot_general(left, right, (((0,), (0,)), ((), ())), preferred_element_type=F32)


def rms_scale(values):
    return lax.rsqrt(jnp.mean(values * values, axis=-1, keepdims=True) + 1e-05)


def norm_back(gradient, values, scale, gain):
    scaled = gradient * gain
    mean_term = jnp.mean(scaled * values, axis=-1, keepdims=True)
    return scale * scaled - values * scale * scale * scale * mean_term


def on_device(
    tokens,
    cotangent,
    lengths,
    in_weight,
    conv_weight,
    out_weight,
    gain_one,
    gain_two,
    gate_weight,
    up_weight,
    down_weight,
):
    nx, nc, nz, ny = (lax.axis_size(name) for name in ("x", "c", "z", "y"))
    sizes = (nx, nc, ny)
    ndp = nx * nc
    slots, span, width = tokens.shape
    rows = slots * span
    own_in = in_weight.shape[0]
    own_hid = down_weight.shape[0]
    chan = nz * own_in
    hid = nz * own_hid
    hops = [(dx, dc, dy) for dx in range(nx) for dc in range(nc) for dy in range(ny)]
    sides = [(dx, dc) for dx in range(nx) for dc in range(nc)]
    line = Line(nz)
    row_y = lax.axis_index("y")
    first = (lax.axis_index("z") * ny + row_y) * span
    positions = first + jnp.arange(span, dtype=jnp.int32)
    mask = (positions[None, :] < lengths[:, None]).astype(F32).reshape(rows, 1)

    x_bf = tokens.reshape(rows, width)
    x = x_bf.astype(F32)
    d_out_bf = (mask * cotangent.reshape(rows, width).astype(F32)).astype(BF)

    gains = lax.all_gather(
        jnp.stack([gain_one, gain_two], axis=0), ("x", "c", "z", "y"), axis=1, tiled=True
    ).astype(F32)
    gain_a, gain_b = gains[0], gains[1]
    taps = line.gather(conv_weight, 1).reshape(3, chan).astype(F32)

    cut = in_weight.reshape(own_in, 3, ndp, nz, ny, own_in).transpose(2, 4, 0, 1, 3, 5)
    cut = cut.reshape(ndp * ny, own_in, 3 * chan)
    cut = lax.all_to_all(cut, GROUP, 0, 0, tiled=True).reshape(ndp, ny, own_in, 3 * chan)
    w_in = line.gather(cut, 1).reshape(width, 3 * chan)

    x_all = group_gather(x_bf, sizes)
    x_all = jnp.concatenate([x_all[h] for h in hops], axis=0).astype(F32)
    a_all = (x_all * rms_scale(x_all) * gain_a).astype(BF)

    w_out = line.gather(out_weight, 0).reshape(chan, width)
    w_out = group_gather(w_out, sizes)
    w_out = jnp.concatenate([w_out[h] for h in hops], axis=0)

    both = jnp.stack([gate_weight, up_weight], axis=1)
    both = both.reshape(own_in, 2, ndp, nz, ny, own_hid).transpose(2, 4, 0, 1, 3, 5)
    both = both.reshape(ndp * ny, own_in, 2 * hid)
    both = lax.all_to_all(both, GROUP, 0, 0, tiled=True).reshape(ndp, ny, own_in, 2 * hid)
    w_both = line.gather(both, 1).reshape(width, 2 * hid)
    w_down = line.gather(down_weight, 0).reshape(hid, width)

    bcx = dot(a_all, w_in)
    wide = (len(sides), ny, slots, span, chan)
    b_part = bcx[:, :chan].reshape(wide)
    c_part = bcx[:, chan : 2 * chan].reshape(wide)
    v_part = bcx[:, 2 * chan :].reshape(wide)
    bx = b_part * v_part
    even = row_y == 0
    tail = bx[:, :, :, -2:, :]
    over = lax.ppermute(jnp.where(even, tail[:, 1], tail[:, 0]), "z", [(i, i + 1) for i in range(nz - 1)])
    before = jnp.stack(
        [jnp.where(even, over, tail[:, 1]), jnp.where(even, tail[:, 0], over)], axis=1
    )
    padded = jnp.concatenate([before, bx], axis=3)
    past_two, past_one = padded[:, :, :, :-2], padded[:, :, :, 1:-1]
    conv = taps[0] * past_two + taps[1] * past_one + taps[2] * bx
    o_all = (c_part * conv).astype(BF).reshape(len(hops), rows, chan)
    o_own = group_exchange({h: o_all[i] for i, h in enumerate(hops)}, sizes)
    o_own = jnp.concatenate([o_own[h] for h in hops], axis=1)
    h1 = x + dot(o_own, w_out)
    scale_two = rms_scale(h1)
    a2 = (h1 * scale_two * gain_b).astype(BF)

    d_all = group_gather(d_out_bf, sizes)
    d_all = jnp.concatenate([d_all[h] for h in hops], axis=0)
    a2_all = group_gather(a2, sizes)
    a2_all = jnp.concatenate([a2_all[h] for h in hops], axis=0)
    gu = dot(a2_all, w_both)
    gate, up = gu[:, :hid], gu[:, hid:]
    sigma = jax.nn.sigmoid(gate)
    active = gate * sigma
    m = (active * up).astype(BF)
    dm = dot_nt(d_all, w_down)
    d_gate = (dm * up * sigma * (1.0 + gate * (1.0 - sigma))).astype(BF)
    d_up = (dm * active).astype(BF)
    d_both = jnp.concatenate([d_gate, d_up], axis=1)
    da2_part = dot_nt(d_both, w_both).reshape(len(hops), rows, width)
    f_part = dot(m, w_down).reshape(len(hops), rows, width)
    da2 = group_reduce({h: da2_part[i] for i, h in enumerate(hops)}, sizes)
    f = group_reduce({h: f_part[i] for i, h in enumerate(hops)}, sizes)
    mixed = (mask * (h1 + f)).astype(BF)

    down_grad = line.reduce(dot_tn(m, d_all).reshape(nz, own_hid, width), 0)
    both_part = dot_tn(a2_all, d_both).reshape(ndp, nz, ny, own_in, 2 * hid)
    both_sum = line.reduce(both_part, 1).astype(BF).reshape(ndp * ny, own_in, 2 * hid)
    both_sum = lax.all_to_all(both_sum, GROUP, 0, 0, tiled=True)
    both_sum = both_sum.reshape(ndp, ny, own_in, 2, nz, own_hid).transpose(3, 2, 0, 4, 1, 5)
    both_sum = both_sum.reshape(2, own_in, ndp * nz * ny * own_hid).astype(F32)
    gate_grad, up_grad = both_sum[0], both_sum[1]
    gain_two_grad = (
        jnp.sum(gate_grad * gate_weight.astype(F32) + up_grad * up_weight.astype(F32), axis=1)
        / gain_two.astype(F32)
    )

    dh1 = d_out_bf.astype(F32) + norm_back(da2, h1, scale_two, gain_b)
    datt = dh1.astype(BF)
    do_own = dot_nt(datt, w_out).astype(BF)
    do_all = group_exchange(
        {h: do_own[:, i * chan : (i + 1) * chan] for i, h in enumerate(hops)}, sizes
    )
    do_all = jnp.stack([do_all[h] for h in hops], axis=0).reshape(wide).astype(F32)
    out_part = dot_tn(o_own, datt).reshape(len(hops), chan, width)
    out_sum = group_reduce({h: out_part[i] for i, h in enumerate(hops)}, sizes)
    out_grad = line.reduce(out_sum.reshape(nz, own_in, width), 0)

    d_c = do_all * conv
    d_conv = do_all * c_part
    head = d_conv[:, :, :, :2, :]
    under = lax.ppermute(jnp.where(even, head[:, 0], head[:, 1]), "z", [(i + 1, i) for i in range(nz - 1)])
    after = jnp.stack(
        [jnp.where(even, head[:, 1], under), jnp.where(even, under, head[:, 0])], axis=1
    )
    padded_grad = jnp.concatenate([d_conv, after], axis=3)
    d_bx = (
        taps[2] * d_conv
        + taps[1] * padded_grad[:, :, :, 1:-1]
        + taps[0] * padded_grad[:, :, :, 2:]
    )
    all_rows = (0, 1, 2, 3)
    conv_part = jnp.stack(
        [
            jnp.sum(d_conv * past_two, axis=all_rows),
            jnp.sum(d_conv * past_one, axis=all_rows),
            jnp.sum(d_conv * bx, axis=all_rows),
        ],
        axis=0,
    )
    conv_grad = lax.psum_scatter(
        conv_part.reshape(3, nz, own_in), "z", scatter_dimension=1, tiled=True
    ).reshape(3, own_in)
    d_bcx = jnp.concatenate([d_bx * v_part, d_c, d_bx * b_part], axis=-1).astype(BF)
    d_bcx = d_bcx.reshape(len(hops) * rows, 3 * chan)
    da_part = dot_nt(d_bcx, w_in).reshape(len(hops), rows, width)
    da = group_reduce({h: da_part[i] for i, h in enumerate(hops)}, sizes)

    in_part = dot_tn(a_all, d_bcx).reshape(ndp, nz, ny, own_in, 3 * chan)
    in_sum = line.reduce(in_part, 1).astype(BF).reshape(ndp * ny, own_in, 3 * chan)
    in_sum = lax.all_to_all(in_sum, GROUP, 0, 0, tiled=True)
    in_sum = in_sum.reshape(ndp, ny, own_in, 3, nz, own_in).transpose(2, 3, 0, 4, 1, 5)
    in_grad = in_sum.reshape(own_in, 3 * width).astype(F32)
    gain_one_grad = jnp.sum(in_grad * in_weight.astype(F32), axis=1) / gain_one.astype(F32)

    input_grad = dh1 + norm_back(da, x, rms_scale(x), gain_a)
    return (
        mixed.reshape(slots, span, width),
        input_grad.reshape(slots, span, width),
        in_grad,
        conv_grad,
        out_grad,
        gain_one_grad,
        gain_two_grad,
        gate_grad,
        up_grad,
        down_grad,
    )


def solution(mesh):
    dp, seq = mesh.shape["dp"], mesh.shape["seq"]
    fine = Mesh(mesh.devices.reshape(dp // 2, 2, seq // 2, 2), ("x", "c", "z", "y"))
    slot, place = ("x", "c"), ("z", "y")
    every = slot + place
    in_specs = (
        P(slot, place, None),
        P(slot, place, None),
        P(slot),
        P(every, None),
        P(None, every),
        P(every, None),
        P(every),
        P(every),
        P(every, None),
        P(every, None),
        P(every, None),
    )
    out_specs = (
        P(slot, place, None),
        P(slot, place, None),
        P(every, None),
        P(None, every),
        P(every, None),
        P(every),
        P(every),
        P(every, None),
        P(every, None),
        P(every, None),
    )
    return jax.shard_map(
        on_device, mesh=fine, in_specs=in_specs, out_specs=out_specs, check_vma=False
    )
```

time: 2300 us -> 984 us (0.43)
  waiting for transfers between devices: 1590 us -> 291 us
  matrix products: 371 us -> 175 us
  local copies, waits for them, and re-layouts: 31.6 us -> 197 us
  starting transfers between devices: 11.5 us -> 97.9 us
  blocking collectives: 156 us -> 73.2 us
    reduce_scatter x2 -> x0, waiting for transfers between devices: 1180 us -> none  [the longest x1 802 us: on_device(): lax.psum_scatter(jnp.concatenate([jnp.einsum('stc,stw->cw', first_all, tr...]
    all_gather x5 -> x0, waiting for transfers between devices: 408 us -> none  [the longest x1 128 us: fetch_weights(): lax.all_gather(shards[6], ('dp', 'seq'), axis=0, tiled=True)]
    ppermute x6 -> x107, waiting for transfers between devices: 0.02 us -> 283 us  [the longest x78 146 us: send(): return lax.ppermute(block, GROUP, route)]
    dot_general x35 -> x12, matrix products: 371 us -> 175 us  [the longest x4 66.7 us: dot_nt(): lax.dot_general(left, right, (((1,), (1,)), ((), ())), preferred_element_...]
    unnamed x2 -> x1, blocking collectives: 89.3 us -> 8.59 us
    concatenate x3 -> x13, other arithmetic: 83.8 us -> 5.59 us  [the longest x1 1.73 us: on_device(): padded_grad = jnp.concatenate([d_conv, after], axis=3)]
    ppermute x6 -> x107, starting transfers between devices: 11.2 us -> 82.1 us  [the longest x78 54.5 us: send(): return lax.ppermute(block, GROUP, route)]
    add x4 -> x10, other arithmetic: 3.67 us -> 33.4 us  [the longest x4 16.5 us: group_reduce(): total + send(parts[dx, dc, dy].astype(BF), (0, dc, 0), sizes).astype(F32)]
  transfers between devices with their start and end apart: 14 -> 111, of which waited for: 6 -> 40; matrix products, arithmetic and copies ran while one was open for 15% -> 37% of each run, Pallas kernels for 0% -> 0%
where the time goes in v1:
time: 984 us; the launch traced here: 973 us
  waiting for transfers between devices  291 us (30%)
  local copies, waits for them, and re-layouts  197 us (20%)
  matrix products  175 us (18%)
  other arithmetic  137 us (14%)
  starting transfers between devices  97.9 us (10%)
  blocking collectives  73.2 us (7%)
    ppermute x78, waiting for transfers between devices, send(): return lax.ppermute(block, GROUP, route)  146 us
    ppermute x12, waiting for transfers between devices, reduce(): total = own + lax.ppermute(total.astype(BF), 'z', self.route).astype(F32)  81.5 us
    dot_general x4, matrix products, dot_nt(): lax.dot_general(left, right, (((1,), (1,)), ((), ())), preferred_element_...  66.7 us
    all_gather x1, blocking collectives, on_device(): lax.all_gather(jnp.stack([gain_one, gain_two], axis=0), ('x', 'c', 'z', '...  64.6 us
    ppermute x15, waiting for transfers between devices, gather(): block = lax.ppermute(block, 'z', self.route)  55.6 us
    dot_general x4, matrix products, dot(): return jnp.dot(left, right, preferred_element_type=F32)  55.3 us
    ppermute x78, starting transfers between devices, send(): return lax.ppermute(block, GROUP, route)  54.5 us
    dot_general x4, matrix products, dot_tn(): lax.dot_general(left, right, (((0,), (0,)), ((), ())), preferred_element_...  52.8 us
  transfers between devices with their start and end apart: 111, of which 40 were waited for; matrix products, arithmetic and copies ran while one was open for 37% of the time, Pallas kernels for 0%

profile of v1, /device:TPU:0, one launch (start us, length us, event | category | flops | bytes accessed | tf_op | source)
XLA Modules:
  0.0 973.1 jit_solution(5560915062328810237)
XLA Ops:
  22.4 64.6 %all-gather = bf16[32,48,2]{1,2,0:T(2,128)(2,1)S(1)} all-gather(bf16[1,48,2]{1,2,0:T(2,128)(2,1)S(1)} %maximum_bitcast_fusion.1), channel_id=1, replica_groups=mesh['x'=2,'c'=2,'z'=4,'y'=2] {'x','c','z','y'}, dimensions={0}, use_global_device_ids=true | all-gather | bytes 6336 | tf_op jit(solution)/shard_map/all_gather | solution.py:181
  132.1 9.3 collective-permute-done.8
  155.3 20.5 %collective-permute-done = bf16[384,1536]{1,0:T(8,128)(2,1)} collective-permute-done((bf16[384,1536]{1,0:T(8,128)(2,1)S(1)}, bf16[384,1536]{1,0:T(8,128)(2,1)}, u32[]{:S(2)}, u32[]{:S(2)}) %collective-permute-start) | collective-permute-done | bytes 1179680 | tf_op jit(solution)/shard_map/ppermute | solution.py:26
  181.0 17.2 %collective-permute-done.55 = bf16[384,1536]{1,0:T(8,128)(2,1)} collective-permute-done((bf16[384,1536]{1,0:T(8,128)(2,1)}, bf16[384,1536]{1,0:T(8,128)(2,1)}, u32[]{:S(2)}, u32[]{:S(2)}) %collective-permute-start.55) | collective-permute-done | bytes 1179680 | tf_op jit(solution)/shard_map/ppermute | solution.py:26
  222.3 7.4 collective-permute-done.10
  231.1 9.9 %collective-permute-done.59 = bf16[192,1536]{1,0:T(8,128)(2,1)S(1)} collective-permute-done((bf16[192,1536]{1,0:T(8,128)(2,1)S(1)}, bf16[192,1536]{1,0:T(8,128)(2,1)S(1)}, u32[]{:S(2)}, u32[]{:S(2)}) %collective-permute-start.59) | collective-permute-done | bytes 589856 | tf_op jit(solution)/shard_map/ppermute | solution.py:26
  259.1 19.3 %collective-permute-done.41 = bf16[4,2,48,1728]{3,2,1,0:T(8,128)(2,1)} collective-permute-done((bf16[4,2,48,1728]{3,2,1,0:T(8,128)(2,1)S(1)}, bf16[4,2,48,1728]{3,2,1,0:T(8,128)(2,1)}, u32[]{:S(2)}, u32[]{:S(2)}) %collective-permute-start.41) | collective-permute-done | bytes 1327136 | tf_op jit(solution)/shard_map/ppermute | solution.py:110
  282.1 8.3 fusion.15
  371.1 9.4 fusion.14
  384.5 12.9 %copy.175 = bf16[1536,3072]{1,0:T(8,128)(2,1)} copy(bf16[1536,3072]{0,1:T(8,128)(2,1)} %fusion.14) | data formatting | bytes 18874368 | tf_op jit(solution)/shard_map/dot_general | solution.py:134
  404.7 7.5 collective-permute-done.37
  421.9 22.3 %fusion.86 = f32[3072,1728]{0,1:T(8,128)} fusion(bf16[3072,1536]{1,0:T(8,128)(2,1)} %constant_dynamic-update-slice_fusion.25, bf16[1536,1728]{1,0:T(8,128)(2,1)S(1)} %bitcast.293), kind=kOutput, calls=%fused_computation.289 | convolution fusion | flops 16307453952 | bytes 35979264 | tf_op jit(solution)/shard_map/dot_general | solution.py:126
  444.2 23.2 %multiply_convert_fusion.1 = (bf16[3072,864]{0,1:T(8,128)(2,1)}, bf16[3072,864]{0,1:T(8,128)(2,1)}, bf16[3072,864]{0,1:T(8,128)(2,1)}) fusion(f32[3072,1728]{0,1:T(8,128)} %fusion.86, bf16[3072,1536]{1,0:T(8,128)(2,1)} %constant_dynamic-update-slice_fusion.34, bf16[864,1536]{1,0:T(8,128)(2,1)} %bitcast.52), kind=kOutput, calls=%fused_computation.7 | convolution fusion | flops 8193540096 | bytes 49250304 | tf_op jit(solution)/shard_map/dot_general | solution.py:130
  467.4 25.0 %fusion.4 = f32[1536,1728]{1,0:T(8,128)} fusion(bf16[3072,1536]{1,0:T(8,128)(2,1)} %constant_dynamic-update-slice_fusion.25, bf16[3072,864]{0,1:T(8,128)(2,1)} %get-tuple-element.25, bf16[3072,864]{0,1:T(8,128)(2,1)} %get-tuple-element.24), kind=kOutput, calls=%fused_computation.11 | convolution fusion | flops 16328687616 | bytes 30670848 | tf_op jit(solution)/shard_map/dot_general | solution.py:134
  492.4 25.1 %fusion.82 = (bf16[3072,1536]{1,0:T(8,128)(2,1)}, f32[3072,1536]{1,0:T(8,128)}) fusion(bf16[1536,1728]{1,0:T(8,128)(2,1)} %bitcast.294, bf16[3072,864]{0,1:T(8,128)(2,1)} %get-tuple-element.25, bf16[3072,864]{0,1:T(8,128)(2,1)} %get-tuple-element.24), kind=kOutput, calls=%fused_computation.285 | convolution fusion | flops 16333406208 | bytes 44236800 | tf_op jit(solution)/shard_map/dot_general | solution.py:130
  517.5 12.8 %fusion.87 = f32[864,1536]{1,0:T(8,128)S(1)} fusion(bf16[3072,864]{0,1:T(8,128)(2,1)} %get-tuple-element.26, bf16[3072,1536]{1,0:T(8,128)(2,1)} %constant_dynamic-update-slice_fusion.34), kind=kOutput, calls=%fused_computation.290 | convolution fusion | flops 8153726976 | bytes 20054016 | tf_op jit(solution)/shard_map/dot_general | solution.py:134
  530.3 19.7 %fusion.83 = (bf16[3072,1536]{1,0:T(8,128)(2,1)}, f32[3072,1536]{1,0:T(8,128)}) fusion(bf16[3072,864]{0,1:T(8,128)(2,1)} %get-tuple-element.26, bf16[864,1536]{1,0:T(8,128)(2,1)} %bitcast.52), kind=kOutput, calls=%fused_computation.286 | convolution fusion | flops 8158445568 | bytes 36274176 | tf_op jit(solution)/shard_map/dot_general | solution.py:126
  560.1 8.7 collective-permute-done.104
  587.6 24.4 %collective-permute-done.105 = bf16[216,1536]{1,0:T(8,128)(2,1)} collective-permute-done((bf16[216,1536]{1,0:T(8,128)(2,1)}, bf16[216,1536]{1,0:T(8,128)(2,1)}, u32[]{:S(2)}, u32[]{:S(2)}) %collective-permute-start.105) | collective-permute-done | bytes 663584 | tf_op jit(solution)/shard_map/ppermute | solution.py:121
  640.1 24.3 %collective-permute-done.102 = bf16[4,2,48,1728]{3,2,1,0:T(8,128)(2,1)S(1)} collective-permute-done((bf16[4,2,48,1728]{3,2,1,0:T(8,128)(2,1)S(1)}, bf16[4,2,48,1728]{3,2,1,0:T(8,128)(2,1)S(1)}, u32[]{:S(2)}, u32[]{:S(2)}) %collective-permute-start.102) | collective-permute-done | bytes 1327136 | tf_op jit(solution)/shard_map/ppermute | solution.py:121
  669.0 9.4 collective-permute-done.54
  678.4 12.1 %collective-permute-done.51 = bf16[384,1536]{1,0:T(8,128)(2,1)S(1)} collective-permute-done((bf16[384,1536]{1,0:T(8,128)(2,1)S(1)}, bf16[384,1536]{1,0:T(8,128)(2,1)S(1)}, u32[]{:S(2)}, u32[]{:S(2)}) %collective-permute-start.51) | collective-permute-done | bytes 1179680 | tf_op jit(solution)/shard_map/ppermute | solution.py:26
  711.4 10.0 %collective-permute-done.71 = bf16[384,192]{1,0:T(8,128)(2,1)S(1)} collective-permute-done((bf16[384,192]{1,0:T(8,128)(2,1)S(1)}, bf16[384,192]{1,0:T(8,128)(2,1)S(1)}, u32[]{:S(2)}, u32[]{:S(2)}) %collective-permute-start.71) | collective-permute-done | bytes 147488 | tf_op jit(solution)/shard_map/ppermute | solution.py:26
  747.4 16.3 %multiply_reduce_fusion.1 = (f32[192]{0:T(256)S(1)}, f32[192]{0:T(256)S(1)}, f32[4,2,3,128,192]{3,2,1,0,4:T(4,128)S(1)}, bf16[4,2,3,128,192]{3,2,1,0,4:T(4,128)(2,1)}) fusion(f32[4,2,3,128,192]{3,2,1,0,4:T(4,128)} %copy-done, f32[4,2,3,128,192]{3,2,1,0,4:T(4,128)} %copy.167, f32[4,2,3,128,192]{3,2,1,0,4:T(4,128)} %reshape.283, ...), kind=kLoop, calls=%fused_computation.29 | loop fusion | flops 5317248 | bytes 13014528 | tf_op jit(solution)/shard_map/reduce_sum | solution.py:287
  763.9 8.6 all-reduce
  803.7 13.1 %fusion.84 = (bf16[3072,1536]{1,0:T(8,128)(2,1)}, f32[3072,1536]{1,0:T(8,128)}) fusion(bf16[3072,576]{0,1:T(8,128)(2,1)S(1)} %constant_dynamic-update-slice_fusion.43, bf16[1536,576]{1,0:T(8,128)(2,1)S(1)} %bitcast.308), kind=kOutput, calls=%fused_computation.287 | convolution fusion | flops 5440536576 | bytes 33619968 | tf_op jit(solution)/shard_map/dot_general | solution.py:130
  816.9 9.9 %fusion.6 = f32[4,4,2,48,576]{4,3,2,1,0:T(8,128)S(1)} fusion(bf16[4,4,2,48,3072]{4,3,2,1,0:T(8,128)(2,1)S(1)} %bitcast.285, bf16[3072,576]{0,1:T(8,128)(2,1)} %copy-done.49), kind=kOutput, calls=%fused_computation.16 | convolution fusion | flops 5435817984 | bytes 16515072 | tf_op jit(solution)/shard_map/dot_general | solution.py:134
  835.4 7.3 collective-permute-done.87
  843.2 9.1 collective-permute-done.96
  856.6 10.5 %collective-permute-done.88 = bf16[4,2,48,576]{3,2,1,0:T(8,128)(2,1)S(1)} collective-permute-done((bf16[4,2,48,576]{3,2,1,0:T(8,128)(2,1)S(1)}, bf16[4,2,48,576]{3,2,1,0:T(8,128)(2,1)S(1)}, u32[]{:S(2)}, u32[]{:S(2)}) %collective-permute-start.88) | collective-permute-done | bytes 442400 | tf_op jit(solution)/shard_map/ppermute | solution.py:121
  875.1 8.7 collective-permute-done.97
  901.6 8.5 all-to-all-done.2
  (613 shorter events, 475.1 us)
Async XLA Ops:
  0.6 102.5 %collective-permute-start.11 = (bf16[3,48]{1,0:T(4,128)(2,1)}, bf16[3,48]{1,0:T(4,128)(2,1)}, u32[]{:S(2)}, u32[]{:S(2)}) collective-permute-start(bf16[3,48]{1,0:T(4,128)(2,1)} %param.15), channel_id=1, source_target_pairs={{0,2},{2,6},{6,4},{4,0},{1,3},{3,7},{7,5},{5,1},{8,10},{10,14},{14... | collective-permute-start | bytes 872 | tf_op jit(solution)/shard_map/ppermute | solution.py:110
  3.7 104.2 %collective-permute-start.22 = (bf16[48,1536]{1,0:T(8,128)(2,1)}, bf16[48,1536]{1,0:T(8,128)(2,1)}, u32[]{:S(2)}, u32[]{:S(2)}) collective-permute-start(bf16[48,1536]{1,0:T(8,128)(2,1)} %param.16), channel_id=1, source_target_pairs={{0,2},{2,6},{6,4},{4,0},{1,3},{3,7},{7,5},{5,1},{8,10},{10,14},{14... | collective-permute-start | bytes 442376 | tf_op jit(solution)/shard_map/ppermute | solution.py:110
  6.3 124.0 %collective-permute-start.44 = (bf16[216,1536]{1,0:T(8,128)(2,1)}, bf16[216,1536]{1,0:T(8,128)(2,1)}, u32[]{:S(2)}, u32[]{:S(2)}) collective-permute-start(bf16[216,1536]{1,0:T(8,128)(2,1)} %param.21), channel_id=1, source_target_pairs={{0,2},{2,6},{6,4},{4,0},{1,3},{3,7},{7,5},{5,1},{8,10},{10,14},{14... | collective-permute-start | bytes 1990664 | tf_op jit(solution)/shard_map/ppermute | solution.py:110
  13.6 109.5 %all-to-all-start = ((bf16[8,48,576]{2,1,0:T(8,128)(2,1)}), bf16[8,48,576]{2,1,0:T(8,128)(2,1)}, u32[]{:S(2)}, u32[]{:S(2)}) async-start(bf16[8,48,576]{2,1,0:T(8,128)(2,1)} %reshape.280), calls=%async_computation | async-start | bytes 983040 | tf_op jit(solution)/shard_map/all_to_all | solution.py:189
  17.9 134.2 %collective-permute-start.3 = (bf16[384,1536]{1,0:T(8,128)(2,1)S(1)}, bf16[384,1536]{1,0:T(8,128)(2,1)}, u32[]{:S(2)}, u32[]{:S(2)}) collective-permute-start(bf16[384,1536]{1,0:T(8,128)(2,1)S(1)} %bitcast.275), channel_id=1, source_target_pairs={{0,16},{1,17},{8,24},{9,25},{16,0},{17,1},{24,8},{25,9},{2,18},{3,... | collective-permute-start | bytes 3538952 | tf_op jit(solution)/shard_map/ppermute | solution.py:26
  130.3 45.5 %collective-permute-start = (bf16[384,1536]{1,0:T(8,128)(2,1)S(1)}, bf16[384,1536]{1,0:T(8,128)(2,1)}, u32[]{:S(2)}, u32[]{:S(2)}) collective-permute-start(bf16[384,1536]{1,0:T(8,128)(2,1)S(1)} %bitcast.277), channel_id=1, source_target_pairs={{0,1},{1,0},{8,9},{9,8},{16,17},{17,16},{24,25},{25,24},{2,3},{3,2... | collective-permute-start | bytes 3538952 | tf_op jit(solution)/shard_map/ppermute | solution.py:26
  141.5 35.4 %collective-permute-start.58 = (bf16[384,1536]{1,0:T(8,128)(2,1)}, bf16[384,1536]{1,0:T(8,128)(2,1)}, u32[]{:S(2)}, u32[]{:S(2)}) collective-permute-start(bf16[384,1536]{1,0:T(8,128)(2,1)} %get-tuple-element.91), channel_id=1, source_target_pairs={{0,16},{1,17},{8,24},{9,25},{16,0},{17,1},{24,8},{25,9},{2,18},{3,... | collective-permute-start | bytes 3538952 | tf_op jit(solution)/shard_map/ppermute | solution.py:26
  143.2 55.0 %collective-permute-start.55 = (bf16[384,1536]{1,0:T(8,128)(2,1)}, bf16[384,1536]{1,0:T(8,128)(2,1)}, u32[]{:S(2)}, u32[]{:S(2)}) collective-permute-start(bf16[384,1536]{1,0:T(8,128)(2,1)} %get-tuple-element.91), channel_id=1, source_target_pairs={{0,1},{1,0},{8,9},{9,8},{16,17},{17,16},{24,25},{25,24},{2,3},{3,2... | collective-permute-start | bytes 3538952 | tf_op jit(solution)/shard_map/ppermute | solution.py:26
  149.6 55.0 %collective-permute-start.1 = (bf16[384,1536]{1,0:T(8,128)(2,1)S(1)}, bf16[384,1536]{1,0:T(8,128)(2,1)}, u32[]{:S(2)}, u32[]{:S(2)}) collective-permute-start(bf16[384,1536]{1,0:T(8,128)(2,1)S(1)} %bitcast.278), channel_id=1, source_target_pairs={{0,8},{1,9},{8,0},{9,1},{16,24},{17,25},{24,16},{25,17},{2,10},{3,... | collective-permute-start | bytes 3538952 | tf_op jit(solution)/shard_map/ppermute | solution.py:26
  152.1 57.3 %collective-permute-start.56 = (bf16[384,1536]{1,0:T(8,128)(2,1)}, bf16[384,1536]{1,0:T(8,128)(2,1)}, u32[]{:S(2)}, u32[]{:S(2)}) collective-permute-start(bf16[384,1536]{1,0:T(8,128)(2,1)} %get-tuple-element.91), channel_id=1, source_target_pairs={{0,8},{1,9},{8,0},{9,1},{16,24},{17,25},{24,16},{25,17},{2,10},{3,... | collective-permute-start | bytes 3538952 | tf_op jit(solution)/shard_map/ppermute | solution.py:26
  175.8 37.3 %collective-permute-start.45 = (bf16[216,1536]{1,0:T(8,128)(2,1)}, bf16[216,1536]{1,0:T(8,128)(2,1)S(1)}, u32[]{:S(2)}, u32[]{:S(2)}) collective-permute-start(bf16[216,1536]{1,0:T(8,128)(2,1)} %collective-permute-done.44), channel_id=1, source_target_pairs={{0,2},{2,6},{6,4},{4,0},{1,3},{3,7},{7,5},{5,1},{8,10},{10,14},{14... | collective-permute-start | bytes 1990664 | tf_op jit(solution)/shard_map/ppermute | solution.py:110
  176.9 34.8 %collective-permute-start.9 = (bf16[4,2,48,576]{3,2,1,0:T(8,128)(2,1)}, bf16[4,2,48,576]{3,2,1,0:T(8,128)(2,1)S(1)}, u32[]{:S(2)}, u32[]{:S(2)}) collective-permute-start(bf16[4,2,48,576]{3,2,1,0:T(8,128)(2,1)} %collective-permute-done.8), channel_id=1, source_target_pairs={{0,2},{2,6},{6,4},{4,0},{1,3},{3,7},{7,5},{5,1},{8,10},{10,14},{14... | collective-permute-start | bytes 1327112 | tf_op jit(solution)/shard_map/ppermute | solution.py:110
  241.0 37.4 %collective-permute-start.41 = (bf16[4,2,48,1728]{3,2,1,0:T(8,128)(2,1)S(1)}, bf16[4,2,48,1728]{3,2,1,0:T(8,128)(2,1)}, u32[]{:S(2)}, u32[]{:S(2)}) collective-permute-start(bf16[4,2,48,1728]{3,2,1,0:T(8,128)(2,1)S(1)} %bitcast.296), channel_id=1, source_target_pairs={{0,2},{2,6},{6,4},{4,0},{1,3},{3,7},{7,5},{5,1},{8,10},{10,14},{14... | collective-permute-start | bytes 3981320 | tf_op jit(solution)/shard_map/ppermute | solution.py:110
  252.5 129.6 %collective-permute-start.62 = (bf16[384,1536]{1,0:T(8,128)(2,1)}, bf16[384,1536]{1,0:T(8,128)(2,1)}, u32[]{:S(2)}, u32[]{:S(2)}) collective-permute-start(bf16[384,1536]{1,0:T(8,128)(2,1)} %pad_maximum_fusion.9), channel_id=1, source_target_pairs={{0,8},{1,9},{8,0},{9,1},{16,24},{17,25},{24,16},{25,17},{2,10},{3,... | collective-permute-start | bytes 3538952 | tf_op jit(solution)/shard_map/ppermute | solution.py:26
  278.4 102.1 %collective-permute-start.42 = (bf16[4,2,48,1728]{3,2,1,0:T(8,128)(2,1)}, bf16[4,2,48,1728]{3,2,1,0:T(8,128)(2,1)}, u32[]{:S(2)}, u32[]{:S(2)}) collective-permute-start(bf16[4,2,48,1728]{3,2,1,0:T(8,128)(2,1)} %collective-permute-done.41), channel_id=1, source_target_pairs={{0,2},{2,6},{6,4},{4,0},{1,3},{3,7},{7,5},{5,1},{8,10},{10,14},{14... | collective-permute-start | bytes 3981320 | tf_op jit(solution)/shard_map/ppermute | solution.py:110
  558.0 56.5 %collective-permute-start.101 = (bf16[4,2,48,1728]{3,2,1,0:T(8,128)(2,1)}, bf16[4,2,48,1728]{3,2,1,0:T(8,128)(2,1)}, u32[]{:S(2)}, u32[]{:S(2)}) collective-permute-start(bf16[4,2,48,1728]{3,2,1,0:T(8,128)(2,1)} %fusion.40), channel_id=1, source_target_pairs={{0,2},{2,6},{6,4},{4,0},{1,3},{3,7},{7,5},{5,1},{8,10},{10,14},{14... | collective-permute-start | bytes 3981320 | tf_op jit(solution)/shard_map/ppermute | solution.py:121
  569.6 69.7 %collective-permute-start.63 = (bf16[384,1536]{1,0:T(8,128)(2,1)}, bf16[384,1536]{1,0:T(8,128)(2,1)S(1)}, u32[]{:S(2)}, u32[]{:S(2)}) collective-permute-start(bf16[384,1536]{1,0:T(8,128)(2,1)} %get-tuple-element.43), channel_id=1, source_target_pairs={{0,8},{1,9},{8,0},{9,1},{16,24},{17,25},{24,16},{25,17},{2,10},{3,... | collective-permute-start | bytes 3538952 | tf_op jit(solution)/shard_map/ppermute | solution.py:26
  580.5 38.8 %collective-permute-start.66 = (bf16[192,1536]{1,0:T(8,128)(2,1)}, bf16[192,1536]{1,0:T(8,128)(2,1)}, u32[]{:S(2)}, u32[]{:S(2)}) collective-permute-start(bf16[192,1536]{1,0:T(8,128)(2,1)} %get-tuple-element.76), channel_id=1, source_target_pairs={{0,1},{1,0},{8,9},{9,8},{16,17},{17,16},{24,25},{25,24},{2,3},{3,2... | collective-permute-start | bytes 1769480 | tf_op jit(solution)/shard_map/ppermute | solution.py:26
  581.2 36.8 %collective-permute-start.69 = (bf16[192,1536]{1,0:T(8,128)(2,1)}, bf16[192,1536]{1,0:T(8,128)(2,1)}, u32[]{:S(2)}, u32[]{:S(2)}) collective-permute-start(bf16[192,1536]{1,0:T(8,128)(2,1)} %get-tuple-element.77), channel_id=1, source_target_pairs={{0,16},{1,17},{8,24},{9,25},{16,0},{17,1},{24,8},{25,9},{2,18},{3,... | collective-permute-start | bytes 1769480 | tf_op jit(solution)/shard_map/ppermute | solution.py:26
  619.4 45.0 %collective-permute-start.102 = (bf16[4,2,48,1728]{3,2,1,0:T(8,128)(2,1)S(1)}, bf16[4,2,48,1728]{3,2,1,0:T(8,128)(2,1)S(1)}, u32[]{:S(2)}, u32[]{:S(2)}) collective-permute-start(bf16[4,2,48,1728]{3,2,1,0:T(8,128)(2,1)S(1)} %fusion.11), channel_id=1, source_target_pairs={{0,2},{2,6},{6,4},{4,0},{1,3},{3,7},{7,5},{5,1},{8,10},{10,14},{14... | collective-permute-start | bytes 3981320 | tf_op jit(solution)/shard_map/ppermute | solution.py:121
  626.7 39.5 %collective-permute-start.70 = (bf16[384,1536]{1,0:T(8,128)(2,1)S(1)}, bf16[384,1536]{1,0:T(8,128)(2,1)S(1)}, u32[]{:S(2)}, u32[]{:S(2)}) collective-permute-start(bf16[384,1536]{1,0:T(8,128)(2,1)S(1)} %pad_maximum_fusion.11), channel_id=1, source_target_pairs={{0,1},{1,0},{8,9},{9,8},{16,17},{17,16},{24,25},{25,24},{2,3},{3,2... | collective-permute-start | bytes 3538952 | tf_op jit(solution)/shard_map/ppermute | solution.py:26
  629.3 37.2 %collective-permute-start.67 = (bf16[384,1536]{1,0:T(8,128)(2,1)S(1)}, bf16[384,1536]{1,0:T(8,128)(2,1)S(1)}, u32[]{:S(2)}, u32[]{:S(2)}) collective-permute-start(bf16[384,1536]{1,0:T(8,128)(2,1)S(1)} %pad_maximum_fusion.10), channel_id=1, source_target_pairs={{0,16},{1,17},{8,24},{9,25},{16,0},{17,1},{24,8},{25,9},{2,18},{3,... | collective-permute-start | bytes 3538952 | tf_op jit(solution)/shard_map/ppermute | solution.py:26
  639.4 39.0 %collective-permute-start.54 = (bf16[384,1536]{1,0:T(8,128)(2,1)S(1)}, bf16[384,1536]{1,0:T(8,128)(2,1)S(1)}, u32[]{:S(2)}, u32[]{:S(2)}) collective-permute-start(bf16[384,1536]{1,0:T(8,128)(2,1)S(1)} %pad_maximum_fusion.8), channel_id=1, source_target_pairs={{0,1},{1,0},{8,9},{9,8},{16,17},{17,16},{24,25},{25,24},{2,3},{3,2... | collective-permute-start | bytes 3538952 | tf_op jit(solution)/shard_map/ppermute | solution.py:26
  666.2 186.3 %collective-permute-start.103 = (bf16[4,2,48,1728]{3,2,1,0:T(8,128)(2,1)}, bf16[4,2,48,1728]{3,2,1,0:T(8,128)(2,1)}, u32[]{:S(2)}, u32[]{:S(2)}) collective-permute-start(bf16[4,2,48,1728]{3,2,1,0:T(8,128)(2,1)} %fusion.12), channel_id=1, source_target_pairs={{0,2},{2,6},{6,4},{4,0},{1,3},{3,7},{7,5},{5,1},{8,10},{10,14},{14... | collective-permute-start | bytes 3981320 | tf_op jit(solution)/shard_map/ppermute | solution.py:121
  736.7 138.4 %collective-permute-start.90 = (bf16[192,1536]{1,0:T(8,128)(2,1)}, bf16[192,1536]{1,0:T(8,128)(2,1)}, u32[]{:S(2)}, u32[]{:S(2)}) collective-permute-start(bf16[192,1536]{1,0:T(8,128)(2,1)} %get-tuple-element.54), channel_id=1, source_target_pairs={{0,8},{1,9},{8,0},{9,1},{16,24},{17,25},{24,16},{25,17},{2,10},{3,... | collective-permute-start | bytes 1769480 | tf_op jit(solution)/shard_map/ppermute | solution.py:26
  736.7 90.1 %collective-permute-start.95 = (bf16[192,1536]{1,0:T(8,128)(2,1)}, bf16[192,1536]{1,0:T(8,128)(2,1)}, u32[]{:S(2)}, u32[]{:S(2)}) collective-permute-start(bf16[192,1536]{1,0:T(8,128)(2,1)} %get-tuple-element.55), channel_id=1, source_target_pairs={{0,8},{1,9},{8,0},{9,1},{16,24},{17,25},{24,16},{25,17},{2,10},{3,... | collective-permute-start | bytes 1769480 | tf_op jit(solution)/shard_map/ppermute | solution.py:26
  737.3 92.2 %collective-permute-start.92 = (bf16[192,1536]{1,0:T(8,128)(2,1)}, bf16[192,1536]{1,0:T(8,128)(2,1)}, u32[]{:S(2)}, u32[]{:S(2)}) collective-permute-start(bf16[192,1536]{1,0:T(8,128)(2,1)} %get-tuple-element.56), channel_id=1, source_target_pairs={{0,8},{1,9},{8,0},{9,1},{16,24},{17,25},{24,16},{25,17},{2,10},{3,... | collective-permute-start | bytes 1769480 | tf_op jit(solution)/shard_map/ppermute | solution.py:26
  782.7 46.8 %collective-permute-start.91 = (bf16[192,1536]{1,0:T(8,128)(2,1)}, bf16[192,1536]{1,0:T(8,128)(2,1)}, u32[]{:S(2)}, u32[]{:S(2)}) collective-permute-start(bf16[192,1536]{1,0:T(8,128)(2,1)} %get-tuple-element.57), channel_id=1, source_target_pairs={{0,8},{1,9},{8,0},{9,1},{16,24},{17,25},{24,16},{25,17},{2,10},{3,... | collective-permute-start | bytes 1769480 | tf_op jit(solution)/shard_map/ppermute | solution.py:26
  867.1 91.3 %collective-permute-start.79 = (bf16[384,1536]{1,0:T(8,128)(2,1)}, bf16[384,1536]{1,0:T(8,128)(2,1)}, u32[]{:S(2)}, u32[]{:S(2)}) collective-permute-start(bf16[384,1536]{1,0:T(8,128)(2,1)} %get-tuple-element.39), channel_id=1, source_target_pairs={{0,8},{1,9},{8,0},{9,1},{16,24},{17,25},{24,16},{25,17},{2,10},{3,... | collective-permute-start | bytes 3538952 | tf_op jit(solution)/shard_map/ppermute | solution.py:26
  889.2 44.0 %collective-permute-start.82 = (bf16[192,1536]{1,0:T(8,128)(2,1)}, bf16[192,1536]{1,0:T(8,128)(2,1)}, u32[]{:S(2)}, u32[]{:S(2)}) collective-permute-start(bf16[192,1536]{1,0:T(8,128)(2,1)} %get-tuple-element.67), channel_id=1, source_target_pairs={{0,1},{1,0},{8,9},{9,8},{16,17},{17,16},{24,25},{25,24},{2,3},{3,2... | collective-permute-start | bytes 1769480 | tf_op jit(solution)/shard_map/ppermute | solution.py:26
  890.3 38.5 %collective-permute-start.85 = (bf16[192,1536]{1,0:T(8,128)(2,1)}, bf16[192,1536]{1,0:T(8,128)(2,1)}, u32[]{:S(2)}, u32[]{:S(2)}) collective-permute-start(bf16[192,1536]{1,0:T(8,128)(2,1)} %get-tuple-element.68), channel_id=1, source_target_pairs={{0,16},{1,17},{8,24},{9,25},{16,0},{17,1},{24,8},{25,9},{2,18},{3,... | collective-permute-start | bytes 1769480 | tf_op jit(solution)/shard_map/ppermute | solution.py:26
  900.5 36.5 %collective-permute-start.100 = (bf16[48,1536]{1,0:T(8,128)(2,1)}, bf16[48,1536]{1,0:T(8,128)(2,1)}, u32[]{:S(2)}, u32[]{:S(2)}) collective-permute-start(bf16[48,1536]{1,0:T(8,128)(2,1)} %fusion.63), channel_id=1, source_target_pairs={{0,2},{2,6},{6,4},{4,0},{1,3},{3,7},{7,5},{5,1},{8,10},{10,14},{14... | collective-permute-start | bytes 442376 | tf_op jit(solution)/shard_map/ppermute | solution.py:121
  (166 other events, 3566.3 us)

commit v2 on v1

v2 whole, which is shorter than its diff:
```python
import jax
import jax.numpy as jnp
from jax import lax
from jax.experimental import pallas as pl
from jax.experimental.pallas import tpu as pltpu
from jax.sharding import Mesh
from jax.sharding import PartitionSpec as P

BF = jnp.bfloat16
F32 = jnp.float32
GROUP = ("x", "c", "y")


def ring_of(count):
    return [0] + list(range(1, count, 2)) + list(range(count - 2 + count % 2, 0, -2))


def send(block, hop, sizes):
    nx, nc, ny = sizes
    dx, dc, dy = hop
    route = []
    for i in range(nx):
        for j in range(nc):
            for k in range(ny):
                source = (i * nc + j) * ny + k
                target = (((i + dx) % nx) * nc + (j + dc) % nc) * ny + (k + dy) % ny
                route.append((source, target))
    return lax.ppermute(block, GROUP, route)


def mirror(hop, sizes):
    return tuple((-h) % n for h, n in zip(hop, sizes))


def fetch(block, hop, sizes):
    return send(block, mirror(hop, sizes), sizes)


def near_gather(block, sizes):
    nx, nc, ny = sizes
    got = {(0, 0): block}
    for dx in range(1, nx):
        got[dx, 0] = fetch(block, (dx, 0, 0), sizes)
    for dy in range(1, ny):
        got[0, dy] = fetch(block, (0, 0, dy), sizes)
    return got


def far_gather(got, sizes):
    nx, nc, ny = sizes
    half = got[0, 0].shape[0] // 2
    got = dict(got)
    for dx in range(1, nx):
        for dy in range(1, ny):
            one = fetch(got[dx, 0][:half], (0, 0, dy), sizes)
            two = fetch(got[0, dy][half:], (dx, 0, 0), sizes)
            got[dx, dy] = jnp.concatenate([one, two], axis=0)
    full = {}
    for (dx, dy), value in got.items():
        full[dx, 0, dy] = value
        for dc in range(1, nc):
            full[dx, dc, dy] = fetch(value, (0, dc, 0), sizes)
    return full


class GroupSum:
    def __init__(self, near, far, sizes):
        nx, _, ny = sizes
        self.sizes = sizes
        self.keys = [(dx, dy) for dx in range(nx) for dy in range(ny)]
        self.here = {key: near[i] for i, key in enumerate(self.keys)}
        self.cross = send(far, (0, 1, 0), sizes)
        self.half = near.shape[1] // 2

    def pair(self, key):
        return self.here[key].astype(F32) + self.cross[self.keys.index(key)].astype(F32)

    def start_far(self):
        half = self.half
        self.more = {}
        for dx, dy in self.keys:
            if dx and dy:
                total = self.pair((dx, dy)).astype(BF)
                self.more[dx, dy] = (
                    send(total[:half], (dx, 0, 0), self.sizes),
                    send(total[half:], (0, 0, dy), self.sizes),
                )

    def start_near(self):
        half = self.half
        self.last = {}
        for key in self.keys:
            if (key[0] == 0) == (key[1] == 0):
                continue
            total = self.pair(key)
            low, high = total[:half], total[half:]
            for (dx, dy), (one, two) in self.more.items():
                if key == (0, dy):
                    low = low + one.astype(F32)
                if key == (dx, 0):
                    high = high + two.astype(F32)
            total = jnp.concatenate([low, high], axis=0).astype(BF)
            self.last[key] = send(total, (key[0], 0, key[1]), self.sizes)

    def terms(self):
        return [self.here[0, 0], self.cross[0]] + list(self.last.values())


class Line:
    def __init__(self, count):
        self.count = count
        self.ring = ring_of(count)
        self.route = [(self.ring[i], self.ring[(i + 1) % count]) for i in range(count)]
        place = {z: i for i, z in enumerate(self.ring)}
        table = [[self.ring[(place[z] - s) % count] for z in range(count)] for s in range(count + 1)]
        here = lax.axis_index("z")
        self.source = [here]
        for s in range(1, count + 1):
            at = jnp.int32(table[s][0])
            for z in range(1, count):
                at = jnp.where(here == z, jnp.int32(table[s][z]), at)
            self.source.append(at)

    def gather(self, block, axis):
        shape = list(block.shape)
        shape.insert(axis, self.count)
        full = jnp.zeros(shape, block.dtype)
        for s in range(self.count):
            if s > 0:
                block = lax.ppermute(block, "z", self.route)
            full = lax.dynamic_update_slice_in_dim(full, jnp.expand_dims(block, axis), self.source[s], axis)
        return full

    def fetch_all(self, block):
        got = [block]
        for s in range(1, self.count):
            route = [(self.ring[i], self.ring[(i + s) % self.count]) for i in range(self.count)]
            got.append(lax.ppermute(block, "z", route))
        return got

    def place(self, blocks, axis):
        shape = list(blocks[0].shape)
        shape.insert(axis, self.count)
        full = jnp.zeros(shape, blocks[0].dtype)
        for s, block in enumerate(blocks):
            full = lax.dynamic_update_slice_in_dim(full, jnp.expand_dims(block, axis), self.source[s], axis)
        return full

    def reduce_direct(self, parts, axis):
        terms = [lax.dynamic_index_in_dim(parts, self.source[0], axis, keepdims=False)]
        for s in range(1, self.count):
            part = lax.dynamic_index_in_dim(parts, self.source[s], axis, keepdims=False)
            route = [(self.ring[i], self.ring[(i - s) % self.count]) for i in range(self.count)]
            terms.append(lax.ppermute(part, "z", route))
        return terms


def dot(left, right):
    return jnp.dot(left, right, preferred_element_type=F32)


def dot_nt(left, right):
    return lax.dot_general(left, right, (((1,), (1,)), ((), ())), preferred_element_type=F32)


def dot_tn(left, right):
    return lax.dot_general(left, right, (((0,), (0,)), ((), ())), preferred_element_type=F32)


def rms_scale(values):
    return lax.rsqrt(jnp.mean(values * values, axis=-1, keepdims=True) + 1e-05)


def norm_back(gradient, values, scale, gain):
    scaled = gradient * gain
    mean_term = jnp.mean(scaled * values, axis=-1, keepdims=True)
    return scale * scaled - values * scale * scale * scale * mean_term


def after(first, second):
    return lax.optimization_barrier((first, second))


def up_to(count, step):
    return (count + step - 1) // step * step


def earlier(values, one, two):
    rows = lax.broadcasted_iota(jnp.int32, values.shape, 0)
    by_one = jnp.where(rows == 0, two, pltpu.roll(values, 1, 0))
    by_two = jnp.where(rows == 0, one, jnp.where(rows == 1, two, pltpu.roll(values, 2, 0)))
    return by_two, by_one


def later(values, one, two):
    count = values.shape[0]
    rows = lax.broadcasted_iota(jnp.int32, values.shape, 0)
    by_one = jnp.where(rows == count - 1, one, pltpu.roll(values, count - 1, 0))
    by_two = jnp.where(
        rows == count - 1, two, jnp.where(rows == count - 2, one, pltpu.roll(values, count - 2, 0))
    )
    return by_one, by_two


def shuffle_plan(ndp, nz, ny):
    return [(dp * ny + y, z) for dp in range(ndp) for z in range(nz) for y in range(ny)]


def cut_body(plan, spots, size, pad, extra, *refs):
    count = 1 + max(which for which, _ in spots)
    sources, more, out = refs[:count], refs[count:-1], refs[-1]
    share = {}
    for at, (group, z) in enumerate(plan):
        share[group, z] = at
    groups = 1 + max(group for group, _ in plan)
    depth = len(plan) // groups
    for group in range(groups):
        for part, (which, start) in enumerate(spots):
            pieces = [
                sources[which][:, start + share[group, z] * size : start + (share[group, z] + 1) * size]
                for z in range(depth)
            ]
            left = pad - depth * size
            if more and part == 0:
                pieces.append(more[0][...])
                left -= extra
            if left:
                pieces.append(jnp.zeros((pieces[0].shape[0], left), pieces[0].dtype))
            out[group, :, part * pad : (part + 1) * pad] = jnp.concatenate(pieces, axis=1)


def cut_columns(sources, size, pad, plan, more=None):
    rows = sources[0].shape[0]
    whole = size * len(plan)
    spots = [(i, start) for i, source in enumerate(sources) for start in range(0, source.shape[1], whole)]
    parts = len(spots)
    groups = 1 + max(group for group, _ in plan)
    extra = 0 if more is None else more.shape[1]
    if rows % 16:
        order = [[i for z in range(len(plan)) for i, p in enumerate(plan) if p == (g, z)] for g in range(groups)]
        out = []
        for group in order:
            row = []
            for part, (which, start) in enumerate(spots):
                pieces = [sources[which][:, start + i * size : start + (i + 1) * size] for i in group]
                left = pad - len(group) * size
                if more is not None and part == 0:
                    pieces.append(more)
                    left -= extra
                pieces.append(jnp.zeros((rows, left), BF))
                row += pieces
            out.append(jnp.concatenate(row, axis=1))
        return jnp.stack(out, axis=0)
    inputs = list(sources) + ([] if more is None else [more])
    return pl.pallas_call(
        lambda *refs: cut_body(plan, spots, size, pad, extra, *refs),
        out_shape=jax.ShapeDtypeStruct((groups, rows, parts * pad), BF),
        compiler_params=pltpu.CompilerParams(vmem_limit_bytes=32 * 2**20),
        cost_estimate=pl.CostEstimate(flops=0, bytes_accessed=6 * 2**20, transcendentals=0),
        name="cut_columns",
    )(*inputs)


def join_body(plan, spots, size, pad, *refs):
    count = 1 + max(which for which, _ in spots)
    shares, weights, gain = refs[0], refs[1 : 1 + count], refs[1 + count]
    grads, gain_grad = refs[2 + count : 2 + 2 * count], refs[-1]
    whole = size * len(plan)
    total = None
    for part, (which, start) in enumerate(spots):
        pieces = [
            shares[group, :, part * pad + z * size : part * pad + (z + 1) * size] for group, z in plan
        ]
        grad = jnp.concatenate(pieces, axis=1).astype(F32)
        grads[which][:, start : start + whole] = grad
        term = jnp.sum(grad * weights[which][:, start : start + whole].astype(F32), axis=1, keepdims=True)
        total = term if total is None else total + term
    gain_grad[...] = total / gain[...]


def join_columns(shares, weights, gain, size, pad, plan):
    rows = weights[0].shape[0]
    whole = size * len(plan)
    spots = [(i, start) for i, weight in enumerate(weights) for start in range(0, weight.shape[1], whole)]
    count = len(weights)
    gain = gain.astype(F32).reshape(rows, 1)
    if rows % 16:
        total, grads = None, [[] for _ in weights]
        for part, (which, start) in enumerate(spots):
            pieces = [shares[g, :, part * pad + z * size : part * pad + (z + 1) * size] for g, z in plan]
            grads[which].append(jnp.concatenate(pieces, axis=1).astype(F32))
            weight = weights[which][:, start : start + whole].astype(F32)
            term = jnp.sum(grads[which][-1] * weight, axis=1, keepdims=True)
            total = term if total is None else total + term
        return [jnp.concatenate(g, axis=1) for g in grads], (total / gain).reshape(rows)
    out = pl.pallas_call(
        lambda *refs: join_body(plan, spots, size, pad, *refs),
        out_shape=[jax.ShapeDtypeStruct(w.shape, F32) for w in weights] + [jax.ShapeDtypeStruct((rows, 1), F32)],
        compiler_params=pltpu.CompilerParams(vmem_limit_bytes=32 * 2**20),
        cost_estimate=pl.CostEstimate(flops=0, bytes_accessed=8 * 2**20, transcendentals=0),
        name="join_columns",
    )(shares, *weights, gain)
    return out[:count], out[count].reshape(rows)


def mix_forward_body(cpad, slots, span, edge, place, x0, x1, e0, e1, w, gain, taps, a, bcx, o_out):
    def normal(ref):
        x = ref[0].astype(F32)
        return (x * rms_scale(x) * gain[...]).astype(BF)

    rows = slots * span
    a0, a1 = normal(x0), normal(x1)
    a[0, 0] = a0
    a[0, 1] = a1
    edges = dot(jnp.concatenate([normal(e0), normal(e1)], axis=0), w[...])
    bcx[0, 2 * rows :] = edges
    past = edges[:edge, :cpad] * edges[:edge, 2 * cpad :]
    low, high = dot(a0, w[...]), dot(a1, w[...])
    bcx[0, :rows] = low
    bcx[0, rows : 2 * rows] = high
    for slot in range(slots):
        both = [part[slot * span : (slot + 1) * span] for part in (low, high)]
        b, c, v = (
            jnp.concatenate([part[:, i * cpad : (i + 1) * cpad] for part in both], axis=0) for i in range(3)
        )
        bx = b * v
        by_two, by_one = earlier(bx, past[2 * slot : 2 * slot + 1], past[2 * slot + 1 : 2 * slot + 2])
        conv = taps[0:1] * by_two + taps[1:2] * by_one + taps[2:3] * bx
        o = (c * conv).astype(BF)
        o_out[0, 0, slot * span : (slot + 1) * span] = o[:span]
        o_out[0, 1, slot * span : (slot + 1) * span] = o[span:]


def mix_forward(x_all, x_past, x_next, w_in, gain, taps, place, sides, slots, span, edge):
    width = x_all.shape[2]
    cpad = w_in.shape[1] // 3
    rows = slots * span
    total = 2 * rows + 2 * edge

    def main(y):
        return pl.BlockSpec((1, rows, width), lambda g, r: (r[2 * g + y], 0, 0))

    rim = pl.BlockSpec((1, edge, width), lambda g, r: (r[2 * g] // 2, 0, 0))

    def fixed(shape):
        return pl.BlockSpec(shape, lambda g, r: (0,) * len(shape))

    return pl.pallas_call(
        lambda *refs: mix_forward_body(cpad, slots, span, edge, *refs),
        grid_spec=pltpu.PrefetchScalarGridSpec(
            num_scalar_prefetch=1,
            grid=(sides,),
            in_specs=[main(0), main(1), rim, rim, fixed(w_in.shape), fixed(gain.shape), fixed(taps.shape)],
            out_specs=[
                pl.BlockSpec((1, 2, rows, width), lambda g, r: (g, 0, 0, 0)),
                pl.BlockSpec((1, total, 3 * cpad), lambda g, r: (g, 0, 0)),
                pl.BlockSpec((1, 2, rows, cpad), lambda g, r: (g, 0, 0, 0)),
            ],
        ),
        out_shape=[
            jax.ShapeDtypeStruct((sides, 2, rows, width), BF),
            jax.ShapeDtypeStruct((sides, total, 3 * cpad), F32),
            jax.ShapeDtypeStruct((sides, 2, rows, cpad), BF),
        ],
        compiler_params=pltpu.CompilerParams(vmem_limit_bytes=56 * 2**20),
        cost_estimate=pl.CostEstimate(
            flops=sides * total * width * 6 * cpad, bytes_accessed=32 * 2**20, transcendentals=0
        ),
        name="mix_forward",
    )(place, x_all, x_all, x_past, x_next, w_in, gain, taps)


def mix_backward_body(
    cpad, slots, span, edge, nat, d0, d1, e1, a, bcx, w, taps, d_part, da_near, da_far, conv_grad, total, grads
):
    step = pl.program_id(0)
    rows = slots * span
    first = step == 0

    @pl.when(first)
    def _():
        conv_grad[...] = jnp.zeros_like(conv_grad)

    edges = bcx[0, 2 * rows :]
    past = edges[:edge, :cpad] * edges[:edge, 2 * cpad :]
    future = e1[0].astype(F32) * edges[edge:, cpad : 2 * cpad]
    sums = [None, None, None]
    for slot in range(slots):
        spots = [slice(y * rows + slot * span, y * rows + (slot + 1) * span) for y in range(2)]
        b, c, v = (
            jnp.concatenate([bcx[0, s, i * cpad : (i + 1) * cpad] for s in spots], axis=0) for i in range(3)
        )
        here = slice(slot * span, (slot + 1) * span)
        d_o = jnp.concatenate([d0[0, here], d1[0, here]], axis=0).astype(F32)
        bx = b * v
        by_two, by_one = earlier(bx, past[2 * slot : 2 * slot + 1], past[2 * slot + 1 : 2 * slot + 2])
        conv = taps[0:1] * by_two + taps[1:2] * by_one + taps[2:3] * bx
        d_c = d_o * conv
        d_conv = d_o * c
        next_one, next_two = later(d_conv, future[2 * slot : 2 * slot + 1], future[2 * slot + 1 : 2 * slot + 2])
        d_bx = taps[2:3] * d_conv + taps[1:2] * next_one + taps[0:1] * next_two
        for i, part in enumerate((d_bx * v, d_c, d_bx * b)):
            part = part.astype(BF)
            grads[spots[0], i * cpad : (i + 1) * cpad] = part[:span]
            grads[spots[1], i * cpad : (i + 1) * cpad] = part[span:]
        for i, term in enumerate((by_two, by_one, bx)):
            term = jnp.sum(d_conv * term, axis=0, keepdims=True)
            sums[i] = term if sums[i] is None else sums[i] + term
    for i in range(3):
        conv_grad[i : i + 1] += sums[i]
    low = dot_nt(grads[:rows], w[...]).astype(BF)
    high = dot_nt(grads[rows:], w[...]).astype(BF)
    even = nat[0] % 2 == 0
    far = step < pl.num_programs(0) // 2

    def keep(ref):
        @pl.when(even)
        def _():
            ref[0, 0] = low
            ref[0, 1] = high

        @pl.when(jnp.logical_not(even))
        def _():
            ref[0, 0] = high
            ref[0, 1] = low

    @pl.when(far)
    def _():
        keep(da_far)

    @pl.when(jnp.logical_not(far))
    def _():
        keep(da_near)

    term = dot_tn(a[...].reshape(2 * rows, a.shape[-1]), grads[...])

    @pl.when(first)
    def _():
        total[...] = term

    @pl.when(jnp.logical_not(first))
    def _():
        total[...] += term

    @pl.when(step == pl.num_programs(0) - 1)
    def _():
        d_part[...] = total[...].astype(BF)


def mix_backward(do_all, do_rim, a_all, bcx, w_in, taps, nat, sides, slots, span, edge):
    width = w_in.shape[0]
    cpad = w_in.shape[1] // 3
    rows = slots * span
    chips = sides // 2

    def side(i, r):
        return r[2 * ((i + chips) % sides)] // 2

    def main(y):
        return pl.BlockSpec((1, rows, cpad), lambda i, r: (2 * side(i, r) + y, 0, 0))

    def fixed(shape):
        return pl.BlockSpec(shape, lambda i, r: (0,) * len(shape))

    da_shape = jax.ShapeDtypeStruct((chips, 2, rows, width), BF)
    work = sides * 2 * rows * width * 3 * cpad * 4
    return pl.pallas_call(
        lambda *refs: mix_backward_body(cpad, slots, span, edge, *refs),
        grid_spec=pltpu.PrefetchScalarGridSpec(
            num_scalar_prefetch=1,
            grid=(sides,),
            in_specs=[
                main(0),
                main(1),
                pl.BlockSpec((1, edge, cpad), lambda i, r: (side(i, r), 0, 0)),
                pl.BlockSpec((1, 2, rows, width), lambda i, r: (side(i, r), 0, 0, 0)),
                pl.BlockSpec((1, 2 * rows + 2 * edge, 3 * cpad), lambda i, r: (side(i, r), 0, 0)),
                fixed(w_in.shape),
                fixed(taps.shape),
            ],
            out_specs=[
                fixed((width, 3 * cpad)),
                pl.BlockSpec((1, 2, rows, width), lambda i, r: (jnp.maximum(i - chips, 0), 0, 0, 0)),
                pl.BlockSpec((1, 2, rows, width), lambda i, r: (jnp.minimum(i, chips - 1), 0, 0, 0)),
                fixed((8, cpad)),
            ],
            scratch_shapes=[pltpu.VMEM((width, 3 * cpad), F32), pltpu.VMEM((2 * rows, 3 * cpad), BF)],
        ),
        out_shape=[
            jax.ShapeDtypeStruct((width, 3 * cpad), BF),
            da_shape,
            da_shape,
            jax.ShapeDtypeStruct((8, cpad), F32),
        ],
        compiler_params=pltpu.CompilerParams(vmem_limit_bytes=60 * 2**20),
        cost_estimate=pl.CostEstimate(flops=work, bytes_accessed=40 * 2**20, transcendentals=0),
        name="mix_backward",
    )(nat, do_all, do_all, do_rim, a_all, bcx, w_in, taps)


def attend_body(count, o, w, x, gain, o_cat, h1, a2):
    joined = jnp.concatenate([o[t] for t in range(count)], axis=1)
    o_cat[...] = joined
    total = x[...].astype(F32) + dot(joined, w[...])
    h1[...] = total
    a2[...] = (total * rms_scale(total) * gain[...]).astype(BF)


def attend(o, w_out, x, gain, block):
    count, rows, cpad = o.shape
    width = w_out.shape[1]

    def row(last):
        return pl.BlockSpec((block, last), lambda i: (i, 0))

    def fixed(shape):
        return pl.BlockSpec(shape, lambda i: (0,) * len(shape))

    return pl.pallas_call(
        lambda *refs: attend_body(count, *refs),
        grid=(rows // block,),
        in_specs=[
            pl.BlockSpec((count, block, cpad), lambda i: (0, i, 0)),
            fixed(w_out.shape),
            row(width),
            fixed(gain.shape),
        ],
        out_specs=[row(count * cpad), row(width), row(width)],
        out_shape=[
            jax.ShapeDtypeStruct((rows, count * cpad), BF),
            jax.ShapeDtypeStruct((rows, width), F32),
            jax.ShapeDtypeStruct((rows, width), BF),
        ],
        compiler_params=pltpu.CompilerParams(vmem_limit_bytes=40 * 2**20),
        cost_estimate=pl.CostEstimate(
            flops=2 * rows * width * count * cpad, bytes_accessed=14 * 2**20, transcendentals=0
        ),
        name="attend",
    )(o, w_out, x, gain)


def turn_body(count, terms, *refs):
    da2 = refs[0][...].astype(F32)
    for ref in refs[1:terms]:
        da2 = da2 + ref[...].astype(F32)
    d_out, h1, gain, w, dh1, datt, d_o = refs[terms:]
    values = h1[...]
    grad = d_out[...].astype(F32) + norm_back(da2, values, rms_scale(values), gain[...])
    dh1[...] = grad
    low = grad.astype(BF)
    datt[...] = low
    cpad = w.shape[0] // count
    for t in range(count):
        d_o[t] = dot_nt(low, w[t * cpad : (t + 1) * cpad]).astype(BF)


def turn(terms, d_out, h1, gain, w_out, count, block):
    rows, width = h1.shape
    cpad = w_out.shape[0] // count

    def row(last):
        return pl.BlockSpec((block, last), lambda i: (i, 0))

    def fixed(shape):
        return pl.BlockSpec(shape, lambda i: (0,) * len(shape))

    return pl.pallas_call(
        lambda *refs: turn_body(count, len(terms), *refs),
        grid=(rows // block,),
        in_specs=[row(width)] * (len(terms) + 2) + [fixed(gain.shape), fixed(w_out.shape)],
        out_specs=[row(width), row(width), pl.BlockSpec((count, block, cpad), lambda i: (0, i, 0))],
        out_shape=[
            jax.ShapeDtypeStruct((rows, width), F32),
            jax.ShapeDtypeStruct((rows, width), BF),
            jax.ShapeDtypeStruct((count, rows, cpad), BF),
        ],
        compiler_params=pltpu.CompilerParams(vmem_limit_bytes=40 * 2**20),
        cost_estimate=pl.CostEstimate(
            flops=2 * rows * width * count * cpad, bytes_accessed=20 * 2**20, transcendentals=0
        ),
        name="turn",
    )(*terms, d_out, h1, gain, w_out)


def finish_body(terms, *refs):
    da = refs[0][...].astype(F32)
    for ref in refs[1:terms]:
        da = da + ref[...].astype(F32)
    x, dh1, gain, out = refs[terms:]
    values = x[...].astype(F32)
    out[...] = dh1[...] + norm_back(da, values, rms_scale(values), gain[...])


def finish(terms, x, dh1, gain, block):
    rows, width = dh1.shape
    spec = pl.BlockSpec((block, width), lambda i: (i, 0))
    return pl.pallas_call(
        lambda *refs: finish_body(len(terms), *refs),
        grid=(rows // block,),
        in_specs=[spec] * (len(terms) + 2) + [pl.BlockSpec(gain.shape, lambda i: (0, 0))],
        out_specs=spec,
        out_shape=jax.ShapeDtypeStruct((rows, width), F32),
        compiler_params=pltpu.CompilerParams(vmem_limit_bytes=40 * 2**20),
        cost_estimate=pl.CostEstimate(flops=rows * width * 8, bytes_accessed=12 * 2**20, transcendentals=0),
        name="finish",
    )(*terms, x, dh1, gain)


def feed_body(hid, hpad, split, a2, d_out, w_both, w_down, m, d_both, f_near, f_far, da_near, da_far):
    gu = dot(a2[0], w_both[...])
    gate, up = gu[:, :hid], gu[:, hpad : hpad + hid]
    dm = dot_nt(d_out[0], w_down[...])
    sigma = 1.0 / (1.0 + jnp.exp(-gate))
    active = gate * sigma
    inner = (active * up).astype(BF)
    m[0] = inner
    if hpad > hid:
        none = jnp.zeros((gu.shape[0], hpad - hid), BF)
        d_both[0, :, hid:hpad] = none
        d_both[0, :, hpad + hid :] = none
    d_both[0, :, :hid] = (dm * up * (sigma * (1.0 + gate * (1.0 - sigma)))).astype(BF)
    d_both[0, :, hpad : hpad + hid] = (dm * active).astype(BF)
    f = dot(inner, w_down[...]).astype(BF)
    da2 = dot_nt(d_both[0], w_both[...]).astype(BF)

    @pl.when(pl.program_id(0) >= split)
    def _():
        f_near[0] = f
        da_near[0] = da2

    @pl.when(pl.program_id(0) < split)
    def _():
        f_far[0] = f
        da_far[0] = da2


def feed(a2_all, d_all, w_both, w_down):
    blocks, rows, width = a2_all.shape
    hid, hpad = w_down.shape[0], w_both.shape[1] // 2
    split = blocks // 2

    def part(last):
        return pl.BlockSpec((1, rows, last), lambda i: ((i + split) % blocks, 0, 0))

    near = pl.BlockSpec((1, rows, width), lambda i: (jnp.maximum(i - split, 0), 0, 0))
    far = pl.BlockSpec((1, rows, width), lambda i: (jnp.minimum(i, split - 1), 0, 0))
    half = jax.ShapeDtypeStruct((split, rows, width), BF)

    def fixed(shape):
        return pl.BlockSpec(shape, lambda i: (0,) * len(shape))

    return pl.pallas_call(
        lambda *refs: feed_body(hid, hpad, split, *refs),
        grid=(blocks,),
        in_specs=[part(width), part(width), fixed(w_both.shape), fixed(w_down.shape)],
        out_specs=[part(hid), part(2 * hpad), near, far, near, far],
        out_shape=[
            jax.ShapeDtypeStruct((blocks, rows, hid), BF),
            jax.ShapeDtypeStruct((blocks, rows, 2 * hpad), BF),
            half,
            half,
            half,
            half,
        ],
        compiler_params=pltpu.CompilerParams(vmem_limit_bytes=60 * 2**20),
        cost_estimate=pl.CostEstimate(
            flops=blocks * rows * width * hid * 12, bytes_accessed=64 * 2**20, transcendentals=blocks * rows * hid
        ),
        name="feed",
    )(a2_all, d_all, w_both, w_down)


def on_device(
    tokens,
    cotangent,
    lengths,
    in_weight,
    conv_weight,
    out_weight,
    gain_one,
    gain_two,
    gate_weight,
    up_weight,
    down_weight,
):
    nx, nc, nz, ny = (lax.axis_size(name) for name in ("x", "c", "z", "y"))
    sizes = (nx, nc, ny)
    ndp = nx * nc
    slots, span, width = tokens.shape
    conv_weight_early = conv_weight
    rows = slots * span
    own_in = in_weight.shape[0]
    own_hid = down_weight.shape[0]
    chan, hid = nz * own_in, nz * own_hid
    cpad, hpad = up_to(chan + 2, 128), up_to(hid, 128)
    edge = up_to(2 * slots, 16)
    hops = [(dx, dc, dy) for dc in range(nc) for dx in range(nx) for dy in range(ny)]
    sides = ndp
    line = Line(nz)
    row_y = lax.axis_index("y")
    here = [lax.axis_index(name) for name in GROUP]
    place = []
    for i in range(nx):
        for j in range(nc):
            for k in range(ny):
                far = [(to + n - at) % n for to, at, n in zip((i, j, k), here, sizes)]
                place.append((far[1] * nx + far[0]) * ny + far[2])
    place = jnp.stack(place).astype(jnp.int32)
    turn_at = []
    for dx, dc, dy in hops:
        at = [(at + far) % n for at, far, n in zip(here, (dx, dc, dy), sizes)]
        turn_at.append((at[0] * nc + at[1]) * ny + at[2])
    nat = jnp.stack(turn_at).astype(jnp.int32)
    first = (lax.axis_index("z") * ny + row_y) * span
    positions = first + jnp.arange(span, dtype=jnp.int32)
    mask = (positions[None, :] < lengths[:, None]).astype(F32).reshape(rows, 1)
    up_route = [(z, z + 1) for z in range(nz - 1)]
    down_route = [(z + 1, z) for z in range(nz - 1)]

    def rim(values, start):
        count, last = values.shape[0], values.shape[-1]
        some = values.reshape(count, slots, span, last)[:, :, start : start + 2].reshape(count, 2 * slots, last)
        return jnp.pad(some, ((0, 0), (0, edge - 2 * slots), (0, 0)))

    x_bf = tokens.reshape(rows, width)
    x = x_bf.astype(F32)
    d_out_bf = (mask * cotangent.reshape(rows, width).astype(F32)).astype(BF)

    plan = shuffle_plan(ndp, nz, ny)
    gains = jnp.stack([gain_one, gain_two], axis=1)
    cut = cut_columns([in_weight], own_in, cpad, plan, gains)
    cut = lax.all_to_all(cut, GROUP, 0, 0, tiled=True).reshape(ndp, ny, own_in, 3 * cpad)
    x_all = near_gather(x_bf, sizes)
    taps_here = jnp.pad(conv_weight.T, ((0, 0), (0, 128 - conv_weight.shape[0])))
    out_here = jnp.concatenate([out_weight, taps_here], axis=1)
    cut = line.fetch_all(cut)

    both = cut_columns([gate_weight, up_weight], own_hid, hpad, plan)
    both = lax.all_to_all(both, GROUP, 0, 0, tiled=True).reshape(ndp, ny * own_in, 2 * hpad)
    x_all, both, out_here = lax.optimization_barrier((x_all, both, out_here))
    w_out = line.fetch_all(out_here)
    w_both = lax.all_gather(both, "z", axis=1, tiled=True).reshape(width, 2 * hpad)

    x_all = far_gather(x_all, sizes)
    x_all = jnp.stack([x_all[h] for h in hops], axis=0)
    pair = x_all.reshape(sides, ny, rows, width)
    even = row_y == 0
    x_past = lax.ppermute(rim(jnp.where(even, pair[:, 1], pair[:, 0]), span - 2), "z", up_route)
    x_next = lax.ppermute(rim(jnp.where(even, pair[:, 0], pair[:, 1]), 0), "z", down_route)
    (x_all, x_past, x_next, w_out), (d_out_bf, down_weight, cut) = after(
        (x_all, x_past, x_next, w_out), (d_out_bf, down_weight, cut)
    )
    w_down = lax.all_gather(down_weight, "z", axis=0, tiled=True)
    w_in = line.place(cut, 1).reshape(width, 3 * cpad)
    gain_a = w_in[:, chan].astype(F32).reshape(1, width)
    gain_b = w_in[:, chan + 1].astype(F32).reshape(1, width)

    w_out = line.place(w_out, 0).reshape(chan, width + 128)
    taps = w_out[:, width : width + 8].astype(F32).T
    taps = jnp.pad(taps, ((0, 0), (0, cpad - chan)))
    w_out = w_out[:, :width]
    w_out = near_gather(w_out, sizes)
    d_all = near_gather(d_out_bf, sizes)

    a_all, bcx, o_all = mix_forward(x_all, x_past, x_next, w_in, gain_a, taps, place, sides, slots, span, edge)
    o_all, w_out = lax.optimization_barrier((o_all, w_out))
    o_own = lax.all_to_all(o_all.reshape(len(hops), rows, cpad), GROUP, 0, 0, tiled=True)
    o_own, d_all = lax.optimization_barrier((o_own, d_all))
    w_some = far_gather(w_out, sizes)
    d_all = far_gather(d_all, sizes)
    w_out = jnp.zeros((len(hops), cpad, width), BF)
    for i, h in enumerate(hops):
        w_out = lax.dynamic_update_slice(w_out, w_some[h][None], (turn_at[i], 0, 0))
    w_out = w_out.reshape(len(hops) * cpad, width)
    block = rows // 2
    o_cat, h1, a2 = attend(o_own, w_out, x_bf, gain_b, block)
    a2, d_all = lax.optimization_barrier((a2, d_all))
    d_all = jnp.stack([d_all[h] for h in hops], axis=0)
    a2_all = far_gather(near_gather(a2, sizes), sizes)
    a2_all = jnp.stack([a2_all[h] for h in hops], axis=0)

    m, d_both, f_near, f_far, da_near, da_far = feed(a2_all, d_all, w_both, w_down)
    hold = lax.optimization_barrier
    da2 = GroupSum(da_near, da_far, sizes)
    d_flat = d_all.reshape(-1, width)
    both_part = dot_tn(a2_all.reshape(-1, width), d_both.reshape(-1, 2 * hpad)).astype(BF)
    both_sum = lax.psum_scatter(
        both_part.reshape(ndp, nz * ny * own_in, 2 * hpad), "z", scatter_dimension=1, tiled=True
    )
    da2.cross, both_part = hold((da2.cross, both_part))
    da2.start_far()
    f = GroupSum(f_near, f_far, sizes)
    down_part = dot_tn(m.reshape(-1, hid), d_flat).astype(BF)
    da2.more, f.cross = hold((da2.more, f.cross))
    da2.start_near()
    da2.last, f.cross, down_part = hold((da2.last, f.cross, down_part))
    down_grad = lax.psum_scatter(down_part, "z", scatter_dimension=0, tiled=True).astype(F32)

    f.start_far()
    dh1, datt, do_own = turn(da2.terms(), d_out_bf, h1, gain_b, w_out, len(hops), block)
    do_all = lax.all_to_all(do_own, GROUP, 0, 0, tiled=True)
    out_part = dot_tn(o_cat, datt).astype(BF).reshape(len(hops), cpad, width)[:, :chan]
    out_near = jnp.stack(
        [lax.dynamic_index_in_dim(out_part, turn_at[i], 0, keepdims=False) for i in range(ndp)], axis=0
    )
    out_far = jnp.stack(
        [lax.dynamic_index_in_dim(out_part, turn_at[i], 0, keepdims=False) for i in range(ndp, 2 * ndp)], axis=0
    )
    out = GroupSum(out_near, out_far, sizes)
    do_all, f.more, out.cross = hold((do_all, f.more, out.cross))
    do_rim = lax.ppermute(rim(do_all.reshape(sides, ny, rows, cpad)[:, 0], 0), "z", down_route)
    do_rim, f.more, out.cross = hold((do_rim, f.more, out.cross))
    f.start_near()
    out.start_far()

    in_part, da_near, da_far, conv_part = mix_backward(
        do_all, do_rim, a_all, bcx, w_in, taps, nat, sides, slots, span, edge
    )
    (in_part, da_near, da_far, conv_part), f.last, out.more = hold(
        ((in_part, da_near, da_far, conv_part), f.last, out.more)
    )
    flat = (ndp, rows, width)
    da = GroupSum(da_near.reshape(flat), da_far.reshape(flat), sizes)
    in_sum = line.reduce_direct(in_part.reshape(ndp, nz, ny, own_in, 3 * cpad), 1)
    both_sum = lax.all_to_all(both_sum.reshape(ndp * ny, own_in, 2 * hpad), GROUP, 0, 0, tiled=True)
    da.cross, both_sum = hold((da.cross, both_sum))
    da.start_far()
    out.start_near()
    da.more, out.last, in_sum[1], in_sum[-1] = hold((da.more, out.last, in_sum[1], in_sum[-1]))
    da.start_near()
    out_sum = sum(term.astype(F32) for term in out.terms()).astype(BF)
    out_grad = line.reduce_direct(out_sum.reshape(nz, own_in, width), 0)
    conv_grad = line.reduce_direct(conv_part[:3, :chan].reshape(3, nz, own_in), 1)
    (gate_grad, up_grad), gain_two_grad = join_columns(
        both_sum, [gate_weight, up_weight], gain_two, own_hid, hpad, plan
    )
    total = h1
    for term in f.terms():
        total = total + term.astype(F32)
    mixed = (mask * total).astype(BF)
    in_sum, da.last, mixed = hold((in_sum, da.last, mixed))
    in_sum = sum(term.astype(F32) for term in in_sum).astype(BF)
    in_sum = lax.all_to_all(in_sum.reshape(ndp * ny, own_in, 3 * cpad), GROUP, 0, 0, tiled=True)
    input_grad = finish(da.terms(), x_bf, dh1, gain_a, block)
    out_grad = sum(term.astype(F32) for term in out_grad)
    conv_grad = sum(conv_grad)
    (in_grad,), gain_one_grad = join_columns(in_sum, [in_weight], gain_one, own_in, cpad, plan)
    return (
        mixed.reshape(slots, span, width),
        input_grad.reshape(slots, span, width),
        in_grad,
        conv_grad,
        out_grad,
        gain_one_grad,
        gain_two_grad,
        gate_grad,
        up_grad,
        down_grad,
    )


def solution(mesh):
    dp, seq = mesh.shape["dp"], mesh.shape["seq"]
    fine = Mesh(mesh.devices.reshape(dp // 2, 2, seq // 2, 2), ("x", "c", "z", "y"))
    slot, place = ("x", "c"), ("z", "y")
    every = slot + place
    in_specs = (
        P(slot, place, None),
        P(slot, place, None),
        P(slot),
        P(every, None),
        P(None, every),
        P(every, None),
        P(every),
        P(every),
        P(every, None),
        P(every, None),
        P(every, None),
    )
    out_specs = (
        P(slot, place, None),
        P(slot, place, None),
        P(every, None),
        P(None, every),
        P(every, None),
        P(every),
        P(every),
        P(every, None),
        P(every, None),
        P(every, None),
    )
    return jax.shard_map(
        on_device, mesh=fine, in_specs=in_specs, out_specs=out_specs, check_vma=False
    )
```

time: 984 us -> 684 us (0.70)
  matrix products: 175 us -> 37.9 us
  Pallas kernels: 0 us -> 137 us
  local copies, waits for them, and re-layouts: 197 us -> 86.4 us
  other arithmetic: 137 us -> 50.8 us
  blocking collectives: 73.2 us -> 0 us
  waiting for transfers between devices: 291 us -> 236 us
  between operations: 2.78 us -> 15.8 us
  starting transfers between devices: 97.9 us -> 109 us
    pallas_call x0 -> x10, Pallas kernels: none -> 137 us  [the longest x1 65.1 us: feed(): pl.pallas_call(lambda *refs: feed_body(hid, hpad, split, *refs), grid=(bl...]
    dot_general x8 -> x0, matrix products: 122 us -> none  [the longest x4 66.7 us: dot_nt(): lax.dot_general(left, right, (((1,), (1,)), ((), ())), preferred_element_...]
    ppermute x29 -> x18, waiting for transfers between devices: 137 us -> 48.1 us  [the longest x9 37.2 us: reduce_direct(): terms.append(lax.ppermute(part, 'z', route))]
    all_gather x1 -> x0, blocking collectives: 64.6 us -> none  [on_device(): lax.all_gather(jnp.stack([gain_one, gain_two], axis=0), ('x', 'c', 'z', '...]
    reduce_sum x8 -> x0, other arithmetic: 32.6 us -> none  [the longest x1 16.3 us: on_device(): jnp.sum(d_conv * past_two, axis=all_rows)]
    reshape x9 -> x6, local copies, waits for them, and re-layouts: 27.4 us -> 1.52 us  [the longest x2 1.39 us: join_columns(): gain = gain.astype(F32).reshape(rows, 1)]
    convert_element_type x11 -> x2, local copies, waits for them, and re-layouts: 24.7 us -> 0.61 us  [the longest x1 0.6 us: on_device(): gain_a = w_in[:, chan].astype(F32).reshape(1, width)]
    unnamed x228 -> x133, local copies, waits for them, and re-layouts: 45.6 us -> 27.6 us
  transfers between devices with their start and end apart: 111 -> 80, of which waited for: 40 -> 29; matrix products, arithmetic and copies ran while one was open for 37% -> 23% of each run, Pallas kernels for 0% -> 10%
where the time goes in v2:
time: 684 us; the launch traced here: 674 us
  waiting for transfers between devices  236 us (35%)
  Pallas kernels  137 us (20%)
  starting transfers between devices  109 us (16%)
  local copies, waits for them, and re-layouts  86.4 us (13%)
  other arithmetic  50.8 us (7%)
  matrix products  37.9 us (6%)
  between operations  15.8 us (2%)
    ppermute x52, waiting for transfers between devices, send(): return lax.ppermute(block, GROUP, route)  159 us
    pallas_call x1, Pallas kernels, feed(): pl.pallas_call(lambda *refs: feed_body(hid, hpad, split, *refs), grid=(bl...  65.1 us
    ppermute x52, starting transfers between devices, send(): return lax.ppermute(block, GROUP, route)  41.9 us
    dot_general x3, matrix products, dot_tn(): lax.dot_general(left, right, (((0,), (0,)), ((), ())), preferred_element_...  37.9 us
    ppermute x9, waiting for transfers between devices, reduce_direct(): terms.append(lax.ppermute(part, 'z', route))  37.2 us
    pallas_call x1, Pallas kernels, mix_backward(): pl.pallas_call(lambda *refs: mix_backward_body(cpad, slots, span, edge, *...  28.9 us
    unnamed x133, local copies, waits for them, and re-layouts  27.6 us
    ppermute x9, starting transfers between devices, reduce_direct(): terms.append(lax.ppermute(part, 'z', route))  21.7 us
  transfers between devices with their start and end apart: 80, of which 29 were waited for; matrix products, arithmetic and copies ran while one was open for 23% of the time, Pallas kernels for 10%

profile of v2, /device:TPU:0, one launch (start us, length us, event | category | flops | bytes accessed | tf_op | source)
XLA Modules:
  0.0 673.8 jit_solution(5777527692711710923)
XLA Ops:
  10.4 5.2 all-to-all-start.1
  17.2 8.0 %all-to-all-done.1 = bf16[8,48,768]{2,1,0:T(8,128)(2,1)} async-done(((bf16[8,48,768]{2,1,0:T(8,128)(2,1)}), bf16[8,48,768]{2,1,0:T(8,128)(2,1)}, u32[]{:S(2)}, u32[]{:S(2)}) %all-to-all-start.1) | async-done | bytes 589856 | tf_op jit(solution)/shard_map/all_to_all | solution.py:732
  25.2 4.3 all-to-all-start
  39.8 32.8 %collective-permute-done = bf16[384,1536]{1,0:T(8,128)(2,1)S(1)} collective-permute-done((bf16[384,1536]{1,0:T(8,128)(2,1)S(1)}, bf16[384,1536]{1,0:T(8,128)(2,1)S(1)}, u32[]{:S(2)}, u32[]{:S(2)}) %collective-permute-start) | collective-permute-done | bytes 1179680 | tf_op jit(solution)/shard_map/ppermute | solution.py:28
  75.3 13.4 %collective-permute-done.2 = bf16[192,1536]{1,0:T(8,128)(2,1)S(1)} collective-permute-done((bf16[192,1536]{1,0:T(8,128)(2,1)S(1)}, bf16[192,1536]{1,0:T(8,128)(2,1)S(1)}, u32[]{:S(2)}, u32[]{:S(2)}) %collective-permute-start.2) | collective-permute-done | bytes 589856 | tf_op jit(solution)/shard_map/ppermute | solution.py:28
  138.5 16.2 %mix_forward.1 = (bf16[4,2,384,1536]{3,2,1,0:T(8,128)(2,1)}, f32[4,800,768]{2,1,0:T(8,128)}, bf16[4,2,384,256]{3,2,1,0:T(8,128)(2,1)}) custom-call(s32[8]{0:T(128)} %stack.168.refs_0_, bf16[8,384,1536]{2,1,0:T(8,128)(2,1)} %copy-done.22, bf16[8,384,1536]{2,1,0:T(8,128)(2,1)} %copy-done.22, bf16[4,16,1536]{2,1,0:T(8,128)(2,1)} %copy-done.42, ...), custom_call_target="tpu_custom_call" | custom-call | flops 7549747200 | bytes 33554432 | tf_op jit(solution)/shard_map/mix_forward/pallas_call | solution.py:348
  154.6 4.3 all-to-all-start.2
  173.3 16.9 %collective-permute-done.20 = bf16[96,1536]{1,0:T(8,128)(2,1)S(1)} collective-permute-done((bf16[96,1536]{1,0:T(8,128)(2,1)S(1)}, bf16[96,1536]{1,0:T(8,128)(2,1)S(1)}, u32[]{:S(2)}, u32[]{:S(2)}) %collective-permute-start.20) | collective-permute-done | bytes 294944 | tf_op jit(solution)/shard_map/ppermute | solution.py:28
  201.8 9.3 %collective-permute-done.28 = bf16[192,1536]{1,0:T(8,128)(2,1)S(1)} collective-permute-done((bf16[192,1536]{1,0:T(8,128)(2,1)S(1)}, bf16[192,1536]{1,0:T(8,128)(2,1)S(1)}, u32[]{:S(2)}, u32[]{:S(2)}) %collective-permute-start.28) | collective-permute-done | bytes 589856 | tf_op jit(solution)/shard_map/ppermute | solution.py:28
  218.8 6.3 attend.1
  230.3 23.2 %collective-permute-done.33 = bf16[384,1536]{1,0:T(8,128)(2,1)S(1)} collective-permute-done((bf16[384,1536]{1,0:T(8,128)(2,1)S(1)}, bf16[384,1536]{1,0:T(8,128)(2,1)S(1)}, u32[]{:S(2)}, u32[]{:S(2)}) %collective-permute-start.33) | collective-permute-done | bytes 1179680 | tf_op jit(solution)/shard_map/ppermute | solution.py:28
  258.3 9.4 %collective-permute-done.34 = bf16[192,1536]{1,0:T(8,128)(2,1)S(1)} collective-permute-done((bf16[192,1536]{1,0:T(8,128)(2,1)S(1)}, bf16[192,1536]{1,0:T(8,128)(2,1)S(1)}, u32[]{:S(2)}, u32[]{:S(2)}) %collective-permute-start.34) | collective-permute-done | bytes 589856 | tf_op jit(solution)/shard_map/ppermute | solution.py:28
  274.7 9.2 %all-gather.3.cloned.1.call-done = bf16[4,384,1792]{2,1,0:T(8,128)(2,1)} async-done(((bf16[4,96,1792]{2,1,0:T(8,128)(2,1)}), bf16[4,384,1792]{2,1,0:T(8,128)(2,1)}) %all-gather.3.cloned.1.call-update) | async-done | bytes 5505040 | tf_op jit(solution)/shard_map/all_gather | solution.py:742
  283.9 65.1 %feed.1 = (bf16[8,384,864]{2,1,0:T(8,128)(2,1)}, bf16[8,384,1792]{2,1,0:T(8,128)(2,1)}, bf16[4,384,1536]{2,1,0:T(8,128)(2,1)}, bf16[4,384,1536]{2,1,0:T(8,128)(2...) custom-call(bf16[8,384,1536]{2,1,0:T(8,128)(2,1)} %bitcast_dynamic-update-slice_fusion.8.refs_0_, ...), custom_call_target="tpu_custom_call" | custom-call | flops 48922361856 | bytes 67108864 | tf_op jit(solution)/shard_map/feed/pallas_call | solution.py:652
  349.6 24.2 %bitcast_convert_fusion = bf16[1536,1792]{1,0:T(8,128)(2,1)} fusion(bf16[8,384,1536]{2,1,0:T(8,128)(2,1)} %bitcast_dynamic-update-slice_fusion.8.refs_0_, bf16[8,384,1792]{2,1,0:T(8,128)(2,1)} %get-tuple-element.147), kind=kOutput, calls=%fused_computation | convolution fusion | flops 16914186240 | bytes 25952256 | tf_op jit(solution)/shard_map/dot_general | solution.py:167
  373.8 4.2 convert_add_fusion.6
  381.3 12.2 %collective-permute-done.41 = bf16[192,1536]{1,0:T(8,128)(2,1)S(1)} collective-permute-done((bf16[192,1536]{1,0:T(8,128)(2,1)S(1)}, bf16[192,1536]{1,0:T(8,128)(2,1)S(1)}, u32[]{:S(2)}, u32[]{:S(2)}) %collective-permute-start.41) | collective-permute-done | bytes 589856 | tf_op jit(solution)/shard_map/ppermute | solution.py:28
  399.2 10.0 %bitcast_convert_fusion.1 = bf16[864,1536]{1,0:T(8,128)(2,1)} fusion(bf16[8,384,864]{2,1,0:T(8,128)(2,1)S(1)} %bitcast.323, bf16[8,384,1536]{2,1,0:T(8,128)(2,1)S(1)} %bitcast.311), kind=kOutput, calls=%fused_computation.2 | convolution fusion | flops 8155054080 | bytes 17399808 | tf_op jit(solution)/shard_map/dot_general | solution.py:167
  412.1 10.9 %collective-permute-done.44.refs_2_ = bf16[384,1536]{1,0:T(8,128)(2,1)S(1)} collective-permute-done((bf16[384,1536]{1,0:T(8,128)(2,1)}, bf16[384,1536]{1,0:T(8,128)(2,1)S(1)}, u32[]{:S(2)}, u32[]{:S(2)}) %collective-permute-start.44) | collective-permute-done | bytes 1179680 | tf_op jit(solution)/shard_map/ppermute | solution.py:28
  425.5 8.9 %turn.1 = (f32[384,1536]{1,0:T(8,128)S(1)}, bf16[384,1536]{1,0:T(8,128)(2,1)S(1)}, bf16[8,384,256]{2,1,0:T(8,128)(2,1)S(1)}) custom-call(bf16[384,1536]{1,0:T(8,128)(2,1)S(1)} %slice_bitcast_fusion.9.refs_0_, bf16[384,1536]{1,0:T(8,128)(2,1)S(1)} %slice_bitcast_fusion.8.refs_1_, bf16[384,1536]{1,0:T(8,128)(2,1)S(1)} %collective-permute-done.44.refs_2_, ...), custom_call_target="tpu_custom_call" | custom-call | flops 2415919104 | bytes 20971520 | tf_op jit(solution)/shard_map/turn/pallas_call | solution.py:567
  442.4 4.3 all-to-all-start.3
  446.7 6.3 convert_add_fusion.4
  459.4 20.0 %collective-permute-done.46 = bf16[192,1536]{1,0:T(8,128)(2,1)S(1)} collective-permute-done((bf16[192,1536]{1,0:T(8,128)(2,1)}, bf16[192,1536]{1,0:T(8,128)(2,1)S(1)}, u32[]{:S(2)}, u32[]{:S(2)}) %collective-permute-start.46) | collective-permute-done | bytes 589856 | tf_op jit(solution)/shard_map/ppermute | solution.py:28
  498.8 28.9 %mix_backward.1 = (bf16[1536,768]{1,0:T(8,128)(2,1)}, bf16[2,2,384,1536]{3,2,1,0:T(8,128)(2,1)}, bf16[2,2,384,1536]{3,2,1,0:T(8,128)(2,1)}, f32[8,256]{1,0:T(8,128)}) custom-call(s32[8]{0:T(128)} %stack.159.refs_0_, bf16[8,384,256]{2,1,0:T(8,128)(2,1)} %all-to-all-done.3.refs_1_.refs_2_, bf16[8,384,256]{2,1,0:T(8,128)(2,1)} %all-to-all-done.3.refs_1_.refs_2_, ...), custom_call_target="tpu_custom_call" | custom-call | flops 14495514624 | bytes 41943040 | tf_op jit(solution)/shard_map/mix_backward/pallas_call | solution.py:467
  534.5 4.3 all-to-all-start.4
  546.1 5.0 fusion.3
  551.0 11.3 %all-to-all-done.4.refs_0_ = bf16[8,48,1792]{2,1,0:T(8,128)(2,1)} async-done(((bf16[8,48,1792]{2,1,0:T(8,128)(2,1)}), bf16[8,48,1792]{2,1,0:T(8,128)(2,1)}, u32[]{:S(2)}, u32[]{:S(2)}) %all-to-all-start.4) | async-done | bytes 1376288 | tf_op jit(solution)/shard_map/all_to_all | solution.py:825
  569.5 26.5 %collective-permute-done.59 = bf16[4,2,48,768]{3,2,1,0:T(8,128)(2,1)S(1)} collective-permute-done((bf16[4,2,48,768]{3,2,1,0:T(8,128)(2,1)}, bf16[4,2,48,768]{3,2,1,0:T(8,128)(2,1)S(1)}, u32[]{:S(2)}, u32[]{:S(2)}) %collective-permute-start.59) | collective-permute-done | bytes 589856 | tf_op jit(solution)/shard_map/ppermute | solution.py:154
  615.8 7.8 %collective-permute-done.61 = bf16[4,2,48,768]{3,2,1,0:T(8,128)(2,1)} collective-permute-done((bf16[4,2,48,768]{3,2,1,0:T(8,128)(2,1)}, bf16[4,2,48,768]{3,2,1,0:T(8,128)(2,1)}, u32[]{:S(2)}, u32[]{:S(2)}) %collective-permute-start.61) | collective-permute-done | bytes 589856 | tf_op jit(solution)/shard_map/ppermute | solution.py:154
  623.6 13.9 %collective-permute-start.67 = (bf16[48,1536]{1,0:T(8,128)(2,1)}, bf16[48,1536]{1,0:T(8,128)(2,1)}, u32[]{:S(2)}, u32[]{:S(2)}) collective-permute-start(bf16[48,1536]{1,0:T(8,128)(2,1)} %get-tuple-element.236), channel_id=1, source_target_pairs={{0,4},{2,0},{6,2},{4,6},{1,5},{3,1},{7,3},{5,7},{8,12},{10,8},{14,... | collective-permute-start | bytes 442376 | tf_op jit(solution)/shard_map/ppermute | solution.py:154
  640.9 4.6 all-to-all-start.5
  658.3 4.2 finish.1
  (398 shorter events, 226.8 us)
Async XLA Ops:
  25.2 47.5 %all-to-all-start = ((bf16[8,48,1792]{2,1,0:T(8,128)(2,1)}), bf16[8,48,1792]{2,1,0:T(8,128)(2,1)}, u32[]{:S(2)}, u32[]{:S(2)}) async-start(bf16[8,48,1792]{2,1,0:T(8,128)(2,1)} %copy-done.3), calls=%async_computation | async-start | bytes 2752512 | tf_op jit(solution)/shard_map/all_to_all | solution.py:739
  29.5 245.2 %all-gather.5.cloned.1.call-start = ((), (), s32[]{:S(2)}) async-start(), calls=%async_computation.9 | async-start | bytes 3317760 | tf_op jit(solution)/shard_map/all_gather | solution.py:753
  29.6 43.1 %collective-permute-start = (bf16[384,1536]{1,0:T(8,128)(2,1)S(1)}, bf16[384,1536]{1,0:T(8,128)(2,1)S(1)}, u32[]{:S(2)}, u32[]{:S(2)}) collective-permute-start(bf16[384,1536]{1,0:T(8,128)(2,1)S(1)} %bitcast.281), channel_id=1, source_target_pairs={{0,1},{1,0},{8,9},{9,8},{16,17},{17,16},{24,25},{25,24},{2,3},{3,2... | collective-permute-start | bytes 3538952 | tf_op jit(solution)/shard_map/ppermute | solution.py:28
  31.5 41.3 %collective-permute-start.1 = (bf16[384,1536]{1,0:T(8,128)(2,1)S(1)}, bf16[384,1536]{1,0:T(8,128)(2,1)S(1)}, u32[]{:S(2)}, u32[]{:S(2)}) collective-permute-start(bf16[384,1536]{1,0:T(8,128)(2,1)S(1)} %bitcast.282), channel_id=1, source_target_pairs={{0,16},{1,17},{8,24},{9,25},{16,0},{17,1},{24,8},{25,9},{2,18},{3,... | collective-permute-start | bytes 3538952 | tf_op jit(solution)/shard_map/ppermute | solution.py:28
  35.4 74.8 %collective-permute-start.13 = (bf16[4,2,48,768]{3,2,1,0:T(8,128)(2,1)}, bf16[4,2,48,768]{3,2,1,0:T(8,128)(2,1)}, u32[]{:S(2)}, u32[]{:S(2)}) collective-permute-start(bf16[4,2,48,768]{3,2,1,0:T(8,128)(2,1)} %bitcast.36), channel_id=1, source_target_pairs={{0,2},{2,6},{6,4},{4,0},{1,3},{3,7},{7,5},{5,1},{8,10},{10,14},{14... | collective-permute-start | bytes 1769480 | tf_op jit(solution)/shard_map/ppermute | solution.py:138
  37.3 73.8 %collective-permute-start.14 = (bf16[4,2,48,768]{3,2,1,0:T(8,128)(2,1)}, bf16[4,2,48,768]{3,2,1,0:T(8,128)(2,1)}, u32[]{:S(2)}, u32[]{:S(2)}) collective-permute-start(bf16[4,2,48,768]{3,2,1,0:T(8,128)(2,1)} %bitcast.36), channel_id=1, source_target_pairs={{0,6},{2,4},{6,0},{4,2},{1,7},{3,5},{7,1},{5,3},{8,14},{10,12},{14... | collective-permute-start | bytes 1769480 | tf_op jit(solution)/shard_map/ppermute | solution.py:138
  124.0 160.0 %all-gather.3.cloned.1.call-start = ((), (), s32[]{:S(2)}) async-start(), calls=%async_computation.8 | async-start | bytes 6881280 | tf_op jit(solution)/shard_map/all_gather | solution.py:742
  128.6 65.6 %collective-permute-start.18 = (bf16[384,1536]{1,0:T(8,128)(2,1)S(1)}, bf16[384,1536]{1,0:T(8,128)(2,1)S(1)}, u32[]{:S(2)}, u32[]{:S(2)}) collective-permute-start(bf16[384,1536]{1,0:T(8,128)(2,1)S(1)} %fusion.4.refs_4_), channel_id=1, source_target_pairs={{0,1},{1,0},{8,9},{9,8},{16,17},{17,16},{24,25},{25,24},{2,3},{3,2... | collective-permute-start | bytes 3538952 | tf_op jit(solution)/shard_map/ppermute | solution.py:28
  130.0 64.7 %collective-permute-start.19 = (bf16[384,1536]{1,0:T(8,128)(2,1)S(1)}, bf16[384,1536]{1,0:T(8,128)(2,1)}, u32[]{:S(2)}, u32[]{:S(2)}) collective-permute-start(bf16[384,1536]{1,0:T(8,128)(2,1)S(1)} %fusion.4.refs_4_), channel_id=1, source_target_pairs={{0,16},{1,17},{8,24},{9,25},{16,0},{17,1},{24,8},{25,9},{2,18},{3,... | collective-permute-start | bytes 3538952 | tf_op jit(solution)/shard_map/ppermute | solution.py:28
  154.6 40.1 %all-to-all-start.2 = ((bf16[8,384,256]{2,1,0:T(8,128)(2,1)}), bf16[8,384,256]{2,1,0:T(8,128)(2,1)}, u32[]{:S(2)}, u32[]{:S(2)}) async-start(bf16[8,384,256]{2,1,0:T(8,128)(2,1)} %bitcast.304), calls=%async_computation.2 | async-start | bytes 3145728 | tf_op jit(solution)/shard_map/all_to_all | solution.py:767
  158.9 375.6 %reduce-scatter.3.cloned.1.call-start = ((), (), s32[]{:S(2)}) async-start(), calls=%async_computation.10 | async-start | bytes 6881280 | tf_op jit(solution)/shard_map/reduce_scatter | solution.py:787
  164.4 32.4 %collective-permute-start.22 = (bf16[192,1536]{1,0:T(8,128)(2,1)}, bf16[192,1536]{1,0:T(8,128)(2,1)}, u32[]{:S(2)}, u32[]{:S(2)}) collective-permute-start(bf16[192,1536]{1,0:T(8,128)(2,1)} %slice.400), channel_id=1, source_target_pairs={{0,8},{1,9},{8,0},{9,1},{16,24},{17,25},{24,16},{25,17},{2,10},{3,... | collective-permute-start | bytes 1769480 | tf_op jit(solution)/shard_map/ppermute | solution.py:28
  227.2 43.1 %collective-permute-start.36 = (bf16[384,1536]{1,0:T(8,128)(2,1)S(1)}, bf16[384,1536]{1,0:T(8,128)(2,1)S(1)}, u32[]{:S(2)}, u32[]{:S(2)}) collective-permute-start(bf16[384,1536]{1,0:T(8,128)(2,1)S(1)} %get-tuple-element.134), channel_id=1, source_target_pairs={{0,8},{1,9},{8,0},{9,1},{16,24},{17,25},{24,16},{25,17},{2,10},{3,... | collective-permute-start | bytes 3538952 | tf_op jit(solution)/shard_map/ppermute | solution.py:28
  349.1 32.2 %collective-permute-start.43 = (bf16[4,384,1536]{2,1,0:T(8,128)(2,1)}, bf16[4,384,1536]{2,1,0:T(8,128)(2,1)}, u32[]{:S(2)}, u32[]{:S(2)}) collective-permute-start(bf16[4,384,1536]{2,1,0:T(8,128)(2,1)} %get-tuple-element.149), channel_id=1, source_target_pairs={{0,8},{1,9},{8,0},{9,1},{16,24},{17,25},{24,16},{25,17},{2,10},{3,... | collective-permute-start | bytes 14155784 | tf_op jit(solution)/shard_map/ppermute | solution.py:28
  442.4 37.0 %collective-permute-start.48 = (bf16[4,192,1536]{2,1,0:T(8,128)(2,1)}, bf16[4,192,1536]{2,1,0:T(8,128)(2,1)}, u32[]{:S(2)}, u32[]{:S(2)}) collective-permute-start(bf16[4,192,1536]{2,1,0:T(8,128)(2,1)} %pad_maximum_fusion), channel_id=1, source_target_pairs={{0,8},{1,9},{8,0},{9,1},{16,24},{17,25},{24,16},{25,17},{2,10},{3,... | collective-permute-start | bytes 7077896 | tf_op jit(solution)/shard_map/ppermute | solution.py:28
  442.4 37.0 %all-to-all-start.3 = ((bf16[8,384,256]{2,1,0:T(8,128)(2,1)}), bf16[8,384,256]{2,1,0:T(8,128)(2,1)}, u32[]{:S(2)}, u32[]{:S(2)}) async-start(bf16[8,384,256]{2,1,0:T(8,128)(2,1)} %copy-done.13), calls=%async_computation.3 | async-start | bytes 3145728 | tf_op jit(solution)/shard_map/all_to_all | solution.py:801
  446.6 160.9 %reduce-scatter.5.cloned.1.call-start = ((), (), s32[]{:S(2)}) async-start(), calls=%async_computation.11 | async-start | bytes 3317760 | tf_op jit(solution)/shard_map/reduce_scatter | solution.py:797
  490.4 37.4 %collective-permute-start.50 = (bf16[384,1536]{1,0:T(8,128)(2,1)}, bf16[384,1536]{1,0:T(8,128)(2,1)}, u32[]{:S(2)}, u32[]{:S(2)}) collective-permute-start(bf16[384,1536]{1,0:T(8,128)(2,1)} %pad_maximum_fusion.3), channel_id=1, source_target_pairs={{0,1},{1,0},{8,9},{9,8},{16,17},{17,16},{24,25},{25,24},{2,3},{3,2... | collective-permute-start | bytes 3538952 | tf_op jit(solution)/shard_map/ppermute | solution.py:28
  493.1 34.7 %collective-permute-start.51 = (bf16[384,1536]{1,0:T(8,128)(2,1)}, bf16[384,1536]{1,0:T(8,128)(2,1)}, u32[]{:S(2)}, u32[]{:S(2)}) collective-permute-start(bf16[384,1536]{1,0:T(8,128)(2,1)} %pad_maximum_fusion.4), channel_id=1, source_target_pairs={{0,16},{1,17},{8,24},{9,25},{16,0},{17,1},{24,8},{25,9},{2,18},{3,... | collective-permute-start | bytes 3538952 | tf_op jit(solution)/shard_map/ppermute | solution.py:28
  496.8 31.0 %collective-permute-start.52 = (bf16[96,1536]{1,0:T(8,128)(2,1)}, bf16[96,1536]{1,0:T(8,128)(2,1)}, u32[]{:S(2)}, u32[]{:S(2)}) collective-permute-start(bf16[96,1536]{1,0:T(8,128)(2,1)} %get-tuple-element.240), channel_id=1, source_target_pairs={{0,16},{1,17},{8,24},{9,25},{16,0},{17,1},{24,8},{25,9},{2,18},{3,... | collective-permute-start | bytes 884744 | tf_op jit(solution)/shard_map/ppermute | solution.py:28
  527.8 34.6 %collective-permute-start.54 = (bf16[4,384,1536]{2,1,0:T(8,128)(2,1)}, bf16[4,384,1536]{2,1,0:T(8,128)(2,1)}, u32[]{:S(2)}, u32[]{:S(2)}) collective-permute-start(bf16[4,384,1536]{2,1,0:T(8,128)(2,1)} %bitcast.319), channel_id=1, source_target_pairs={{0,8},{1,9},{8,0},{9,1},{16,24},{17,25},{24,16},{25,17},{2,10},{3,... | collective-permute-start | bytes 14155784 | tf_op jit(solution)/shard_map/ppermute | solution.py:28
  532.0 35.1 %collective-permute-start.57 = (bf16[192,1536]{1,0:T(8,128)(2,1)}, bf16[192,1536]{1,0:T(8,128)(2,1)}, u32[]{:S(2)}, u32[]{:S(2)}) collective-permute-start(bf16[192,1536]{1,0:T(8,128)(2,1)} %pad_maximum_fusion.7), channel_id=1, source_target_pairs={{0,1},{1,0},{8,9},{9,8},{16,17},{17,16},{24,25},{25,24},{2,3},{3,2... | collective-permute-start | bytes 1769480 | tf_op jit(solution)/shard_map/ppermute | solution.py:28
  538.9 30.6 %collective-permute-start.58 = (bf16[192,1536]{1,0:T(8,128)(2,1)S(1)}, bf16[192,1536]{1,0:T(8,128)(2,1)}, u32[]{:S(2)}, u32[]{:S(2)}) collective-permute-start(bf16[192,1536]{1,0:T(8,128)(2,1)S(1)} %pad_maximum_fusion.8), channel_id=1, source_target_pairs={{0,16},{1,17},{8,24},{9,25},{16,0},{17,1},{24,8},{25,9},{2,18},{3,... | collective-permute-start | bytes 1769480 | tf_op jit(solution)/shard_map/ppermute | solution.py:28
  543.9 52.1 %collective-permute-start.59 = (bf16[4,2,48,768]{3,2,1,0:T(8,128)(2,1)}, bf16[4,2,48,768]{3,2,1,0:T(8,128)(2,1)S(1)}, u32[]{:S(2)}, u32[]{:S(2)}) collective-permute-start(bf16[4,2,48,768]{3,2,1,0:T(8,128)(2,1)} %get-tuple-element.228), channel_id=1, source_target_pairs={{0,4},{2,0},{6,2},{4,6},{1,5},{3,1},{7,3},{5,7},{8,12},{10,8},{14,... | collective-permute-start | bytes 1769480 | tf_op jit(solution)/shard_map/ppermute | solution.py:154
  544.6 55.1 %collective-permute-start.60 = (bf16[4,2,48,768]{3,2,1,0:T(8,128)(2,1)}, bf16[4,2,48,768]{3,2,1,0:T(8,128)(2,1)}, u32[]{:S(2)}, u32[]{:S(2)}) collective-permute-start(bf16[4,2,48,768]{3,2,1,0:T(8,128)(2,1)} %get-tuple-element.227), channel_id=1, source_target_pairs={{0,2},{2,6},{6,4},{4,0},{1,3},{3,7},{7,5},{5,1},{8,10},{10,14},{14... | collective-permute-start | bytes 1769480 | tf_op jit(solution)/shard_map/ppermute | solution.py:154
  566.5 33.2 %collective-permute-start.55 = (bf16[192,1536]{1,0:T(8,128)(2,1)S(1)}, bf16[192,1536]{1,0:T(8,128)(2,1)S(1)}, u32[]{:S(2)}, u32[]{:S(2)}) collective-permute-start(bf16[192,1536]{1,0:T(8,128)(2,1)S(1)} %get-tuple-element.231), channel_id=1, source_target_pairs={{0,16},{1,17},{8,24},{9,25},{16,0},{17,1},{24,8},{25,9},{2,18},{3,... | collective-permute-start | bytes 1769480 | tf_op jit(solution)/shard_map/ppermute | solution.py:28
  567.1 32.6 %collective-permute-start.56 = (bf16[192,1536]{1,0:T(8,128)(2,1)S(1)}, bf16[192,1536]{1,0:T(8,128)(2,1)S(1)}, u32[]{:S(2)}, u32[]{:S(2)}) collective-permute-start(bf16[192,1536]{1,0:T(8,128)(2,1)S(1)} %get-tuple-element.230), channel_id=1, source_target_pairs={{0,1},{1,0},{8,9},{9,8},{16,17},{17,16},{24,25},{25,24},{2,3},{3,2... | collective-permute-start | bytes 1769480 | tf_op jit(solution)/shard_map/ppermute | solution.py:28
  569.5 35.6 %collective-permute-start.66 = (f32[3,48]{1,0:T(4,128)S(1)}, f32[3,48]{1,0:T(4,128)S(1)}, u32[]{:S(2)}, u32[]{:S(2)}) collective-permute-start(f32[3,48]{1,0:T(4,128)S(1)} %bitcast.317), channel_id=1, source_target_pairs={{0,2},{2,6},{6,4},{4,0},{1,3},{3,7},{7,5},{5,1},{8,10},{10,14},{14... | collective-permute-start | bytes 1736 | tf_op jit(solution)/shard_map/ppermute | solution.py:154
  601.0 36.5 %collective-permute-start.62 = (bf16[384,1536]{1,0:T(8,128)(2,1)}, bf16[384,1536]{1,0:T(8,128)(2,1)S(1)}, u32[]{:S(2)}, u32[]{:S(2)}) collective-permute-start(bf16[384,1536]{1,0:T(8,128)(2,1)} %pad_maximum_fusion.5), channel_id=1, source_target_pairs={{0,1},{1,0},{8,9},{9,8},{16,17},{17,16},{24,25},{25,24},{2,3},{3,2... | collective-permute-start | bytes 3538952 | tf_op jit(solution)/shard_map/ppermute | solution.py:28
  603.7 34.9 %collective-permute-start.63 = (bf16[384,1536]{1,0:T(8,128)(2,1)}, bf16[384,1536]{1,0:T(8,128)(2,1)}, u32[]{:S(2)}, u32[]{:S(2)}) collective-permute-start(bf16[384,1536]{1,0:T(8,128)(2,1)} %pad_maximum_fusion.6), channel_id=1, source_target_pairs={{0,16},{1,17},{8,24},{9,25},{16,0},{17,1},{24,8},{25,9},{2,18},{3,... | collective-permute-start | bytes 3538952 | tf_op jit(solution)/shard_map/ppermute | solution.py:28
  612.7 39.5 %collective-permute-start.69 = (bf16[48,1536]{1,0:T(8,128)(2,1)}, bf16[48,1536]{1,0:T(8,128)(2,1)}, u32[]{:S(2)}, u32[]{:S(2)}) collective-permute-start(bf16[48,1536]{1,0:T(8,128)(2,1)} %get-tuple-element.237), channel_id=1, source_target_pairs={{0,2},{2,6},{6,4},{4,0},{1,3},{3,7},{7,5},{5,1},{8,10},{10,14},{14... | collective-permute-start | bytes 442376 | tf_op jit(solution)/shard_map/ppermute | solution.py:154
  613.0 39.1 %collective-permute-start.68 = (bf16[48,1536]{1,0:T(8,128)(2,1)}, bf16[48,1536]{1,0:T(8,128)(2,1)}, u32[]{:S(2)}, u32[]{:S(2)}) collective-permute-start(bf16[48,1536]{1,0:T(8,128)(2,1)} %get-tuple-element.238), channel_id=1, source_target_pairs={{0,6},{2,4},{6,0},{4,2},{1,7},{3,5},{7,1},{5,3},{8,14},{10,12},{14... | collective-permute-start | bytes 442376 | tf_op jit(solution)/shard_map/ppermute | solution.py:154
  (100 other events, 1459.1 us)
Sparse Core Ops, SparseCore 0:
  124.1 57.0 all-gather.4
  182.8 101.1 all-gather.2
  373.9 96.3 reduce-scatter.2
  529.4 75.1 reduce-scatter.4

commit v3 on v2

--- a/solution.py
+++ b/solution.py
@@ -46,8 +46,8 @@
     return got
 
 
-def far_gather(got, sizes):
-    nx, nc, ny = sizes
+def diag_gather(got, sizes):
+    nx, _, ny = sizes
     half = got[0, 0].shape[0] // 2
     got = dict(got)
     for dx in range(1, nx):
@@ -55,12 +55,78 @@
             one = fetch(got[dx, 0][:half], (0, 0, dy), sizes)
             two = fetch(got[0, dy][half:], (dx, 0, 0), sizes)
             got[dx, dy] = jnp.concatenate([one, two], axis=0)
+    return got
+
+
+def cross_gather(got, sizes):
     full = {}
     for (dx, dy), value in got.items():
         full[dx, 0, dy] = value
-        for dc in range(1, nc):
+        for dc in range(1, sizes[1]):
             full[dx, dc, dy] = fetch(value, (0, dc, 0), sizes)
     return full
+
+
+def far_gather(got, sizes):
+    return cross_gather(diag_gather(got, sizes), sizes)
+
+
+def stack(blocks):
+    count = len(blocks)
+
+    def body(*refs):
+        parts, out, held, came, left = refs[:count], *refs[count:]
+        ins = [pltpu.make_async_copy(parts[i], held.at[i], came.at[i]) for i in range(count)]
+        outs = [pltpu.make_async_copy(held.at[i], out.at[i], left.at[i]) for i in range(count)]
+        for copy in ins:
+            copy.start()
+        for i in range(count):
+            ins[i].wait()
+            outs[i].start()
+        for copy in outs:
+            copy.wait()
+
+    return pl.pallas_call(
+        body,
+        in_specs=[pl.BlockSpec(memory_space=pl.ANY)] * count,
+        out_specs=pl.BlockSpec(memory_space=pl.ANY),
+        out_shape=jax.ShapeDtypeStruct((count, *blocks[0].shape), blocks[0].dtype),
+        scratch_shapes=[
+            pltpu.VMEM((count, *blocks[0].shape), blocks[0].dtype),
+            pltpu.SemaphoreType.DMA((count,)),
+            pltpu.SemaphoreType.DMA((count,)),
+        ],
+        compiler_params=pltpu.CompilerParams(vmem_limit_bytes=60 * 2**20),
+        cost_estimate=pl.CostEstimate(
+            flops=0, bytes_accessed=4 * count * blocks[0].size, transcendentals=0
+        ),
+        name="stack",
+    )(*blocks)
+
+
+def merge(near, cross, at, one=None, two=None):
+    _, rows, width = near.shape
+    half = rows // 2
+    extra = [] if one is None else [one, two]
+
+    def body(*refs):
+        total = refs[0][0].astype(F32) + refs[1][0].astype(F32)
+        if extra:
+            upper = pl.program_id(0) == 0
+            total = total + jnp.where(upper, refs[2][...], refs[3][...]).astype(F32)
+        refs[-1][...] = total.astype(BF)
+
+    block = pl.BlockSpec((1, half, width), lambda i: (at, i, 0))
+    return pl.pallas_call(
+        body,
+        grid=(2,),
+        in_specs=[block, block] + [pl.BlockSpec((half, width), lambda i: (0, 0))] * len(extra),
+        out_specs=pl.BlockSpec((half, width), lambda i: (i, 0)),
+        out_shape=jax.ShapeDtypeStruct((rows, width), BF),
+        compiler_params=pltpu.CompilerParams(vmem_limit_bytes=24 * 2**20),
+        cost_estimate=pl.CostEstimate(flops=3 * rows * width, bytes_accessed=10 * rows * width, transcendentals=0),
+        name="merge",
+    )(near, cross, *extra)
 
 
 class GroupSum:
@@ -68,42 +134,41 @@
         nx, _, ny = sizes
         self.sizes = sizes
         self.keys = [(dx, dy) for dx in range(nx) for dy in range(ny)]
-        self.here = {key: near[i] for i, key in enumerate(self.keys)}
+        self.near = near
         self.cross = send(far, (0, 1, 0), sizes)
-        self.half = near.shape[1] // 2
-
-    def pair(self, key):
-        return self.here[key].astype(F32) + self.cross[self.keys.index(key)].astype(F32)
-
-    def start_far(self):
-        half = self.half
-        self.more = {}
-        for dx, dy in self.keys:
-            if dx and dy:
-                total = self.pair((dx, dy)).astype(BF)
-                self.more[dx, dy] = (
-                    send(total[:half], (dx, 0, 0), self.sizes),
-                    send(total[half:], (0, 0, dy), self.sizes),
-                )
-
-    def start_near(self):
-        half = self.half
-        self.last = {}
-        for key in self.keys:
+        self.more, self.last = {}, {}
+
+    def sum_far(self):
+        self.total = {
+            key: merge(self.near, self.cross, i) for i, key in enumerate(self.keys) if key[0] and key[1]
+        }
+
+    def send_far(self):
+        for (dx, dy), total in self.total.items():
+            half = total.shape[0] // 2
+            self.more[dx, dy] = (
+                send(total[:half], (dx, 0, 0), self.sizes),
+                send(total[half:], (0, 0, dy), self.sizes),
+            )
+
+    def sum_near(self):
+        self.total = {}
+        for i, key in enumerate(self.keys):
             if (key[0] == 0) == (key[1] == 0):
                 continue
-            total = self.pair(key)
-            low, high = total[:half], total[half:]
-            for (dx, dy), (one, two) in self.more.items():
-                if key == (0, dy):
-                    low = low + one.astype(F32)
-                if key == (dx, 0):
-                    high = high + two.astype(F32)
-            total = jnp.concatenate([low, high], axis=0).astype(BF)
+            low = [one for (dx, dy), (one, _) in self.more.items() if key == (0, dy)]
+            high = [two for (dx, dy), (_, two) in self.more.items() if key == (dx, 0)]
+            none = jnp.zeros((self.near.shape[1] // 2, self.near.shape[2]), BF)
+            low = sum(v.astype(F32) for v in low[1:]) + low[0].astype(F32) if len(low) > 1 else (low + [none])[0]
+            high = sum(v.astype(F32) for v in high[1:]) + high[0].astype(F32) if len(high) > 1 else (high + [none])[0]
+            self.total[key] = merge(self.near, self.cross, i, low.astype(BF), high.astype(BF))
+
+    def send_near(self):
+        for key, total in self.total.items():
             self.last[key] = send(total, (key[0], 0, key[1]), self.sizes)
 
     def terms(self):
-        return [self.here[0, 0], self.cross[0]] + list(self.last.values())
+        return [self.near, self.cross] + [v[None] for v in self.last.values()]
 
 
 class Line:
@@ -146,9 +211,9 @@
             full = lax.dynamic_update_slice_in_dim(full, jnp.expand_dims(block, axis), self.source[s], axis)
         return full
 
-    def reduce_direct(self, parts, axis):
+    def reduce_direct(self, parts, axis, steps=None):
         terms = [lax.dynamic_index_in_dim(parts, self.source[0], axis, keepdims=False)]
-        for s in range(1, self.count):
+        for s in steps or range(1, self.count):
             part = lax.dynamic_index_in_dim(parts, self.source[s], axis, keepdims=False)
             route = [(self.ring[i], self.ring[(i - s) % self.count]) for i in range(self.count)]
             terms.append(lax.ppermute(part, "z", route))
@@ -331,7 +396,7 @@
         o_out[0, 1, slot * span : (slot + 1) * span] = o[span:]
 
 
-def mix_forward(x_all, x_past, x_next, w_in, gain, taps, place, sides, slots, span, edge):
+def mix_forward(x_all, w_in, gain, taps, place, sides, slots, span, edge):
     width = x_all.shape[2]
     cpad = w_in.shape[1] // 3
     rows = slots * span
@@ -340,7 +405,8 @@
     def main(y):
         return pl.BlockSpec((1, rows, width), lambda g, r: (r[2 * g + y], 0, 0))
 
-    rim = pl.BlockSpec((1, edge, width), lambda g, r: (r[2 * g] // 2, 0, 0))
+    def rim(y):
+        return pl.BlockSpec((1, edge, width), lambda g, r: (r[2 * g + y], rows // edge, 0))
 
     def fixed(shape):
         return pl.BlockSpec(shape, lambda g, r: (0,) * len(shape))
@@ -350,7 +416,7 @@
         grid_spec=pltpu.PrefetchScalarGridSpec(
             num_scalar_prefetch=1,
             grid=(sides,),
-            in_specs=[main(0), main(1), rim, rim, fixed(w_in.shape), fixed(gain.shape), fixed(taps.shape)],
+            in_specs=[main(0), main(1), rim(0), rim(1), fixed(w_in.shape), fixed(gain.shape), fixed(taps.shape)],
             out_specs=[
                 pl.BlockSpec((1, 2, rows, width), lambda g, r: (g, 0, 0, 0)),
                 pl.BlockSpec((1, total, 3 * cpad), lambda g, r: (g, 0, 0)),
@@ -367,7 +433,7 @@
             flops=sides * total * width * 6 * cpad, bytes_accessed=32 * 2**20, transcendentals=0
         ),
         name="mix_forward",
-    )(place, x_all, x_all, x_past, x_next, w_in, gain, taps)
+    )(place, x_all, x_all, x_all, x_all, w_in, gain, taps)
 
 
 def mix_backward_body(
@@ -540,9 +606,9 @@
 
 
 def turn_body(count, terms, *refs):
-    da2 = refs[0][...].astype(F32)
+    da2 = refs[0][0].astype(F32)
     for ref in refs[1:terms]:
-        da2 = da2 + ref[...].astype(F32)
+        da2 = da2 + ref[0].astype(F32)
     d_out, h1, gain, w, dh1, datt, d_o = refs[terms:]
     values = h1[...]
     grad = d_out[...].astype(F32) + norm_back(da2, values, rms_scale(values), gain[...])
@@ -567,7 +633,8 @@
     return pl.pallas_call(
         lambda *refs: turn_body(count, len(terms), *refs),
         grid=(rows // block,),
-        in_specs=[row(width)] * (len(terms) + 2) + [fixed(gain.shape), fixed(w_out.shape)],
+        in_specs=[pl.BlockSpec((1, block, width), lambda i: (0, i, 0))] * len(terms)
+        + [row(width), row(width), fixed(gain.shape), fixed(w_out.shape)],
         out_specs=[row(width), row(width), pl.BlockSpec((count, block, cpad), lambda i: (0, i, 0))],
         out_shape=[
             jax.ShapeDtypeStruct((rows, width), F32),
@@ -583,9 +650,9 @@
 
 
 def finish_body(terms, *refs):
-    da = refs[0][...].astype(F32)
+    da = refs[0][0].astype(F32)
     for ref in refs[1:terms]:
-        da = da + ref[...].astype(F32)
+        da = da + ref[0].astype(F32)
     x, dh1, gain, out = refs[terms:]
     values = x[...].astype(F32)
     out[...] = dh1[...] + norm_back(da, values, rms_scale(values), gain[...])
@@ -597,7 +664,9 @@
     return pl.pallas_call(
         lambda *refs: finish_body(len(terms), *refs),
         grid=(rows // block,),
-        in_specs=[spec] * (len(terms) + 2) + [pl.BlockSpec(gain.shape, lambda i: (0, 0))],
+        in_specs=[pl.BlockSpec((1, block, width), lambda i: (0, i, 0))] * len(terms)
+        + [spec] * 2
+        + [pl.BlockSpec(gain.shape, lambda i: (0, 0))],
         out_specs=spec,
         out_shape=jax.ShapeDtypeStruct((rows, width), F32),
         compiler_params=pltpu.CompilerParams(vmem_limit_bytes=40 * 2**20),
@@ -606,7 +675,8 @@
     )(*terms, x, dh1, gain)
 
 
-def feed_body(hid, hpad, split, a2, d_out, w_both, w_down, m, d_both, f_near, f_far, da_near, da_far):
+def feed_body(hid, hpad, a2, d_out, w_both, w_down, *refs):
+    m, d_both, f, da2 = refs[-4:]
     gu = dot(a2[0], w_both[...])
     gate, up = gu[:, :hid], gu[:, hpad : hpad + hid]
     dm = dot_nt(d_out[0], w_down[...])
@@ -620,54 +690,41 @@
         d_both[0, :, hpad + hid :] = none
     d_both[0, :, :hid] = (dm * up * (sigma * (1.0 + gate * (1.0 - sigma)))).astype(BF)
     d_both[0, :, hpad : hpad + hid] = (dm * active).astype(BF)
-    f = dot(inner, w_down[...]).astype(BF)
-    da2 = dot_nt(d_both[0], w_both[...]).astype(BF)
-
-    @pl.when(pl.program_id(0) >= split)
-    def _():
-        f_near[0] = f
-        da_near[0] = da2
-
-    @pl.when(pl.program_id(0) < split)
-    def _():
-        f_far[0] = f
-        da_far[0] = da2
-
-
-def feed(a2_all, d_all, w_both, w_down):
+    f[0] = dot(inner, w_down[...]).astype(BF)
+    da2[0] = dot_nt(d_both[0], w_both[...]).astype(BF)
+
+
+def feed(a2_all, d_all, w_both, w_down, first, kept=()):
     blocks, rows, width = a2_all.shape
+    half = blocks // 2
     hid, hpad = w_down.shape[0], w_both.shape[1] // 2
-    split = blocks // 2
 
     def part(last):
-        return pl.BlockSpec((1, rows, last), lambda i: ((i + split) % blocks, 0, 0))
-
-    near = pl.BlockSpec((1, rows, width), lambda i: (jnp.maximum(i - split, 0), 0, 0))
-    far = pl.BlockSpec((1, rows, width), lambda i: (jnp.minimum(i, split - 1), 0, 0))
-    half = jax.ShapeDtypeStruct((split, rows, width), BF)
+        return pl.BlockSpec((1, rows, last), lambda i: (i + first, 0, 0))
 
     def fixed(shape):
-        return pl.BlockSpec(shape, lambda i: (0,) * len(shape))
-
+        return pl.BlockSpec(shape, lambda i: (0,) * len(shape), pipeline_mode=pl.Buffered(1))
+
+    own = pl.BlockSpec((1, rows, width), lambda i: (i, 0, 0))
     return pl.pallas_call(
-        lambda *refs: feed_body(hid, hpad, split, *refs),
-        grid=(blocks,),
-        in_specs=[part(width), part(width), fixed(w_both.shape), fixed(w_down.shape)],
-        out_specs=[part(hid), part(2 * hpad), near, far, near, far],
+        lambda *refs: feed_body(hid, hpad, *refs),
+        grid=(half,),
+        in_specs=[part(width), part(width), fixed(w_both.shape), fixed(w_down.shape)]
+        + [pl.BlockSpec(memory_space=pl.ANY)] * len(kept),
+        out_specs=[part(hid), part(2 * hpad), own, own],
         out_shape=[
             jax.ShapeDtypeStruct((blocks, rows, hid), BF),
             jax.ShapeDtypeStruct((blocks, rows, 2 * hpad), BF),
-            half,
-            half,
-            half,
-            half,
+            jax.ShapeDtypeStruct((half, rows, width), BF),
+            jax.ShapeDtypeStruct((half, rows, width), BF),
         ],
+        input_output_aliases={4 + i: i for i in range(len(kept))},
         compiler_params=pltpu.CompilerParams(vmem_limit_bytes=60 * 2**20),
         cost_estimate=pl.CostEstimate(
-            flops=blocks * rows * width * hid * 12, bytes_accessed=64 * 2**20, transcendentals=blocks * rows * hid
+            flops=half * rows * width * hid * 12, bytes_accessed=40 * 2**20, transcendentals=half * rows * hid
         ),
         name="feed",
-    )(a2_all, d_all, w_both, w_down)
+    )(a2_all, d_all, w_both, w_down, *kept)
 
 
 def on_device(
@@ -714,7 +771,9 @@
     first = (lax.axis_index("z") * ny + row_y) * span
     positions = first + jnp.arange(span, dtype=jnp.int32)
     mask = (positions[None, :] < lengths[:, None]).astype(F32).reshape(rows, 1)
-    up_route = [(z, z + 1) for z in range(nz - 1)]
+    rim_route = []
+    for z in range(nz - 1):
+        rim_route += [(z * ny + 1, (z + 1) * ny), ((z + 1) * ny, z * ny + 1)]
     down_route = [(z + 1, z) for z in range(nz - 1)]
 
     def rim(values, start):
@@ -726,125 +785,150 @@
     x = x_bf.astype(F32)
     d_out_bf = (mask * cotangent.reshape(rows, width).astype(F32)).astype(BF)
 
+    hold = lax.optimization_barrier
     plan = shuffle_plan(ndp, nz, ny)
+
     gains = jnp.stack([gain_one, gain_two], axis=1)
     cut = cut_columns([in_weight], own_in, cpad, plan, gains)
     cut = lax.all_to_all(cut, GROUP, 0, 0, tiled=True).reshape(ndp, ny, own_in, 3 * cpad)
-    x_all = near_gather(x_bf, sizes)
     taps_here = jnp.pad(conv_weight.T, ((0, 0), (0, 128 - conv_weight.shape[0])))
-    out_here = jnp.concatenate([out_weight, taps_here], axis=1)
-    cut = line.fetch_all(cut)
-
-    both = cut_columns([gate_weight, up_weight], own_hid, hpad, plan)
-    both = lax.all_to_all(both, GROUP, 0, 0, tiled=True).reshape(ndp, ny * own_in, 2 * hpad)
-    x_all, both, out_here = lax.optimization_barrier((x_all, both, out_here))
-    w_out = line.fetch_all(out_here)
-    w_both = lax.all_gather(both, "z", axis=1, tiled=True).reshape(width, 2 * hpad)
-
-    x_all = far_gather(x_all, sizes)
-    x_all = jnp.stack([x_all[h] for h in hops], axis=0)
-    pair = x_all.reshape(sides, ny, rows, width)
-    even = row_y == 0
-    x_past = lax.ppermute(rim(jnp.where(even, pair[:, 1], pair[:, 0]), span - 2), "z", up_route)
-    x_next = lax.ppermute(rim(jnp.where(even, pair[:, 0], pair[:, 1]), 0), "z", down_route)
-    (x_all, x_past, x_next, w_out), (d_out_bf, down_weight, cut) = after(
-        (x_all, x_past, x_next, w_out), (d_out_bf, down_weight, cut)
-    )
-    w_down = lax.all_gather(down_weight, "z", axis=0, tiled=True)
-    w_in = line.place(cut, 1).reshape(width, 3 * cpad)
-    gain_a = w_in[:, chan].astype(F32).reshape(1, width)
-    gain_b = w_in[:, chan + 1].astype(F32).reshape(1, width)
-
+    w_out = line.fetch_all(jnp.concatenate([out_weight, taps_here], axis=1))
+    pairs = tokens.reshape(slots, span, width)
+    pairs = jnp.where(row_y == 0, pairs[:, :2], pairs[:, -2:]).reshape(2 * slots, width)
+    x_rim = lax.ppermute(jnp.pad(pairs, ((0, edge - 2 * slots), (0, 0))), ("z", "y"), rim_route)
+    (cut, w_out, x_rim), (x_late, gate_late) = after((cut, w_out, x_rim), (x_bf, gate_weight))
+    x_late = jnp.concatenate([x_late, x_rim], axis=0)
+
+    w_in = lax.all_gather(cut.reshape(ndp, ny * own_in, 3 * cpad), "z", axis=1, tiled=True).reshape(width, 3 * cpad)
     w_out = line.place(w_out, 0).reshape(chan, width + 128)
     taps = w_out[:, width : width + 8].astype(F32).T
     taps = jnp.pad(taps, ((0, 0), (0, cpad - chan)))
-    w_out = w_out[:, :width]
-    w_out = near_gather(w_out, sizes)
-    d_all = near_gather(d_out_bf, sizes)
-
-    a_all, bcx, o_all = mix_forward(x_all, x_past, x_next, w_in, gain_a, taps, place, sides, slots, span, edge)
-    o_all, w_out = lax.optimization_barrier((o_all, w_out))
+    w_out = near_gather(w_out[:, :width], sizes)
+    x_all = near_gather(x_late, sizes)
+    both = cut_columns([gate_late, up_weight], own_hid, hpad, plan)
+    both = lax.all_to_all(both, GROUP, 0, 0, tiled=True).reshape(ndp, ny * own_in, 2 * hpad)
+    x_all, both, w_in, w_out = hold((x_all, both, w_in, w_out))
+
+    w_both = lax.all_gather(both, "z", axis=1, tiled=True).reshape(width, 2 * hpad)
+    x_all = far_gather(x_all, sizes)
+    gain_a = w_in[:, chan].astype(F32).reshape(1, width)
+    gain_b = w_in[:, chan + 1].astype(F32).reshape(1, width)
+    x_all, (w_out, d_late) = after(x_all, (w_out, d_out_bf))
+
+    w_out = diag_gather(w_out, sizes)
+    x_all = stack([x_all[h] for h in hops])
+    d_all = near_gather(d_late, sizes)
+    a_all, bcx, o_all = mix_forward(x_all, w_in, gain_a, taps, place, sides, slots, span, edge)
+    o_all, w_out, d_all = hold((o_all, w_out, d_all))
+
     o_own = lax.all_to_all(o_all.reshape(len(hops), rows, cpad), GROUP, 0, 0, tiled=True)
-    o_own, d_all = lax.optimization_barrier((o_own, d_all))
-    w_some = far_gather(w_out, sizes)
-    d_all = far_gather(d_all, sizes)
+    w_some = cross_gather(w_out, sizes)
+    d_all = diag_gather(d_all, sizes)
     w_out = jnp.zeros((len(hops), cpad, width), BF)
     for i, h in enumerate(hops):
         w_out = lax.dynamic_update_slice(w_out, w_some[h][None], (turn_at[i], 0, 0))
     w_out = w_out.reshape(len(hops) * cpad, width)
+    o_own, w_out = hold((o_own, w_out))
+
     block = rows // 2
     o_cat, h1, a2 = attend(o_own, w_out, x_bf, gain_b, block)
-    a2, d_all = lax.optimization_barrier((a2, d_all))
-    d_all = jnp.stack([d_all[h] for h in hops], axis=0)
-    a2_all = far_gather(near_gather(a2, sizes), sizes)
-    a2_all = jnp.stack([a2_all[h] for h in hops], axis=0)
-
-    m, d_both, f_near, f_far, da_near, da_far = feed(a2_all, d_all, w_both, w_down)
-    hold = lax.optimization_barrier
+    (a2, d_all, w_both), down_weight = after((a2, d_all, w_both), down_weight)
+
+    w_down = lax.all_gather(down_weight, "z", axis=0, tiled=True)
+    d_all = cross_gather(d_all, sizes)
+    a2_all = near_gather(a2, sizes)
+    a2_all, d_all = hold((a2_all, d_all))
+    d_all = stack([d_all[h] for h in hops])
+    a2_all, d_all = hold((diag_gather(a2_all, sizes), d_all))
+    a2_all = cross_gather(a2_all, sizes)
+    a2_all = stack([a2_all[h] for h in hops])
+
+    m, d_both, f_far, da_far = feed(a2_all, d_all, w_both, w_down, len(hops) // 2)
+    m, d_both, f_near, da_near = feed(a2_all, d_all, w_both, w_down, 0, (m, d_both))
     da2 = GroupSum(da_near, da_far, sizes)
+    f = GroupSum(f_near, f_far, sizes)
     d_flat = d_all.reshape(-1, width)
+    da2.sum_far()
+    da2.total, m = after(da2.total, m)
+    da2.send_far()
+    down_part = dot_tn(m.reshape(-1, hid), d_flat).astype(BF)
+    da2.more, f.cross, down_part = hold((da2.more, f.cross, down_part))
+
+    da2.sum_near()
+    da2.total, d_both = after(da2.total, d_both)
+    da2.send_near()
     both_part = dot_tn(a2_all.reshape(-1, width), d_both.reshape(-1, 2 * hpad)).astype(BF)
+    da2.last, both_part, f.cross = hold((da2.last, both_part, f.cross))
     both_sum = lax.psum_scatter(
         both_part.reshape(ndp, nz * ny * own_in, 2 * hpad), "z", scatter_dimension=1, tiled=True
     )
-    da2.cross, both_part = hold((da2.cross, both_part))
-    da2.start_far()
-    f = GroupSum(f_near, f_far, sizes)
-    down_part = dot_tn(m.reshape(-1, hid), d_flat).astype(BF)
-    da2.more, f.cross = hold((da2.more, f.cross))
-    da2.start_near()
-    da2.last, f.cross, down_part = hold((da2.last, f.cross, down_part))
-    down_grad = lax.psum_scatter(down_part, "z", scatter_dimension=0, tiled=True).astype(F32)
-
-    f.start_far()
+
+    f.sum_far()
+    da2.last, f.total = hold((da2.last, f.total))
+    f.send_far()
     dh1, datt, do_own = turn(da2.terms(), d_out_bf, h1, gain_b, w_out, len(hops), block)
+    do_own, datt, f.more = hold((do_own, datt, f.more))
+
     do_all = lax.all_to_all(do_own, GROUP, 0, 0, tiled=True)
     out_part = dot_tn(o_cat, datt).astype(BF).reshape(len(hops), cpad, width)[:, :chan]
-    out_near = jnp.stack(
-        [lax.dynamic_index_in_dim(out_part, turn_at[i], 0, keepdims=False) for i in range(ndp)], axis=0
-    )
-    out_far = jnp.stack(
-        [lax.dynamic_index_in_dim(out_part, turn_at[i], 0, keepdims=False) for i in range(ndp, 2 * ndp)], axis=0
-    )
+    out_near = jnp.stack([lax.dynamic_index_in_dim(out_part, t, 0, keepdims=False) for t in turn_at[:ndp]], axis=0)
+    out_far = jnp.stack([lax.dynamic_index_in_dim(out_part, t, 0, keepdims=False) for t in turn_at[ndp:]], axis=0)
     out = GroupSum(out_near, out_far, sizes)
-    do_all, f.more, out.cross = hold((do_all, f.more, out.cross))
+    f.sum_near()
+    do_all, out.cross, f.total = hold((do_all, out.cross, f.total))
+
     do_rim = lax.ppermute(rim(do_all.reshape(sides, ny, rows, cpad)[:, 0], 0), "z", down_route)
-    do_rim, f.more, out.cross = hold((do_rim, f.more, out.cross))
-    f.start_near()
-    out.start_far()
-
+    out.sum_far()
+    do_rim, f.total, out.total = hold((do_rim, f.total, out.total))
+
+    f.send_near()
+    out.send_far()
     in_part, da_near, da_far, conv_part = mix_backward(
         do_all, do_rim, a_all, bcx, w_in, taps, nat, sides, slots, span, edge
     )
     (in_part, da_near, da_far, conv_part), f.last, out.more = hold(
         ((in_part, da_near, da_far, conv_part), f.last, out.more)
     )
+
     flat = (ndp, rows, width)
     da = GroupSum(da_near.reshape(flat), da_far.reshape(flat), sizes)
-    in_sum = line.reduce_direct(in_part.reshape(ndp, nz, ny, own_in, 3 * cpad), 1)
+    in_part, both_sum = hold((in_part, both_sum))
+    in_sum = lax.psum_scatter(
+        in_part.reshape(ndp, nz * ny * own_in, 3 * cpad), "z", scatter_dimension=1, tiled=True
+    )
     both_sum = lax.all_to_all(both_sum.reshape(ndp * ny, own_in, 2 * hpad), GROUP, 0, 0, tiled=True)
-    da.cross, both_sum = hold((da.cross, both_sum))
-    da.start_far()
-    out.start_near()
-    da.more, out.last, in_sum[1], in_sum[-1] = hold((da.more, out.last, in_sum[1], in_sum[-1]))
-    da.start_near()
-    out_sum = sum(term.astype(F32) for term in out.terms()).astype(BF)
+    da.cross = hold(da.cross)
+
+    da.sum_far()
+    da.send_far()
+    out.sum_near()
+    out.send_near()
+    da.more, both_sum, out.last = hold((da.more, both_sum, out.last))
+    da.sum_near()
+    da.total, in_sum = after(da.total, in_sum)
+    in_sum, down_part = after(in_sum, down_part)
+    down_grad = lax.psum_scatter(down_part, "z", scatter_dimension=0, tiled=True)
+    da.send_near()
+    in_sum = lax.all_to_all(in_sum.reshape(ndp * ny, own_in, 3 * cpad), GROUP, 0, 0, tiled=True)
+    out_sum = sum(term[0].astype(F32) for term in out.terms()).astype(BF)
     out_grad = line.reduce_direct(out_sum.reshape(nz, own_in, width), 0)
     conv_grad = line.reduce_direct(conv_part[:3, :chan].reshape(3, nz, own_in), 1)
+    total = h1
+    for term in f.terms():
+        total = total + term[0].astype(F32)
+    mixed = (mask * total).astype(BF)
     (gate_grad, up_grad), gain_two_grad = join_columns(
         both_sum, [gate_weight, up_weight], gain_two, own_hid, hpad, plan
     )
-    total = h1
-    for term in f.terms():
-        total = total + term.astype(F32)
-    mixed = (mask * total).astype(BF)
-    in_sum, da.last, mixed = hold((in_sum, da.last, mixed))
-    in_sum = sum(term.astype(F32) for term in in_sum).astype(BF)
-    in_sum = lax.all_to_all(in_sum.reshape(ndp * ny, own_in, 3 * cpad), GROUP, 0, 0, tiled=True)
+    in_sum, da.last, out_grad, conv_grad, mixed, gate_grad, up_grad = hold(
+        (in_sum, da.last, out_grad, conv_grad, mixed, gate_grad, up_grad)
+    )
+
     input_grad = finish(da.terms(), x_bf, dh1, gain_a, block)
     out_grad = sum(term.astype(F32) for term in out_grad)
     conv_grad = sum(conv_grad)
     (in_grad,), gain_one_grad = join_columns(in_sum, [in_weight], gain_one, own_in, cpad, plan)
+    down_grad = down_grad.astype(F32)
     return (
         mixed.reshape(slots, span, width),
         input_grad.reshape(slots, span, width),

time: 684 us -> 633 us (0.925)
  Pallas kernels: 137 us -> 181 us
  waiting for transfers between devices: 236 us -> 211 us
  other arithmetic: 50.8 us -> 25.9 us
  local copies, waits for them, and re-layouts: 86.4 us -> 62.8 us
  starting transfers between devices: 109 us -> 87.1 us
    pallas_call x1 -> x17, Pallas kernels: 65.1 us -> 108 us  [the longest x2 66.3 us: feed(): pl.pallas_call(lambda *refs: feed_body(hid, hpad, *refs), grid=(half,), i...]
    ppermute x9 -> x6, waiting for transfers between devices: 37.2 us -> 18.3 us  [reduce_direct(): terms.append(lax.ppermute(part, 'z', route))]
    add x4 -> x0, other arithmetic: 17 us -> none  [pair(): self.here[key].astype(F32) + self.cross[self.keys.index(key)].astype(F32)]
    dynamic_update_slice x8, local copies, waits for them, and re-layouts: 15.5 us -> 1.47 us  [on_device(): w_out = lax.dynamic_update_slice(w_out, w_some[h][None], (turn_at[i], 0, 0))]
    unnamed x133 -> x170, local copies, waits for them, and re-layouts: 27.6 us -> 41.3 us
    all_to_all x1, waiting for transfers between devices: 0.01 us -> 12.4 us  [on_device(): do_all = lax.all_to_all(do_own, GROUP, 0, 0, tiled=True)]
    ppermute x9 -> x6, starting transfers between devices: 21.7 us -> 10.1 us  [reduce_direct(): terms.append(lax.ppermute(part, 'z', route))]
    all_to_all x1, waiting for transfers between devices: 11.3 us -> 0.01 us  [on_device(): lax.all_to_all(both_sum.reshape(ndp * ny, own_in, 2 * hpad), GROUP, 0, 0,...]
  transfers between devices with their start and end apart: 80 -> 75, of which waited for: 29 -> 32; matrix products, arithmetic and copies ran while one was open for 23% -> 14% of each run, Pallas kernels for 10% -> 23%
where the time goes in v3:
time: 633 us; the launch traced here: 623 us
  waiting for transfers between devices  211 us (33%)
  Pallas kernels  181 us (29%)
  starting transfers between devices  87.1 us (14%)
  local copies, waits for them, and re-layouts  62.8 us (10%)
  matrix products  39.4 us (6%)
  other arithmetic  25.9 us (4%)
  between operations  15.7 us (2%)
    ppermute x52, waiting for transfers between devices, send(): return lax.ppermute(block, GROUP, route)  163 us
    pallas_call x2, Pallas kernels, feed(): pl.pallas_call(lambda *refs: feed_body(hid, hpad, *refs), grid=(half,), i...  66.3 us
    ppermute x52, starting transfers between devices, send(): return lax.ppermute(block, GROUP, route)  42.6 us
    unnamed x170, local copies, waits for them, and re-layouts  41.3 us
    dot_general x3, matrix products, dot_tn(): lax.dot_general(left, right, (((0,), (0,)), ((), ())), preferred_element_...  39.4 us
    pallas_call x1, Pallas kernels, mix_backward(): pl.pallas_call(lambda *refs: mix_backward_body(cpad, slots, span, edge, *...  28.7 us
    pallas_call x3, Pallas kernels, stack(): pl.pallas_call(body, in_specs=[pl.BlockSpec(memory_space=pl.ANY)] * count...  22.6 us
    pallas_call x12, Pallas kernels, merge(): pl.pallas_call(body, grid=(2,), in_specs=[block, block] + [pl.BlockSpec((...  19 us
  transfers between devices with their start and end apart: 75, of which 32 were waited for; matrix products, arithmetic and copies ran while one was open for 14% of the time, Pallas kernels for 23%

profile of v3, /device:TPU:0, one launch (start us, length us, event | category | flops | bytes accessed | tf_op | source)
XLA Modules:
  0.0 623.3 jit_solution(8818981967600421383)
XLA Ops:
  10.3 5.3 all-to-all-start
  25.3 4.8 collective-permute-done.1
  49.3 42.1 %collective-permute-done.6 = bf16[192,1536]{1,0:T(8,128)(2,1)S(1)} collective-permute-done((bf16[192,1536]{1,0:T(8,128)(2,1)S(1)}, bf16[192,1536]{1,0:T(8,128)(2,1)S(1)}, u32[]{:S(2)}, u32[]{:S(2)}) %collective-permute-start.6) | collective-permute-done | bytes 589856 | tf_op jit(solution)/shard_map/ppermute | solution.py:28
  99.0 10.6 %collective-permute-done.10 = bf16[200,1536]{1,0:T(8,128)(2,1)S(1)} collective-permute-done((bf16[200,1536]{1,0:T(8,128)(2,1)S(1)}, bf16[200,1536]{1,0:T(8,128)(2,1)S(1)}, u32[]{:S(2)}, u32[]{:S(2)}) %collective-permute-start.10) | collective-permute-done | bytes 614432 | tf_op jit(solution)/shard_map/ppermute | solution.py:28
  125.7 7.7 %stack.103.refs_1_.refs_2_.refs_3_.refs_4_ = bf16[8,400,1536]{2,1,0:T(8,128)(2,1)} custom-call(bf16[400,1536]{1,0:T(8,128)(2,1)} %constant_dynamic-update-slice_fusion.refs_0_, bf16[400,1536]{1,0:T(8,128)(2,1)} %collective-permute-done.4.refs_1_, bf16[400,1536]{1,0:T(8,128)(2,1)} %collective-permute-done.5.refs_2_, ...), custom_call_target="tpu_custom_call" | custom-call | bytes 19660800 | tf_op jit(solution)/shard_map/stack/pallas_call | solution.py:89
  133.5 16.0 %mix_forward.1 = (bf16[4,2,384,1536]{3,2,1,0:T(8,128)(2,1)}, f32[4,800,768]{2,1,0:T(8,128)}, bf16[4,2,384,256]{3,2,1,0:T(8,128)(2,1)}) custom-call(s32[8]{0:T(128)} %stack.97.refs_0_, bf16[8,400,1536]{2,1,0:T(8,128)(2,1)} %stack.103.refs_1_.refs_2_.refs_3_.refs_4_, bf16[8,400,1536]{2,1,0:T(8,128)(2,1)} %stack.103.refs_1_.refs_2_.refs_3_.refs_4_, ...), custom_call_target="tpu_custom_call" | custom-call | flops 7549747200 | bytes 33554432 | tf_op jit(solution)/shard_map/mix_forward/pallas_call | solution.py:414
  152.7 4.3 all-to-all-start.2
  164.8 25.0 %collective-permute-done.23 = bf16[192,1536]{1,0:T(8,128)(2,1)S(1)} collective-permute-done((bf16[192,1536]{1,0:T(8,128)(2,1)S(1)}, bf16[192,1536]{1,0:T(8,128)(2,1)S(1)}, u32[]{:S(2)}, u32[]{:S(2)}) %collective-permute-start.23) | collective-permute-done | bytes 589856 | tf_op jit(solution)/shard_map/ppermute | solution.py:28
  196.3 4.3 attend.1
  206.3 24.4 %collective-permute-done.24.refs_1_ = bf16[384,1536]{1,0:T(8,128)(2,1)S(1)} collective-permute-done((bf16[384,1536]{1,0:T(8,128)(2,1)S(1)}, bf16[384,1536]{1,0:T(8,128)(2,1)S(1)}, u32[]{:S(2)}, u32[]{:S(2)}) %collective-permute-start.24) | collective-permute-done | bytes 1179680 | tf_op jit(solution)/shard_map/ppermute | solution.py:28
  238.3 7.5 %stack.104.refs_1_ = bf16[8,384,1536]{2,1,0:T(8,128)(2,1)} custom-call(bf16[384,1536]{1,0:T(8,128)(2,1)} %copy-done.13, bf16[384,1536]{1,0:T(8,128)(2,1)} %copy-done.41, bf16[384,1536]{1,0:T(8,128)(2,1)} %collective-permute-done.17.refs_2_, bf16[384,1536]{1,0:T(8,128)(2,1)} %pad_maximum_fusion.2.refs_3_, bf16[384,1536]{1,0:T(8,128)(2,1)} %copy-done.54, ...), custom_call_target="tpu_custom_call" | custom-call | bytes 18874368 | tf_op jit(solution)/shard_map/stack/pallas_call | solution.py:89
  245.8 4.1 collective-permute-done.31
  261.8 7.4 %stack.105.refs_0_ = bf16[8,384,1536]{2,1,0:T(8,128)(2,1)} custom-call(bf16[384,1536]{1,0:T(8,128)(2,1)} %copy-done.27, bf16[384,1536]{1,0:T(8,128)(2,1)} %copy-done.42, bf16[384,1536]{1,0:T(8,128)(2,1)} %copy-done.43, bf16[384,1536]{1,0:T(8,128)(2,1)} %copy-done.40, bf16[384,1536]{1,0:T(8,128)(2,1)} %copy-done.57, bf16[384,1536]{1,0:T(8,128)(2,1)} %copy-done.58, ...), custom_call_target="tpu_custom_call" | custom-call | bytes 18874368 | tf_op jit(solution)/shard_map/stack/pallas_call | solution.py:89
  269.2 33.2 %feed.2 = (bf16[8,384,864]{2,1,0:T(8,128)(2,1)}, bf16[8,384,1792]{2,1,0:T(8,128)(2,1)}, bf16[4,384,1536]{2,1,0:T(8,128)(2,1)}, bf16[4,384,1536]{2,1,0:T(8,128)(2,1)}) custom-call(bf16[8,384,1536]{2,1,0:T(8,128)(2,1)} %stack.105.refs_0_, bf16[8,384,1536]{2,1,0:T(8,128)(2,1)} %stack.104.refs_1_, bf16[1536,1792]{1,0:T(8,128)(2,1)} %bitcast.154, ...), custom_call_target="tpu_custom_call" | custom-call | flops 24461180928 | bytes 41943040 | tf_op jit(solution)/shard_map/feed/pallas_call | solution.py:709
  303.0 33.0 %feed.3 = (bf16[8,384,864]{2,1,0:T(8,128)(2,1)}, bf16[8,384,1792]{2,1,0:T(8,128)(2,1)}, bf16[4,384,1536]{2,1,0:T(8,128)(2,1)}, bf16[4,384,1536]{2,1,0:T(8,128)(2,1)}) custom-call(bf16[8,384,1536]{2,1,0:T(8,128)(2,1)} %stack.105.refs_0_, bf16[8,384,1536]{2,1,0:T(8,128)(2,1)} %stack.104.refs_1_, ...), custom_call_target="tpu_custom_call", output_to_operand_aliasing={{0}: (4, {}), {1}: (5, {})} | custom-call | flops 24461180928 | bytes 41943040 | tf_op jit(solution)/shard_map/feed/pallas_call | solution.py:709
  341.8 12.4 %bitcast_convert_fusion.1 = bf16[864,1536]{1,0:T(8,128)(2,1)} fusion(bf16[8,384,864]{2,1,0:T(8,128)(2,1)S(1)} %copy-done.75, bf16[8,384,1536]{2,1,0:T(8,128)(2,1)} %stack.104.refs_1_), kind=kOutput, calls=%fused_computation.2 | convolution fusion | flops 8155054080 | bytes 17399808 | tf_op jit(solution)/shard_map/dot_general | solution.py:232
  364.7 23.3 %bitcast_convert_fusion = bf16[1536,1792]{1,0:T(8,128)(2,1)} fusion(bf16[8,384,1536]{2,1,0:T(8,128)(2,1)S(1)} %bitcast.133, bf16[8,384,1792]{2,1,0:T(8,128)(2,1)} %get-tuple-element.235), kind=kOutput, calls=%fused_computation | convolution fusion | flops 16914186240 | bytes 25952256 | tf_op jit(solution)/shard_map/dot_general | solution.py:232
  396.4 10.1 %turn.1 = (f32[384,1536]{1,0:T(8,128)S(1)}, bf16[384,1536]{1,0:T(8,128)(2,1)S(1)}, bf16[8,384,256]{2,1,0:T(8,128)(2,1)S(1)}) custom-call(bf16[4,384,1536]{2,1,0:T(8,128)(2,1)} %get-tuple-element.224.refs_0_, bf16[4,384,1536]{2,1,0:T(8,128)(2,1)} %collective-permute-done.36.refs_1_, bf16[1,384,1536]{2,1,0:T(8,128)(2,1)S(1)} %bitcast.130, ...), custom_call_target="tpu_custom_call" | custom-call | flops 2415919104 | bytes 20971520 | tf_op jit(solution)/shard_map/turn/pallas_call | solution.py:633
  408.1 3.7 convolution_convert_fusion
  415.5 4.3 all-to-all-start.3
  427.5 12.4 %all-to-all-done.3.refs_1_.refs_2_ = bf16[8,384,256]{2,1,0:T(8,128)(2,1)} async-done(((bf16[8,384,256]{2,1,0:T(8,128)(2,1)}), bf16[8,384,256]{2,1,0:T(8,128)(2,1)}, u32[]{:S(2)}, u32[]{:S(2)}) %all-to-all-start.3) | async-done | bytes 1572896 | tf_op jit(solution)/shard_map/all_to_all | solution.py:872
  446.0 6.5 %collective-permute-done.45.refs_3_ = bf16[4,16,256]{2,1,0:T(8,128)(2,1)S(1)} collective-permute-done((bf16[4,16,256]{2,1,0:T(8,128)(2,1)S(1)}, bf16[4,16,256]{2,1,0:T(8,128)(2,1)S(1)}, u32[]{:S(2)}, u32[]{:S(2)}) %collective-permute-start.45) | collective-permute-done | bytes 32800 | tf_op jit(solution)/shard_map/ppermute | solution.py:880
  457.3 28.7 %mix_backward.1 = (bf16[1536,768]{1,0:T(8,128)(2,1)}, bf16[2,2,384,1536]{3,2,1,0:T(8,128)(2,1)}, bf16[2,2,384,1536]{3,2,1,0:T(8,128)(2,1)}, f32[8,256]{1,0:T(8,128)}) custom-call(s32[8]{0:T(128)} %stack.88.refs_0_, bf16[8,384,256]{2,1,0:T(8,128)(2,1)} %all-to-all-done.3.refs_1_.refs_2_, bf16[8,384,256]{2,1,0:T(8,128)(2,1)} %all-to-all-done.3.refs_1_.refs_2_, ...), custom_call_target="tpu_custom_call" | custom-call | flops 14495514624 | bytes 41943040 | tf_op jit(solution)/shard_map/mix_backward/pallas_call | solution.py:533
  491.5 4.3 all-to-all-start.4
  504.2 22.5 %collective-permute-done.53 = bf16[192,1536]{1,0:T(8,128)(2,1)S(1)} collective-permute-done((bf16[192,1536]{1,0:T(8,128)(2,1)S(1)}, bf16[192,1536]{1,0:T(8,128)(2,1)S(1)}, u32[]{:S(2)}, u32[]{:S(2)}) %collective-permute-start.53) | collective-permute-done | bytes 589856 | tf_op jit(solution)/shard_map/ppermute | solution.py:28
  526.9 12.2 %collective-permute-done.51.refs_2_ = bf16[192,1536]{1,0:T(8,128)(2,1)S(1)} collective-permute-done((bf16[192,1536]{1,0:T(8,128)(2,1)S(1)}, bf16[192,1536]{1,0:T(8,128)(2,1)S(1)}, u32[]{:S(2)}, u32[]{:S(2)}) %collective-permute-start.51) | collective-permute-done | bytes 589856 | tf_op jit(solution)/shard_map/ppermute | solution.py:28
  558.3 4.2 all-to-all-start.5
  568.9 4.2 fusion.3
  573.2 3.7 join_columns.2
  578.8 4.1 collective-permute-done.58
  582.9 14.2 %collective-permute-done.59 = bf16[48,1536]{1,0:T(8,128)(2,1)} collective-permute-done((bf16[48,1536]{1,0:T(8,128)(2,1)}, bf16[48,1536]{1,0:T(8,128)(2,1)}, u32[]{:S(2)}, u32[]{:S(2)}) %collective-permute-start.59) | collective-permute-done | bytes 147488 | tf_op jit(solution)/shard_map/ppermute | solution.py:219
  605.8 4.7 finish.1
  (399 shorter events, 202.2 us)
Async XLA Ops:
  15.6 77.3 %all-gather.4.cloned.1.call-start = ((), (), s32[]{:S(2)}) async-start(), calls=%async_computation.9 | async-start | bytes 2949120 | tf_op jit(solution)/shard_map/all_gather | solution.py:802
  34.7 58.2 %collective-permute-start.4 = (bf16[400,1536]{1,0:T(8,128)(2,1)}, bf16[400,1536]{1,0:T(8,128)(2,1)}, u32[]{:S(2)}, u32[]{:S(2)}) collective-permute-start(bf16[400,1536]{1,0:T(8,128)(2,1)} %constant_dynamic-update-slice_fusion.refs_0_), channel_id=1, source_target_pairs={{0,1},{1,0},{8,9},{9,8},{16,17},{17,16},{24,25},{25,24},{2,3},{3,2... | collective-permute-start | bytes 3686408 | tf_op jit(solution)/shard_map/ppermute | solution.py:28
  36.8 56.1 %collective-permute-start.5 = (bf16[400,1536]{1,0:T(8,128)(2,1)}, bf16[400,1536]{1,0:T(8,128)(2,1)}, u32[]{:S(2)}, u32[]{:S(2)}) collective-permute-start(bf16[400,1536]{1,0:T(8,128)(2,1)} %constant_dynamic-update-slice_fusion.refs_0_), channel_id=1, source_target_pairs={{0,16},{1,17},{8,24},{9,25},{16,0},{17,1},{24,8},{25,9},{2,18},{3,... | collective-permute-start | bytes 3686408 | tf_op jit(solution)/shard_map/ppermute | solution.py:28
  40.1 52.8 %all-to-all-start.1 = ((bf16[8,48,1792]{2,1,0:T(8,128)(2,1)}), bf16[8,48,1792]{2,1,0:T(8,128)(2,1)S(1)}, u32[]{:S(2)}, u32[]{:S(2)}) async-start(bf16[8,48,1792]{2,1,0:T(8,128)(2,1)} %cut_columns.3), calls=%async_computation.1 | async-start | bytes 2752512 | tf_op jit(solution)/shard_map/all_to_all | solution.py:809
  43.7 159.5 %all-gather.6.cloned.1.call-start = ((), (), s32[]{:S(2)}) async-start(), calls=%async_computation.10 | async-start | bytes 6881280 | tf_op jit(solution)/shard_map/all_gather | solution.py:812
  45.8 45.5 %collective-permute-start.6 = (bf16[192,1536]{1,0:T(8,128)(2,1)S(1)}, bf16[192,1536]{1,0:T(8,128)(2,1)S(1)}, u32[]{:S(2)}, u32[]{:S(2)}) collective-permute-start(bf16[192,1536]{1,0:T(8,128)(2,1)S(1)} %slice.116), channel_id=1, source_target_pairs={{0,1},{1,0},{8,9},{9,8},{16,17},{17,16},{24,25},{25,24},{2,3},{3,2... | collective-permute-start | bytes 1769480 | tf_op jit(solution)/shard_map/ppermute | solution.py:28
  47.8 45.1 %collective-permute-start.7 = (bf16[192,1536]{1,0:T(8,128)(2,1)S(1)}, bf16[192,1536]{1,0:T(8,128)(2,1)}, u32[]{:S(2)}, u32[]{:S(2)}) collective-permute-start(bf16[192,1536]{1,0:T(8,128)(2,1)S(1)} %slice.116), channel_id=1, source_target_pairs={{0,16},{1,17},{8,24},{9,25},{16,0},{17,1},{24,8},{25,9},{2,18},{3,... | collective-permute-start | bytes 1769480 | tf_op jit(solution)/shard_map/ppermute | solution.py:28
  116.0 36.7 %collective-permute-start.16 = (bf16[384,1536]{1,0:T(8,128)(2,1)S(1)}, bf16[384,1536]{1,0:T(8,128)(2,1)S(1)}, u32[]{:S(2)}, u32[]{:S(2)}) collective-permute-start(bf16[384,1536]{1,0:T(8,128)(2,1)S(1)} %fusion.4.refs_0_.refs_4_), channel_id=1, source_target_pairs={{0,1},{1,0},{8,9},{9,8},{16,17},{17,16},{24,25},{25,24},{2,3},{3,2... | collective-permute-start | bytes 3538952 | tf_op jit(solution)/shard_map/ppermute | solution.py:28
  116.6 36.1 %collective-permute-start.17 = (bf16[384,1536]{1,0:T(8,128)(2,1)S(1)}, bf16[384,1536]{1,0:T(8,128)(2,1)}, u32[]{:S(2)}, u32[]{:S(2)}) collective-permute-start(bf16[384,1536]{1,0:T(8,128)(2,1)S(1)} %fusion.4.refs_0_.refs_4_), channel_id=1, source_target_pairs={{0,16},{1,17},{8,24},{9,25},{16,0},{17,1},{24,8},{25,9},{2,18},{3,... | collective-permute-start | bytes 3538952 | tf_op jit(solution)/shard_map/ppermute | solution.py:28
  120.9 29.9 %collective-permute-start.15 = (bf16[96,1536]{1,0:T(8,128)(2,1)S(1)}, bf16[96,1536]{1,0:T(8,128)(2,1)}, u32[]{:S(2)}, u32[]{:S(2)}) collective-permute-start(bf16[96,1536]{1,0:T(8,128)(2,1)S(1)} %slice.95), channel_id=1, source_target_pairs={{0,16},{1,17},{8,24},{9,25},{16,0},{17,1},{24,8},{25,9},{2,18},{3,... | collective-permute-start | bytes 884744 | tf_op jit(solution)/shard_map/ppermute | solution.py:28
  152.7 40.8 %all-to-all-start.2 = ((bf16[8,384,256]{2,1,0:T(8,128)(2,1)}), bf16[8,384,256]{2,1,0:T(8,128)(2,1)}, u32[]{:S(2)}, u32[]{:S(2)}) async-start(bf16[8,384,256]{2,1,0:T(8,128)(2,1)} %bitcast.146), calls=%async_computation.2 | async-start | bytes 3145728 | tf_op jit(solution)/shard_map/all_to_all | solution.py:824
  157.0 112.2 %all-gather.8.cloned.1.call-start = ((), (), s32[]{:S(2)}) async-start(), calls=%async_computation.11 | async-start | bytes 3317760 | tf_op jit(solution)/shard_map/all_gather | solution.py:837
  157.7 33.2 %collective-permute-start.20 = (bf16[192,1536]{1,0:T(8,128)(2,1)}, bf16[192,1536]{1,0:T(8,128)(2,1)S(1)}, u32[]{:S(2)}, u32[]{:S(2)}) collective-permute-start(bf16[192,1536]{1,0:T(8,128)(2,1)} %collective-permute-done.7), channel_id=1, source_target_pairs={{0,8},{1,9},{8,0},{9,1},{16,24},{17,25},{24,16},{25,17},{2,10},{3,... | collective-permute-start | bytes 1769480 | tf_op jit(solution)/shard_map/ppermute | solution.py:28
  157.9 32.9 %collective-permute-start.21 = (bf16[192,1536]{1,0:T(8,128)(2,1)}, bf16[192,1536]{1,0:T(8,128)(2,1)S(1)}, u32[]{:S(2)}, u32[]{:S(2)}) collective-permute-start(bf16[192,1536]{1,0:T(8,128)(2,1)} %pad_maximum_fusion.4), channel_id=1, source_target_pairs={{0,8},{1,9},{8,0},{9,1},{16,24},{17,25},{24,16},{25,17},{2,10},{3,... | collective-permute-start | bytes 1769480 | tf_op jit(solution)/shard_map/ppermute | solution.py:28
  158.2 31.5 %collective-permute-start.23 = (bf16[192,1536]{1,0:T(8,128)(2,1)S(1)}, bf16[192,1536]{1,0:T(8,128)(2,1)S(1)}, u32[]{:S(2)}, u32[]{:S(2)}) collective-permute-start(bf16[192,1536]{1,0:T(8,128)(2,1)S(1)} %slice.98), channel_id=1, source_target_pairs={{0,16},{1,17},{8,24},{9,25},{16,0},{17,1},{24,8},{25,9},{2,18},{3,... | collective-permute-start | bytes 1769480 | tf_op jit(solution)/shard_map/ppermute | solution.py:28
  204.7 286.9 %reduce-scatter.4.cloned.1.call-start = ((), (), s32[]{:S(2)}) async-start(), calls=%async_computation.12 | async-start | bytes 6881280 | tf_op jit(solution)/shard_map/reduce_scatter | solution.py:862
  302.5 33.6 %collective-permute-start.36 = (bf16[4,384,1536]{2,1,0:T(8,128)(2,1)}, bf16[4,384,1536]{2,1,0:T(8,128)(2,1)}, u32[]{:S(2)}, u32[]{:S(2)}) collective-permute-start(bf16[4,384,1536]{2,1,0:T(8,128)(2,1)} %get-tuple-element.225), channel_id=1, source_target_pairs={{0,8},{1,9},{8,0},{9,1},{16,24},{17,25},{24,16},{25,17},{2,10},{3,... | collective-permute-start | bytes 14155784 | tf_op jit(solution)/shard_map/ppermute | solution.py:28
  302.6 51.6 %collective-permute-start.39 = (bf16[4,384,1536]{2,1,0:T(8,128)(2,1)}, bf16[4,384,1536]{2,1,0:T(8,128)(2,1)}, u32[]{:S(2)}, u32[]{:S(2)}) collective-permute-start(bf16[4,384,1536]{2,1,0:T(8,128)(2,1)} %get-tuple-element.228), channel_id=1, source_target_pairs={{0,8},{1,9},{8,0},{9,1},{16,24},{17,25},{24,16},{25,17},{2,10},{3,... | collective-permute-start | bytes 14155784 | tf_op jit(solution)/shard_map/ppermute | solution.py:28
  419.8 126.5 %reduce-scatter.6.cloned.1.call-start = ((), (), s32[]{:S(2)}) async-start(), calls=%async_computation.13 | async-start | bytes 2949120 | tf_op jit(solution)/shard_map/reduce_scatter | solution.py:896
  452.5 35.8 %collective-permute-start.46 = (bf16[384,1536]{1,0:T(8,128)(2,1)}, bf16[384,1536]{1,0:T(8,128)(2,1)}, u32[]{:S(2)}, u32[]{:S(2)}) collective-permute-start(bf16[384,1536]{1,0:T(8,128)(2,1)} %merge.16), channel_id=1, source_target_pairs={{0,1},{1,0},{8,9},{9,8},{16,17},{17,16},{24,25},{25,24},{2,3},{3,2... | collective-permute-start | bytes 3538952 | tf_op jit(solution)/shard_map/ppermute | solution.py:28
  454.0 34.4 %collective-permute-start.47 = (bf16[384,1536]{1,0:T(8,128)(2,1)}, bf16[384,1536]{1,0:T(8,128)(2,1)}, u32[]{:S(2)}, u32[]{:S(2)}) collective-permute-start(bf16[384,1536]{1,0:T(8,128)(2,1)} %merge.17), channel_id=1, source_target_pairs={{0,16},{1,17},{8,24},{9,25},{16,0},{17,1},{24,8},{25,9},{2,18},{3,... | collective-permute-start | bytes 3538952 | tf_op jit(solution)/shard_map/ppermute | solution.py:28
  456.2 32.2 %collective-permute-start.48 = (bf16[96,1536]{1,0:T(8,128)(2,1)}, bf16[96,1536]{1,0:T(8,128)(2,1)S(1)}, u32[]{:S(2)}, u32[]{:S(2)}) collective-permute-start(bf16[96,1536]{1,0:T(8,128)(2,1)} %get-tuple-element.329), channel_id=1, source_target_pairs={{0,16},{1,17},{8,24},{9,25},{16,0},{17,1},{24,8},{25,9},{2,18},{3,... | collective-permute-start | bytes 884744 | tf_op jit(solution)/shard_map/ppermute | solution.py:28
  456.8 31.6 %collective-permute-start.49 = (bf16[96,1536]{1,0:T(8,128)(2,1)S(1)}, bf16[96,1536]{1,0:T(8,128)(2,1)S(1)}, u32[]{:S(2)}, u32[]{:S(2)}) collective-permute-start(bf16[96,1536]{1,0:T(8,128)(2,1)S(1)} %get-tuple-element.328), channel_id=1, source_target_pairs={{0,1},{1,0},{8,9},{9,8},{16,17},{17,16},{24,25},{25,24},{2,3},{3,2... | collective-permute-start | bytes 884744 | tf_op jit(solution)/shard_map/ppermute | solution.py:28
  491.5 47.5 %all-to-all-start.4 = ((bf16[8,48,1792]{2,1,0:T(8,128)(2,1)}), bf16[8,48,1792]{2,1,0:T(8,128)(2,1)}, u32[]{:S(2)}, u32[]{:S(2)}) async-start(bf16[8,48,1792]{2,1,0:T(8,128)(2,1)} %bitcast.147), calls=%async_computation.5 | async-start | bytes 2752512 | tf_op jit(solution)/shard_map/all_to_all | solution.py:899
  495.8 117.8 %reduce-scatter.8.cloned.1.call-start = ((), (), s32[]{:S(2)}) async-start(), calls=%async_computation.14 | async-start | bytes 3317760 | tf_op jit(solution)/shard_map/reduce_scatter | solution.py:910
  498.0 28.8 %collective-permute-start.53 = (bf16[192,1536]{1,0:T(8,128)(2,1)S(1)}, bf16[192,1536]{1,0:T(8,128)(2,1)S(1)}, u32[]{:S(2)}, u32[]{:S(2)}) collective-permute-start(bf16[192,1536]{1,0:T(8,128)(2,1)S(1)} %merge.20), channel_id=1, source_target_pairs={{0,1},{1,0},{8,9},{9,8},{16,17},{17,16},{24,25},{25,24},{2,3},{3,2... | collective-permute-start | bytes 1769480 | tf_op jit(solution)/shard_map/ppermute | solution.py:28
  503.3 35.8 %collective-permute-start.51 = (bf16[192,1536]{1,0:T(8,128)(2,1)S(1)}, bf16[192,1536]{1,0:T(8,128)(2,1)S(1)}, u32[]{:S(2)}, u32[]{:S(2)}) collective-permute-start(bf16[192,1536]{1,0:T(8,128)(2,1)S(1)} %get-tuple-element.319), channel_id=1, source_target_pairs={{0,16},{1,17},{8,24},{9,25},{16,0},{17,1},{24,8},{25,9},{2,18},{3,... | collective-permute-start | bytes 1769480 | tf_op jit(solution)/shard_map/ppermute | solution.py:28
  503.9 35.2 %collective-permute-start.52 = (bf16[192,1536]{1,0:T(8,128)(2,1)S(1)}, bf16[192,1536]{1,0:T(8,128)(2,1)S(1)}, u32[]{:S(2)}, u32[]{:S(2)}) collective-permute-start(bf16[192,1536]{1,0:T(8,128)(2,1)S(1)} %get-tuple-element.318), channel_id=1, source_target_pairs={{0,1},{1,0},{8,9},{9,8},{16,17},{17,16},{24,25},{25,24},{2,3},{3,2... | collective-permute-start | bytes 1769480 | tf_op jit(solution)/shard_map/ppermute | solution.py:28
  554.0 43.2 %collective-permute-start.55 = (bf16[384,1536]{1,0:T(8,128)(2,1)}, bf16[384,1536]{1,0:T(8,128)(2,1)}, u32[]{:S(2)}, u32[]{:S(2)}) collective-permute-start(bf16[384,1536]{1,0:T(8,128)(2,1)} %merge.22), channel_id=1, source_target_pairs={{0,1},{1,0},{8,9},{9,8},{16,17},{17,16},{24,25},{25,24},{2,3},{3,2... | collective-permute-start | bytes 3538952 | tf_op jit(solution)/shard_map/ppermute | solution.py:28
  555.4 41.7 %collective-permute-start.56 = (bf16[384,1536]{1,0:T(8,128)(2,1)}, bf16[384,1536]{1,0:T(8,128)(2,1)}, u32[]{:S(2)}, u32[]{:S(2)}) collective-permute-start(bf16[384,1536]{1,0:T(8,128)(2,1)} %merge.23), channel_id=1, source_target_pairs={{0,16},{1,17},{8,24},{9,25},{16,0},{17,1},{24,8},{25,9},{2,18},{3,... | collective-permute-start | bytes 3538952 | tf_op jit(solution)/shard_map/ppermute | solution.py:28
  558.3 38.8 %all-to-all-start.5 = ((bf16[8,48,768]{2,1,0:T(8,128)(2,1)}), bf16[8,48,768]{2,1,0:T(8,128)(2,1)}, u32[]{:S(2)}, u32[]{:S(2)}) async-start(bf16[8,48,768]{2,1,0:T(8,128)(2,1)} %bitcast.56), calls=%async_computation.7 | async-start | bytes 1179648 | tf_op jit(solution)/shard_map/all_to_all | solution.py:912
  568.5 28.6 %collective-permute-start.59 = (bf16[48,1536]{1,0:T(8,128)(2,1)}, bf16[48,1536]{1,0:T(8,128)(2,1)}, u32[]{:S(2)}, u32[]{:S(2)}) collective-permute-start(bf16[48,1536]{1,0:T(8,128)(2,1)} %get-tuple-element.324), channel_id=1, source_target_pairs={{0,2},{2,6},{6,4},{4,0},{1,3},{3,7},{7,5},{5,1},{8,10},{10,14},{14... | collective-permute-start | bytes 442376 | tf_op jit(solution)/shard_map/ppermute | solution.py:219
  (124 other events, 1363.7 us)
Sparse Core Ops, SparseCore 0:
  33.1 55.0 all-gather.3
  94.2 105.5 all-gather.5
  204.8 57.5 all-gather.7
  390.1 101.3 reduce-scatter.3
  493.7 48.5 reduce-scatter.5
  546.4 61.6 reduce-scatter.7

commit v4 on v3

--- a/solution.py
+++ b/solution.py
@@ -71,16 +71,18 @@
     return cross_gather(diag_gather(got, sizes), sizes)
 
 
-def stack(blocks):
-    count = len(blocks)
+def stack(blocks, count=None, first=0, kept=None):
+    here = len(blocks)
+    count = count or here
+    more = [] if kept is None else [kept]
 
     def body(*refs):
-        parts, out, held, came, left = refs[:count], *refs[count:]
-        ins = [pltpu.make_async_copy(parts[i], held.at[i], came.at[i]) for i in range(count)]
-        outs = [pltpu.make_async_copy(held.at[i], out.at[i], left.at[i]) for i in range(count)]
+        parts, (out, held, came, left) = refs[:here], refs[-4:]
+        ins = [pltpu.make_async_copy(parts[i], held.at[i], came.at[i]) for i in range(here)]
+        outs = [pltpu.make_async_copy(held.at[i], out.at[first + i], left.at[i]) for i in range(here)]
         for copy in ins:
             copy.start()
-        for i in range(count):
+        for i in range(here):
             ins[i].wait()
             outs[i].start()
         for copy in outs:
@@ -88,20 +90,19 @@
 
     return pl.pallas_call(
         body,
-        in_specs=[pl.BlockSpec(memory_space=pl.ANY)] * count,
+        in_specs=[pl.BlockSpec(memory_space=pl.ANY)] * (here + len(more)),
         out_specs=pl.BlockSpec(memory_space=pl.ANY),
         out_shape=jax.ShapeDtypeStruct((count, *blocks[0].shape), blocks[0].dtype),
+        input_output_aliases={here: 0} if more else {},
         scratch_shapes=[
-            pltpu.VMEM((count, *blocks[0].shape), blocks[0].dtype),
-            pltpu.SemaphoreType.DMA((count,)),
-            pltpu.SemaphoreType.DMA((count,)),
+            pltpu.VMEM((here, *blocks[0].shape), blocks[0].dtype),
+            pltpu.SemaphoreType.DMA((here,)),
+            pltpu.SemaphoreType.DMA((here,)),
         ],
         compiler_params=pltpu.CompilerParams(vmem_limit_bytes=60 * 2**20),
-        cost_estimate=pl.CostEstimate(
-            flops=0, bytes_accessed=4 * count * blocks[0].size, transcendentals=0
-        ),
+        cost_estimate=pl.CostEstimate(flops=0, bytes_accessed=4 * here * blocks[0].size, transcendentals=0),
         name="stack",
-    )(*blocks)
+    )(*blocks, *more)
 
 
 def merge(near, cross, at, one=None, two=None):
@@ -776,6 +777,10 @@
         rim_route += [(z * ny + 1, (z + 1) * ny), ((z + 1) * ny, z * ny + 1)]
     down_route = [(z + 1, z) for z in range(nz - 1)]
 
+    def stack_sides(parts):
+        near = stack([parts[h] for h in hops[:sides]], len(hops))
+        return stack([parts[h] for h in hops[sides:]], len(hops), sides, near)
+
     def rim(values, start):
         count, last = values.shape[0], values.shape[-1]
         some = values.reshape(count, slots, span, last)[:, :, start : start + 2].reshape(count, 2 * slots, last)
@@ -796,18 +801,18 @@
     pairs = tokens.reshape(slots, span, width)
     pairs = jnp.where(row_y == 0, pairs[:, :2], pairs[:, -2:]).reshape(2 * slots, width)
     x_rim = lax.ppermute(jnp.pad(pairs, ((0, edge - 2 * slots), (0, 0))), ("z", "y"), rim_route)
-    (cut, w_out, x_rim), (x_late, gate_late) = after((cut, w_out, x_rim), (x_bf, gate_weight))
+    (cut, x_rim), (x_late, gate_late) = after((cut, x_rim), (x_bf, gate_weight))
     x_late = jnp.concatenate([x_late, x_rim], axis=0)
 
     w_in = lax.all_gather(cut.reshape(ndp, ny * own_in, 3 * cpad), "z", axis=1, tiled=True).reshape(width, 3 * cpad)
     w_out = line.place(w_out, 0).reshape(chan, width + 128)
     taps = w_out[:, width : width + 8].astype(F32).T
     taps = jnp.pad(taps, ((0, 0), (0, cpad - chan)))
-    w_out = near_gather(w_out[:, :width], sizes)
+    w_out = w_out[:, :width]
     x_all = near_gather(x_late, sizes)
     both = cut_columns([gate_late, up_weight], own_hid, hpad, plan)
     both = lax.all_to_all(both, GROUP, 0, 0, tiled=True).reshape(ndp, ny * own_in, 2 * hpad)
-    x_all, both, w_in, w_out = hold((x_all, both, w_in, w_out))
+    x_all, both, w_out = hold((x_all, both, w_out))
 
     w_both = lax.all_gather(both, "z", axis=1, tiled=True).reshape(width, 2 * hpad)
     x_all = far_gather(x_all, sizes)
@@ -815,15 +820,15 @@
     gain_b = w_in[:, chan + 1].astype(F32).reshape(1, width)
     x_all, (w_out, d_late) = after(x_all, (w_out, d_out_bf))
 
-    w_out = diag_gather(w_out, sizes)
-    x_all = stack([x_all[h] for h in hops])
+    w_out = near_gather(w_out, sizes)
+    x_all = stack_sides(x_all)
     d_all = near_gather(d_late, sizes)
     a_all, bcx, o_all = mix_forward(x_all, w_in, gain_a, taps, place, sides, slots, span, edge)
-    o_all, w_out, d_all = hold((o_all, w_out, d_all))
+    o_all, w_out = hold((o_all, w_out))
+    w_out = diag_gather(w_out, sizes)
 
     o_own = lax.all_to_all(o_all.reshape(len(hops), rows, cpad), GROUP, 0, 0, tiled=True)
     w_some = cross_gather(w_out, sizes)
-    d_all = diag_gather(d_all, sizes)
     w_out = jnp.zeros((len(hops), cpad, width), BF)
     for i, h in enumerate(hops):
         w_out = lax.dynamic_update_slice(w_out, w_some[h][None], (turn_at[i], 0, 0))
@@ -832,16 +837,16 @@
 
     block = rows // 2
     o_cat, h1, a2 = attend(o_own, w_out, x_bf, gain_b, block)
-    (a2, d_all, w_both), down_weight = after((a2, d_all, w_both), down_weight)
+    (_, w_both), down_weight = after((a2, w_both), down_weight)
 
     w_down = lax.all_gather(down_weight, "z", axis=0, tiled=True)
-    d_all = cross_gather(d_all, sizes)
     a2_all = near_gather(a2, sizes)
+    d_all = cross_gather(diag_gather(d_all, sizes), sizes)
     a2_all, d_all = hold((a2_all, d_all))
     d_all = stack([d_all[h] for h in hops])
     a2_all, d_all = hold((diag_gather(a2_all, sizes), d_all))
     a2_all = cross_gather(a2_all, sizes)
-    a2_all = stack([a2_all[h] for h in hops])
+    a2_all = stack_sides(a2_all)
 
     m, d_both, f_far, da_far = feed(a2_all, d_all, w_both, w_down, len(hops) // 2)
     m, d_both, f_near, da_near = feed(a2_all, d_all, w_both, w_down, 0, (m, d_both))
@@ -903,9 +908,9 @@
     da.send_far()
     out.sum_near()
     out.send_near()
-    da.more, both_sum, out.last = hold((da.more, both_sum, out.last))
+    da.more = hold(da.more)
     da.sum_near()
-    da.total, in_sum = after(da.total, in_sum)
+    _, in_sum, both_sum, out.last = hold((da.total, in_sum, both_sum, out.last))
     in_sum, down_part = after(in_sum, down_part)
     down_grad = lax.psum_scatter(down_part, "z", scatter_dimension=0, tiled=True)
     da.send_near()
@@ -920,9 +925,7 @@
     (gate_grad, up_grad), gain_two_grad = join_columns(
         both_sum, [gate_weight, up_weight], gain_two, own_hid, hpad, plan
     )
-    in_sum, da.last, out_grad, conv_grad, mixed, gate_grad, up_grad = hold(
-        (in_sum, da.last, out_grad, conv_grad, mixed, gate_grad, up_grad)
-    )
+    in_sum, da.last, mixed, gate_grad, up_grad = hold((in_sum, da.last, mixed, gate_grad, up_grad))
 
     input_grad = finish(da.terms(), x_bf, dh1, gain_a, block)
     out_grad = sum(term.astype(F32) for term in out_grad)

time: 633 us -> 608 us (0.961)
  the two profiles are of different devices: /device:TPU:0 before, /device:TPU:10 now
where the time goes in v4:
time: 608 us; the launch traced here: 599 us
  waiting for transfers between devices  193 us (32%)
  Pallas kernels  179 us (29%)
  starting transfers between devices  83 us (14%)
  local copies, waits for them, and re-layouts  65.4 us (11%)
  matrix products  39.4 us (6%)
  other arithmetic  22.6 us (4%)
  between operations  15.6 us (3%)
    ppermute x52, waiting for transfers between devices, send(): return lax.ppermute(block, GROUP, route)  113 us
    pallas_call x2, Pallas kernels, feed(): pl.pallas_call(lambda *refs: feed_body(hid, hpad, *refs), grid=(half,), i...  66.3 us
    dot_general x3, matrix products, dot_tn(): lax.dot_general(left, right, (((0,), (0,)), ((), ())), preferred_element_...  39.4 us
    unnamed x145, local copies, waits for them, and re-layouts  36.5 us
    ppermute x52, starting transfers between devices, send(): return lax.ppermute(block, GROUP, route)  34.9 us
    pallas_call x1, Pallas kernels, mix_backward(): pl.pallas_call(lambda *refs: mix_backward_body(cpad, slots, span, edge, *...  28.8 us
    ppermute x6, waiting for transfers between devices, reduce_direct(): terms.append(lax.ppermute(part, 'z', route))  24.3 us
    pallas_call x5, Pallas kernels, stack(): pl.pallas_call(body, in_specs=[pl.BlockSpec(memory_space=pl.ANY)] * (here...  23 us
  transfers between devices with their start and end apart: 75, of which 37 were waited for; matrix products, arithmetic and copies ran while one was open for 15% of the time, Pallas kernels for 24%

profile of v4, /device:TPU:10, one launch (start us, length us, event | category | flops | bytes accessed | tf_op | source)
XLA Modules:
  0.0 598.5 jit_solution(15609811297929868229)
XLA Ops:
  10.3 4.3 all-to-all-start
  19.0 4.2 collective-permute-done
  34.8 4.8 all-to-all-start.1
  39.5 4.6 collective-permute-done.3
  45.0 11.9 %collective-permute-done.4 = bf16[48,1664]{1,0:T(8,128)(2,1)} collective-permute-done((bf16[48,1664]{1,0:T(8,128)(2,1)S(1)}, bf16[48,1664]{1,0:T(8,128)(2,1)}, u32[]{:S(2)}, u32[]{:S(2)}) %collective-permute-start.4) | collective-permute-done | bytes 159776 | tf_op jit(solution)/shard_map/ppermute | solution.py:204
  59.7 15.5 %all-to-all-done.1 = bf16[8,48,1792]{2,1,0:T(8,128)(2,1)S(1)} async-done(((bf16[8,48,1792]{2,1,0:T(8,128)(2,1)}), bf16[8,48,1792]{2,1,0:T(8,128)(2,1)S(1)}, u32[]{:S(2)}, u32[]{:S(2)}) %all-to-all-start.1) | async-done | bytes 1376288 | tf_op jit(solution)/shard_map/all_to_all | solution.py:814
  81.2 12.1 %collective-permute-done.8 = bf16[200,1536]{1,0:T(8,128)(2,1)S(1)} collective-permute-done((bf16[200,1536]{1,0:T(8,128)(2,1)S(1)}, bf16[200,1536]{1,0:T(8,128)(2,1)S(1)}, u32[]{:S(2)}, u32[]{:S(2)}) %collective-permute-start.8) | collective-permute-done | bytes 614432 | tf_op jit(solution)/shard_map/ppermute | solution.py:28
  103.2 4.0 stack.105.refs_4_
  107.1 4.1 stack.106.refs_1_.refs_2_.refs_3_.refs_4_
  113.6 16.0 %mix_forward.1 = (bf16[4,2,384,1536]{3,2,1,0:T(8,128)(2,1)}, f32[4,800,768]{2,1,0:T(8,128)}, bf16[4,2,384,256]{3,2,1,0:T(8,128)(2,1)}) custom-call(s32[8]{0:T(128)} %stack.99.refs_0_, bf16[8,400,1536]{2,1,0:T(8,128)(2,1)} %stack.106.refs_1_.refs_2_.refs_3_.refs_4_, bf16[8,400,1536]{2,1,0:T(8,128)(2,1)} %stack.106.refs_1_.refs_2_.refs_3_.refs_4_, ...), custom_call_target="tpu_custom_call" | custom-call | flops 7549747200 | bytes 33554432 | tf_op jit(solution)/shard_map/mix_forward/pallas_call | solution.py:415
  129.7 4.5 all-to-all-start.2
  141.1 22.4 %collective-permute-done.14 = bf16[96,1536]{1,0:T(8,128)(2,1)S(1)} collective-permute-done((bf16[96,1536]{1,0:T(8,128)(2,1)S(1)}, bf16[96,1536]{1,0:T(8,128)(2,1)S(1)}, u32[]{:S(2)}, u32[]{:S(2)}) %collective-permute-start.14) | collective-permute-done | bytes 294944 | tf_op jit(solution)/shard_map/ppermute | solution.py:28
  178.1 4.3 attend.1
  191.9 25.5 %collective-permute-done.20.refs_1_ = bf16[384,1536]{1,0:T(8,128)(2,1)S(1)} collective-permute-done((bf16[384,1536]{1,0:T(8,128)(2,1)S(1)}, bf16[384,1536]{1,0:T(8,128)(2,1)S(1)}, u32[]{:S(2)}, u32[]{:S(2)}) %collective-permute-start.20) | collective-permute-done | bytes 1179680 | tf_op jit(solution)/shard_map/ppermute | solution.py:28
  223.2 7.4 %stack.107.refs_1_ = bf16[8,384,1536]{2,1,0:T(8,128)(2,1)} custom-call(bf16[384,1536]{1,0:T(8,128)(2,1)} %copy-done.13, bf16[384,1536]{1,0:T(8,128)(2,1)} %copy-done.39, bf16[384,1536]{1,0:T(8,128)(2,1)} %collective-permute-done.25.refs_2_, bf16[384,1536]{1,0:T(8,128)(2,1)} %copy-done.42, bf16[384,1536]{1,0:T(8,128)(2,1)} %collective-permute-done.23.refs_4_, ...), custom_call_target="tpu_custom_call" | custom-call | bytes 18874368 | tf_op jit(solution)/shard_map/stack/pallas_call | solution.py:91
  250.6 33.2 %feed.2 = (bf16[8,384,864]{2,1,0:T(8,128)(2,1)}, bf16[8,384,1792]{2,1,0:T(8,128)(2,1)}, bf16[4,384,1536]{2,1,0:T(8,128)(2,1)}, bf16[4,384,1536]{2,1,0:T(8,128)(2,1)}) custom-call(bf16[8,384,1536]{2,1,0:T(8,128)(2,1)} %stack.109.refs_0_, bf16[8,384,1536]{2,1,0:T(8,128)(2,1)} %stack.107.refs_1_, bf16[1536,1792]{1,0:T(8,128)(2,1)} %bitcast.160, ...), custom_call_target="tpu_custom_call" | custom-call | flops 24461180928 | bytes 41943040 | tf_op jit(solution)/shard_map/feed/pallas_call | solution.py:710
  284.4 33.1 %feed.3 = (bf16[8,384,864]{2,1,0:T(8,128)(2,1)}, bf16[8,384,1792]{2,1,0:T(8,128)(2,1)}, bf16[4,384,1536]{2,1,0:T(8,128)(2,1)}, bf16[4,384,1536]{2,1,0:T(8,128)(2,1)}) custom-call(bf16[8,384,1536]{2,1,0:T(8,128)(2,1)} %stack.109.refs_0_, bf16[8,384,1536]{2,1,0:T(8,128)(2,1)} %stack.107.refs_1_, ...), custom_call_target="tpu_custom_call", output_to_operand_aliasing={{0}: (4, {}), {1}: (5, {})} | custom-call | flops 24461180928 | bytes 41943040 | tf_op jit(solution)/shard_map/feed/pallas_call | solution.py:710
  322.9 12.4 %bitcast_convert_fusion.1 = bf16[864,1536]{1,0:T(8,128)(2,1)} fusion(bf16[8,384,864]{2,1,0:T(8,128)(2,1)S(1)} %copy-done.62, bf16[8,384,1536]{2,1,0:T(8,128)(2,1)} %stack.107.refs_1_), kind=kOutput, calls=%fused_computation.2 | convolution fusion | flops 8155054080 | bytes 17399808 | tf_op jit(solution)/shard_map/dot_general | solution.py:233
  345.8 23.3 %bitcast_convert_fusion = bf16[1536,1792]{1,0:T(8,128)(2,1)} fusion(bf16[8,384,1536]{2,1,0:T(8,128)(2,1)S(1)} %bitcast.137, bf16[8,384,1792]{2,1,0:T(8,128)(2,1)} %get-tuple-element.189), kind=kOutput, calls=%fused_computation | convolution fusion | flops 16914186240 | bytes 25952256 | tf_op jit(solution)/shard_map/dot_general | solution.py:233
  377.8 9.4 %turn.1 = (f32[384,1536]{1,0:T(8,128)S(1)}, bf16[384,1536]{1,0:T(8,128)(2,1)S(1)}, bf16[8,384,256]{2,1,0:T(8,128)(2,1)S(1)}) custom-call(bf16[4,384,1536]{2,1,0:T(8,128)(2,1)} %get-tuple-element.178.refs_0_, bf16[4,384,1536]{2,1,0:T(8,128)(2,1)} %collective-permute-done.36.refs_1_, bf16[1,384,1536]{2,1,0:T(8,128)(2,1)S(1)} %bitcast.134, ...), custom_call_target="tpu_custom_call" | custom-call | flops 2415919104 | bytes 20971520 | tf_op jit(solution)/shard_map/turn/pallas_call | solution.py:634
  396.5 5.0 all-to-all-start.3
  409.4 11.7 %all-to-all-done.3.refs_1_.refs_2_ = bf16[8,384,256]{2,1,0:T(8,128)(2,1)} async-done(((bf16[8,384,256]{2,1,0:T(8,128)(2,1)}), bf16[8,384,256]{2,1,0:T(8,128)(2,1)}, u32[]{:S(2)}, u32[]{:S(2)}) %all-to-all-start.3) | async-done | bytes 1572896 | tf_op jit(solution)/shard_map/all_to_all | solution.py:877
  435.2 28.8 %mix_backward.1 = (bf16[1536,768]{1,0:T(8,128)(2,1)}, bf16[2,2,384,1536]{3,2,1,0:T(8,128)(2,1)}, bf16[2,2,384,1536]{3,2,1,0:T(8,128)(2,1)}, f32[8,256]{1,0:T(8,128)}) custom-call(s32[8]{0:T(128)} %stack.90.refs_0_, bf16[8,384,256]{2,1,0:T(8,128)(2,1)} %all-to-all-done.3.refs_1_.refs_2_, bf16[8,384,256]{2,1,0:T(8,128)(2,1)} %all-to-all-done.3.refs_1_.refs_2_, ...), custom_call_target="tpu_custom_call" | custom-call | flops 14495514624 | bytes 41943040 | tf_op jit(solution)/shard_map/mix_backward/pallas_call | solution.py:534
  465.7 4.1 reduce-scatter.4.cloned.1.call-done
  469.8 4.7 all-to-all-start.4
  483.3 20.5 %collective-permute-done.51.refs_2_ = bf16[192,1536]{1,0:T(8,128)(2,1)S(1)} collective-permute-done((bf16[192,1536]{1,0:T(8,128)(2,1)S(1)}, bf16[192,1536]{1,0:T(8,128)(2,1)S(1)}, u32[]{:S(2)}, u32[]{:S(2)}) %collective-permute-start.51) | collective-permute-done | bytes 589856 | tf_op jit(solution)/shard_map/ppermute | solution.py:28
  509.5 7.8 %collective-permute-done.53 = bf16[192,1536]{1,0:T(8,128)(2,1)S(1)} collective-permute-done((bf16[192,1536]{1,0:T(8,128)(2,1)S(1)}, bf16[192,1536]{1,0:T(8,128)(2,1)S(1)}, u32[]{:S(2)}, u32[]{:S(2)}) %collective-permute-start.53) | collective-permute-done | bytes 589856 | tf_op jit(solution)/shard_map/ppermute | solution.py:28
  527.8 4.6 fusion.3
  534.4 5.1 all-to-all-start.5
  551.1 5.1 collective-permute-done.62
  556.3 19.1 %collective-permute-done.61 = bf16[48,1536]{1,0:T(8,128)(2,1)} collective-permute-done((bf16[48,1536]{1,0:T(8,128)(2,1)}, bf16[48,1536]{1,0:T(8,128)(2,1)}, u32[]{:S(2)}, u32[]{:S(2)}) %collective-permute-start.61) | collective-permute-done | bytes 147488 | tf_op jit(solution)/shard_map/ppermute | solution.py:220
  584.3 4.6 finish.1
  (376 shorter events, 205.1 us)
Async XLA Ops:
  14.6 96.6 %all-gather.4.cloned.1.call-start = ((), (), s32[]{:S(2)}) async-start(), calls=%async_computation.9 | async-start | bytes 2949120 | tf_op jit(solution)/shard_map/all_gather | solution.py:807
  28.2 28.7 %collective-permute-start.4 = (bf16[48,1664]{1,0:T(8,128)(2,1)S(1)}, bf16[48,1664]{1,0:T(8,128)(2,1)}, u32[]{:S(2)}, u32[]{:S(2)}) collective-permute-start(bf16[48,1664]{1,0:T(8,128)(2,1)S(1)} %fusion.10), channel_id=1, source_target_pairs={{0,6},{2,4},{6,0},{4,2},{1,7},{3,5},{7,1},{5,3},{8,14},{10,12},{14... | collective-permute-start | bytes 479240 | tf_op jit(solution)/shard_map/ppermute | solution.py:204
  28.2 29.6 %collective-permute-start.5 = (bf16[48,1664]{1,0:T(8,128)(2,1)S(1)}, bf16[48,1664]{1,0:T(8,128)(2,1)}, u32[]{:S(2)}, u32[]{:S(2)}) collective-permute-start(bf16[48,1664]{1,0:T(8,128)(2,1)S(1)} %fusion.10), channel_id=1, source_target_pairs={{0,4},{2,0},{6,2},{4,6},{1,5},{3,1},{7,3},{5,7},{8,12},{10,8},{14,... | collective-permute-start | bytes 479240 | tf_op jit(solution)/shard_map/ppermute | solution.py:204
  31.9 43.2 %collective-permute-start.1 = (bf16[400,1536]{1,0:T(8,128)(2,1)}, bf16[400,1536]{1,0:T(8,128)(2,1)}, u32[]{:S(2)}, u32[]{:S(2)}) collective-permute-start(bf16[400,1536]{1,0:T(8,128)(2,1)} %constant_dynamic-update-slice_fusion.refs_0_), channel_id=1, source_target_pairs={{0,1},{1,0},{8,9},{9,8},{16,17},{17,16},{24,25},{25,24},{2,3},{3,2... | collective-permute-start | bytes 3686408 | tf_op jit(solution)/shard_map/ppermute | solution.py:28
  32.3 42.8 %collective-permute-start.2 = (bf16[400,1536]{1,0:T(8,128)(2,1)}, bf16[400,1536]{1,0:T(8,128)(2,1)}, u32[]{:S(2)}, u32[]{:S(2)}) collective-permute-start(bf16[400,1536]{1,0:T(8,128)(2,1)} %constant_dynamic-update-slice_fusion.refs_0_), channel_id=1, source_target_pairs={{0,16},{1,17},{8,24},{9,25},{16,0},{17,1},{24,8},{25,9},{2,18},{3,... | collective-permute-start | bytes 3686408 | tf_op jit(solution)/shard_map/ppermute | solution.py:28
  34.8 40.4 %all-to-all-start.1 = ((bf16[8,48,1792]{2,1,0:T(8,128)(2,1)}), bf16[8,48,1792]{2,1,0:T(8,128)(2,1)S(1)}, u32[]{:S(2)}, u32[]{:S(2)}) async-start(bf16[8,48,1792]{2,1,0:T(8,128)(2,1)} %cut_columns.3), calls=%async_computation.1 | async-start | bytes 2752512 | tf_op jit(solution)/shard_map/all_to_all | solution.py:814
  39.5 145.5 %all-gather.6.cloned.1.call-start = ((), (), s32[]{:S(2)}) async-start(), calls=%async_computation.10 | async-start | bytes 6881280 | tf_op jit(solution)/shard_map/all_gather | solution.py:817
  99.1 30.6 %collective-permute-start.12 = (bf16[192,1536]{1,0:T(8,128)(2,1)}, bf16[192,1536]{1,0:T(8,128)(2,1)}, u32[]{:S(2)}, u32[]{:S(2)}) collective-permute-start(bf16[192,1536]{1,0:T(8,128)(2,1)} %slice.116), channel_id=1, source_target_pairs={{0,1},{1,0},{8,9},{9,8},{16,17},{17,16},{24,25},{25,24},{2,3},{3,2... | collective-permute-start | bytes 1769480 | tf_op jit(solution)/shard_map/ppermute | solution.py:28
  100.8 28.8 %collective-permute-start.13 = (bf16[192,1536]{1,0:T(8,128)(2,1)}, bf16[192,1536]{1,0:T(8,128)(2,1)}, u32[]{:S(2)}, u32[]{:S(2)}) collective-permute-start(bf16[192,1536]{1,0:T(8,128)(2,1)} %slice.116), channel_id=1, source_target_pairs={{0,16},{1,17},{8,24},{9,25},{16,0},{17,1},{24,8},{25,9},{2,18},{3,... | collective-permute-start | bytes 1769480 | tf_op jit(solution)/shard_map/ppermute | solution.py:28
  101.2 70.3 %collective-permute-start.22 = (bf16[384,1536]{1,0:T(8,128)(2,1)S(1)}, bf16[384,1536]{1,0:T(8,128)(2,1)S(1)}, u32[]{:S(2)}, u32[]{:S(2)}) collective-permute-start(bf16[384,1536]{1,0:T(8,128)(2,1)S(1)} %fusion.4.refs_0_.refs_4_), channel_id=1, source_target_pairs={{0,1},{1,0},{8,9},{9,8},{16,17},{17,16},{24,25},{25,24},{2,3},{3,2... | collective-permute-start | bytes 3538952 | tf_op jit(solution)/shard_map/ppermute | solution.py:28
  101.5 88.2 %collective-permute-start.23 = (bf16[384,1536]{1,0:T(8,128)(2,1)S(1)}, bf16[384,1536]{1,0:T(8,128)(2,1)}, u32[]{:S(2)}, u32[]{:S(2)}) collective-permute-start(bf16[384,1536]{1,0:T(8,128)(2,1)S(1)} %fusion.4.refs_0_.refs_4_), channel_id=1, source_target_pairs={{0,8},{1,9},{8,0},{9,1},{16,24},{17,25},{24,16},{25,17},{2,10},{3,... | collective-permute-start | bytes 3538952 | tf_op jit(solution)/shard_map/ppermute | solution.py:28
  101.5 66.7 %collective-permute-start.25 = (bf16[384,1536]{1,0:T(8,128)(2,1)S(1)}, bf16[384,1536]{1,0:T(8,128)(2,1)}, u32[]{:S(2)}, u32[]{:S(2)}) collective-permute-start(bf16[384,1536]{1,0:T(8,128)(2,1)S(1)} %fusion.4.refs_0_.refs_4_), channel_id=1, source_target_pairs={{0,16},{1,17},{8,24},{9,25},{16,0},{17,1},{24,8},{25,9},{2,18},{3,... | collective-permute-start | bytes 3538952 | tf_op jit(solution)/shard_map/ppermute | solution.py:28
  129.7 45.7 %all-to-all-start.2 = ((bf16[8,384,256]{2,1,0:T(8,128)(2,1)}), bf16[8,384,256]{2,1,0:T(8,128)(2,1)}, u32[]{:S(2)}, u32[]{:S(2)}) async-start(bf16[8,384,256]{2,1,0:T(8,128)(2,1)} %bitcast.151), calls=%async_computation.2 | async-start | bytes 3145728 | tf_op jit(solution)/shard_map/all_to_all | solution.py:830
  134.2 116.5 %all-gather.8.cloned.1.call-start = ((), (), s32[]{:S(2)}) async-start(), calls=%async_computation.11 | async-start | bytes 3317760 | tf_op jit(solution)/shard_map/all_gather | solution.py:842
  185.0 284.8 %reduce-scatter.4.cloned.1.call-start = ((), (), s32[]{:S(2)}) async-start(), calls=%async_computation.12 | async-start | bytes 6881280 | tf_op jit(solution)/shard_map/reduce_scatter | solution.py:867
  189.0 28.4 %collective-permute-start.20 = (bf16[384,1536]{1,0:T(8,128)(2,1)S(1)}, bf16[384,1536]{1,0:T(8,128)(2,1)S(1)}, u32[]{:S(2)}, u32[]{:S(2)}) collective-permute-start(bf16[384,1536]{1,0:T(8,128)(2,1)S(1)} %get-tuple-element.168.refs_0_), channel_id=1, source_target_pairs={{0,1},{1,0},{8,9},{9,8},{16,17},{17,16},{24,25},{25,24},{2,3},{3,2... | collective-permute-start | bytes 3538952 | tf_op jit(solution)/shard_map/ppermute | solution.py:28
  283.8 33.6 %collective-permute-start.36 = (bf16[4,384,1536]{2,1,0:T(8,128)(2,1)}, bf16[4,384,1536]{2,1,0:T(8,128)(2,1)}, u32[]{:S(2)}, u32[]{:S(2)}) collective-permute-start(bf16[4,384,1536]{2,1,0:T(8,128)(2,1)} %get-tuple-element.179), channel_id=1, source_target_pairs={{0,8},{1,9},{8,0},{9,1},{16,24},{17,25},{24,16},{25,17},{2,10},{3,... | collective-permute-start | bytes 14155784 | tf_op jit(solution)/shard_map/ppermute | solution.py:28
  284.0 51.4 %collective-permute-start.39 = (bf16[4,384,1536]{2,1,0:T(8,128)(2,1)}, bf16[4,384,1536]{2,1,0:T(8,128)(2,1)}, u32[]{:S(2)}, u32[]{:S(2)}) collective-permute-start(bf16[4,384,1536]{2,1,0:T(8,128)(2,1)} %get-tuple-element.182), channel_id=1, source_target_pairs={{0,8},{1,9},{8,0},{9,1},{16,24},{17,25},{24,16},{25,17},{2,10},{3,... | collective-permute-start | bytes 14155784 | tf_op jit(solution)/shard_map/ppermute | solution.py:28
  401.5 117.9 %reduce-scatter.6.cloned.1.call-start = ((), (), s32[]{:S(2)}) async-start(), calls=%async_computation.13 | async-start | bytes 2949120 | tf_op jit(solution)/shard_map/reduce_scatter | solution.py:901
  430.3 35.3 %collective-permute-start.46 = (bf16[384,1536]{1,0:T(8,128)(2,1)}, bf16[384,1536]{1,0:T(8,128)(2,1)}, u32[]{:S(2)}, u32[]{:S(2)}) collective-permute-start(bf16[384,1536]{1,0:T(8,128)(2,1)} %merge.16), channel_id=1, source_target_pairs={{0,1},{1,0},{8,9},{9,8},{16,17},{17,16},{24,25},{25,24},{2,3},{3,2... | collective-permute-start | bytes 3538952 | tf_op jit(solution)/shard_map/ppermute | solution.py:28
  431.4 34.3 %collective-permute-start.47 = (bf16[384,1536]{1,0:T(8,128)(2,1)}, bf16[384,1536]{1,0:T(8,128)(2,1)}, u32[]{:S(2)}, u32[]{:S(2)}) collective-permute-start(bf16[384,1536]{1,0:T(8,128)(2,1)} %merge.17), channel_id=1, source_target_pairs={{0,16},{1,17},{8,24},{9,25},{16,0},{17,1},{24,8},{25,9},{2,18},{3,... | collective-permute-start | bytes 3538952 | tf_op jit(solution)/shard_map/ppermute | solution.py:28
  433.2 32.5 %collective-permute-start.48 = (bf16[96,1536]{1,0:T(8,128)(2,1)}, bf16[96,1536]{1,0:T(8,128)(2,1)S(1)}, u32[]{:S(2)}, u32[]{:S(2)}) collective-permute-start(bf16[96,1536]{1,0:T(8,128)(2,1)} %get-tuple-element.272), channel_id=1, source_target_pairs={{0,16},{1,17},{8,24},{9,25},{16,0},{17,1},{24,8},{25,9},{2,18},{3,... | collective-permute-start | bytes 884744 | tf_op jit(solution)/shard_map/ppermute | solution.py:28
  434.2 31.5 %collective-permute-start.49 = (bf16[96,1536]{1,0:T(8,128)(2,1)S(1)}, bf16[96,1536]{1,0:T(8,128)(2,1)S(1)}, u32[]{:S(2)}, u32[]{:S(2)}) collective-permute-start(bf16[96,1536]{1,0:T(8,128)(2,1)S(1)} %get-tuple-element.271), channel_id=1, source_target_pairs={{0,1},{1,0},{8,9},{9,8},{16,17},{17,16},{24,25},{25,24},{2,3},{3,2... | collective-permute-start | bytes 884744 | tf_op jit(solution)/shard_map/ppermute | solution.py:28
  469.8 48.2 %all-to-all-start.4 = ((bf16[8,48,1792]{2,1,0:T(8,128)(2,1)}), bf16[8,48,1792]{2,1,0:T(8,128)(2,1)}, u32[]{:S(2)}, u32[]{:S(2)}) async-start(bf16[8,48,1792]{2,1,0:T(8,128)(2,1)} %bitcast.152), calls=%async_computation.6 | async-start | bytes 2752512 | tf_op jit(solution)/shard_map/all_to_all | solution.py:904
  474.6 114.3 %reduce-scatter.8.cloned.1.call-start = ((), (), s32[]{:S(2)}) async-start(), calls=%async_computation.14 | async-start | bytes 3317760 | tf_op jit(solution)/shard_map/reduce_scatter | solution.py:915
  480.8 36.4 %collective-permute-start.53 = (bf16[192,1536]{1,0:T(8,128)(2,1)S(1)}, bf16[192,1536]{1,0:T(8,128)(2,1)S(1)}, u32[]{:S(2)}, u32[]{:S(2)}) collective-permute-start(bf16[192,1536]{1,0:T(8,128)(2,1)S(1)} %merge.22), channel_id=1, source_target_pairs={{0,1},{1,0},{8,9},{9,8},{16,17},{17,16},{24,25},{25,24},{2,3},{3,2... | collective-permute-start | bytes 1769480 | tf_op jit(solution)/shard_map/ppermute | solution.py:28
  482.3 35.8 %collective-permute-start.54 = (bf16[192,1536]{1,0:T(8,128)(2,1)S(1)}, bf16[192,1536]{1,0:T(8,128)(2,1)}, u32[]{:S(2)}, u32[]{:S(2)}) collective-permute-start(bf16[192,1536]{1,0:T(8,128)(2,1)S(1)} %merge.23), channel_id=1, source_target_pairs={{0,16},{1,17},{8,24},{9,25},{16,0},{17,1},{24,8},{25,9},{2,18},{3,... | collective-permute-start | bytes 1769480 | tf_op jit(solution)/shard_map/ppermute | solution.py:28
  532.4 44.9 %collective-permute-start.55 = (bf16[384,1536]{1,0:T(8,128)(2,1)}, bf16[384,1536]{1,0:T(8,128)(2,1)}, u32[]{:S(2)}, u32[]{:S(2)}) collective-permute-start(bf16[384,1536]{1,0:T(8,128)(2,1)} %merge.20), channel_id=1, source_target_pairs={{0,1},{1,0},{8,9},{9,8},{16,17},{17,16},{24,25},{25,24},{2,3},{3,2... | collective-permute-start | bytes 3538952 | tf_op jit(solution)/shard_map/ppermute | solution.py:28
  533.9 43.5 %collective-permute-start.56 = (bf16[384,1536]{1,0:T(8,128)(2,1)}, bf16[384,1536]{1,0:T(8,128)(2,1)}, u32[]{:S(2)}, u32[]{:S(2)}) collective-permute-start(bf16[384,1536]{1,0:T(8,128)(2,1)} %merge.21), channel_id=1, source_target_pairs={{0,16},{1,17},{8,24},{9,25},{16,0},{17,1},{24,8},{25,9},{2,18},{3,... | collective-permute-start | bytes 3538952 | tf_op jit(solution)/shard_map/ppermute | solution.py:28
  534.4 42.9 %all-to-all-start.5 = ((bf16[8,48,768]{2,1,0:T(8,128)(2,1)}), bf16[8,48,768]{2,1,0:T(8,128)(2,1)S(1)}, u32[]{:S(2)}, u32[]{:S(2)}) async-start(bf16[8,48,768]{2,1,0:T(8,128)(2,1)} %bitcast.155), calls=%async_computation.7 | async-start | bytes 1179648 | tf_op jit(solution)/shard_map/all_to_all | solution.py:917
  542.9 32.5 %collective-permute-start.61 = (bf16[48,1536]{1,0:T(8,128)(2,1)}, bf16[48,1536]{1,0:T(8,128)(2,1)}, u32[]{:S(2)}, u32[]{:S(2)}) collective-permute-start(bf16[48,1536]{1,0:T(8,128)(2,1)} %get-tuple-element.270), channel_id=1, source_target_pairs={{0,6},{2,4},{6,0},{4,2},{1,7},{3,5},{7,1},{5,3},{8,14},{10,12},{14... | collective-permute-start | bytes 442376 | tf_op jit(solution)/shard_map/ppermute | solution.py:220
  544.1 31.3 %collective-permute-start.60 = (bf16[48,1536]{1,0:T(8,128)(2,1)}, bf16[48,1536]{1,0:T(8,128)(2,1)}, u32[]{:S(2)}, u32[]{:S(2)}) collective-permute-start(bf16[48,1536]{1,0:T(8,128)(2,1)} %get-tuple-element.268), channel_id=1, source_target_pairs={{0,4},{2,0},{6,2},{4,6},{1,5},{3,1},{7,3},{5,7},{8,12},{10,8},{14,... | collective-permute-start | bytes 442376 | tf_op jit(solution)/shard_map/ppermute | solution.py:220
  (111 other events, 1319.9 us)
Sparse Core Ops, SparseCore 0:
  25.6 54.7 all-gather.3
  81.9 100.9 all-gather.5
  185.1 53.7 all-gather.7
  371.3 98.4 reduce-scatter.3
  472.0 47.4 reduce-scatter.5
  521.6 65.0 reduce-scatter.7

commit v5 on v4

--- a/solution.py
+++ b/solution.py
@@ -214,7 +214,7 @@
 
     def reduce_direct(self, parts, axis, steps=None):
         terms = [lax.dynamic_index_in_dim(parts, self.source[0], axis, keepdims=False)]
-        for s in steps or range(1, self.count):
+        for s in range(1, self.count) if steps is None else steps:
             part = lax.dynamic_index_in_dim(parts, self.source[s], axis, keepdims=False)
             route = [(self.ring[i], self.ring[(i - s) % self.count]) for i in range(self.count)]
             terms.append(lax.ppermute(part, "z", route))
@@ -511,10 +511,13 @@
 
     @pl.when(step == pl.num_programs(0) - 1)
     def _():
-        d_part[...] = total[...].astype(BF)
-
-
-def mix_backward(do_all, do_rim, a_all, bcx, w_in, taps, nat, sides, slots, span, edge):
+        chan = d_part.shape[1] // 3
+        d_part[...] = jnp.concatenate(
+            [total[:, i * cpad : i * cpad + chan].astype(BF) for i in range(3)], axis=1
+        )
+
+
+def mix_backward(do_all, do_rim, a_all, bcx, w_in, taps, nat, sides, slots, span, edge, chan):
     width = w_in.shape[0]
     cpad = w_in.shape[1] // 3
     rows = slots * span
@@ -546,7 +549,7 @@
                 fixed(taps.shape),
             ],
             out_specs=[
-                fixed((width, 3 * cpad)),
+                fixed((width, 3 * chan)),
                 pl.BlockSpec((1, 2, rows, width), lambda i, r: (jnp.maximum(i - chips, 0), 0, 0, 0)),
                 pl.BlockSpec((1, 2, rows, width), lambda i, r: (jnp.minimum(i, chips - 1), 0, 0, 0)),
                 fixed((8, cpad)),
@@ -554,7 +557,7 @@
             scratch_shapes=[pltpu.VMEM((width, 3 * cpad), F32), pltpu.VMEM((2 * rows, 3 * cpad), BF)],
         ),
         out_shape=[
-            jax.ShapeDtypeStruct((width, 3 * cpad), BF),
+            jax.ShapeDtypeStruct((width, 3 * chan), BF),
             da_shape,
             da_shape,
             jax.ShapeDtypeStruct((8, cpad), F32),
@@ -670,7 +673,7 @@
         + [pl.BlockSpec(gain.shape, lambda i: (0, 0))],
         out_specs=spec,
         out_shape=jax.ShapeDtypeStruct((rows, width), F32),
-        compiler_params=pltpu.CompilerParams(vmem_limit_bytes=40 * 2**20),
+        compiler_params=pltpu.CompilerParams(vmem_limit_bytes=60 * 2**20),
         cost_estimate=pl.CostEstimate(flops=rows * width * 8, bytes_accessed=12 * 2**20, transcendentals=0),
         name="finish",
     )(*terms, x, dh1, gain)
@@ -889,7 +892,7 @@
     f.send_near()
     out.send_far()
     in_part, da_near, da_far, conv_part = mix_backward(
-        do_all, do_rim, a_all, bcx, w_in, taps, nat, sides, slots, span, edge
+        do_all, do_rim, a_all, bcx, w_in, taps, nat, sides, slots, span, edge, chan
     )
     (in_part, da_near, da_far, conv_part), f.last, out.more = hold(
         ((in_part, da_near, da_far, conv_part), f.last, out.more)
@@ -899,7 +902,7 @@
     da = GroupSum(da_near.reshape(flat), da_far.reshape(flat), sizes)
     in_part, both_sum = hold((in_part, both_sum))
     in_sum = lax.psum_scatter(
-        in_part.reshape(ndp, nz * ny * own_in, 3 * cpad), "z", scatter_dimension=1, tiled=True
+        in_part.reshape(ndp, nz * ny * own_in, 3 * chan), "z", scatter_dimension=1, tiled=True
     )
     both_sum = lax.all_to_all(both_sum.reshape(ndp * ny, own_in, 2 * hpad), GROUP, 0, 0, tiled=True)
     da.cross = hold(da.cross)
@@ -914,23 +917,23 @@
     in_sum, down_part = after(in_sum, down_part)
     down_grad = lax.psum_scatter(down_part, "z", scatter_dimension=0, tiled=True)
     da.send_near()
-    in_sum = lax.all_to_all(in_sum.reshape(ndp * ny, own_in, 3 * cpad), GROUP, 0, 0, tiled=True)
+    in_sum = lax.all_to_all(in_sum.reshape(ndp * ny, own_in, 3 * chan), GROUP, 0, 0, tiled=True)
     out_sum = sum(term[0].astype(F32) for term in out.terms()).astype(BF)
     out_grad = line.reduce_direct(out_sum.reshape(nz, own_in, width), 0)
     conv_grad = line.reduce_direct(conv_part[:3, :chan].reshape(3, nz, own_in), 1)
+    (gate_grad, up_grad), gain_two_grad = join_columns(
+        both_sum, [gate_weight, up_weight], gain_two, own_hid, hpad, plan
+    )
+    in_sum, da.last, f.last, gate_grad, up_grad = hold((in_sum, da.last, f.last, gate_grad, up_grad))
     total = h1
     for term in f.terms():
         total = total + term[0].astype(F32)
     mixed = (mask * total).astype(BF)
-    (gate_grad, up_grad), gain_two_grad = join_columns(
-        both_sum, [gate_weight, up_weight], gain_two, own_hid, hpad, plan
-    )
-    in_sum, da.last, mixed, gate_grad, up_grad = hold((in_sum, da.last, mixed, gate_grad, up_grad))
 
     input_grad = finish(da.terms(), x_bf, dh1, gain_a, block)
     out_grad = sum(term.astype(F32) for term in out_grad)
     conv_grad = sum(conv_grad)
-    (in_grad,), gain_one_grad = join_columns(in_sum, [in_weight], gain_one, own_in, cpad, plan)
+    (in_grad,), gain_one_grad = join_columns(in_sum, [in_weight], gain_one, own_in, chan, plan)
     down_grad = down_grad.astype(F32)
     return (
         mixed.reshape(slots, span, width),

time: 608 us -> 600 us (0.987)
  the two profiles are of different devices: /device:TPU:10 before, /device:TPU:0 now
where the time goes in v5:
time: 600 us; the launch traced here: 589 us
  waiting for transfers between devices  193 us (32%)
  Pallas kernels  179 us (30%)
  starting transfers between devices  81.8 us (14%)
  local copies, waits for them, and re-layouts  58.7 us (10%)
  matrix products  39.4 us (7%)
  other arithmetic  21.4 us (4%)
  between operations  15.7 us (3%)
    ppermute x52, waiting for transfers between devices, send(): return lax.ppermute(block, GROUP, route)  111 us
    pallas_call x2, Pallas kernels, feed(): pl.pallas_call(lambda *refs: feed_body(hid, hpad, *refs), grid=(half,), i...  66.3 us
    dot_general x3, matrix products, dot_tn(): lax.dot_general(left, right, (((0,), (0,)), ((), ())), preferred_element_...  39.4 us
    ppermute x52, starting transfers between devices, send(): return lax.ppermute(block, GROUP, route)  39 us
    all_to_all x1, waiting for transfers between devices, on_device(): lax.all_to_all(both, GROUP, 0, 0, tiled=True)  32.6 us
    unnamed x145, local copies, waits for them, and re-layouts  31.7 us
    pallas_call x1, Pallas kernels, mix_backward(): pl.pallas_call(lambda *refs: mix_backward_body(cpad, slots, span, edge, *...  28.6 us
    pallas_call x5, Pallas kernels, stack(): pl.pallas_call(body, in_specs=[pl.BlockSpec(memory_space=pl.ANY)] * (here...  23 us
  transfers between devices with their start and end apart: 75, of which 37 were waited for; matrix products, arithmetic and copies ran while one was open for 15% of the time, Pallas kernels for 24%

profile of v5, /device:TPU:0, one launch (start us, length us, event | category | flops | bytes accessed | tf_op | source)
XLA Modules:
  0.0 589.4 jit_solution(4265847771103009550)
XLA Ops:
  10.3 5.2 all-to-all-start
  17.4 7.7 %all-to-all-done = bf16[8,48,768]{2,1,0:T(8,128)(2,1)S(1)} async-done(((bf16[8,48,768]{2,1,0:T(8,128)(2,1)}), bf16[8,48,768]{2,1,0:T(8,128)(2,1)S(1)}, u32[]{:S(2)}, u32[]{:S(2)}) %all-to-all-start) | async-done | bytes 589856 | tf_op jit(solution)/shard_map/all_to_all | solution.py:801
  37.7 3.6 all-to-all-start.1
  45.0 32.6 %all-to-all-done.1 = bf16[8,48,1792]{2,1,0:T(8,128)(2,1)S(1)} async-done(((bf16[8,48,1792]{2,1,0:T(8,128)(2,1)}), bf16[8,48,1792]{2,1,0:T(8,128)(2,1)S(1)}, u32[]{:S(2)}, u32[]{:S(2)}) %all-to-all-start.1) | async-done | bytes 1376288 | tf_op jit(solution)/shard_map/all_to_all | solution.py:817
  84.9 10.8 %collective-permute-done.8 = bf16[200,1536]{1,0:T(8,128)(2,1)S(1)} collective-permute-done((bf16[200,1536]{1,0:T(8,128)(2,1)S(1)}, bf16[200,1536]{1,0:T(8,128)(2,1)S(1)}, u32[]{:S(2)}, u32[]{:S(2)}) %collective-permute-start.8) | collective-permute-done | bytes 614432 | tf_op jit(solution)/shard_map/ppermute | solution.py:28
  105.7 4.1 stack.105.refs_4_
  109.8 3.9 stack.106.refs_1_.refs_2_.refs_3_.refs_4_
  116.1 16.0 %mix_forward.1 = (bf16[4,2,384,1536]{3,2,1,0:T(8,128)(2,1)}, f32[4,800,768]{2,1,0:T(8,128)}, bf16[4,2,384,256]{3,2,1,0:T(8,128)(2,1)}) custom-call(s32[8]{0:T(128)} %stack.90.refs_0_, bf16[8,400,1536]{2,1,0:T(8,128)(2,1)} %stack.106.refs_1_.refs_2_.refs_3_.refs_4_, bf16[8,400,1536]{2,1,0:T(8,128)(2,1)} %stack.106.refs_1_.refs_2_.refs_3_.refs_4_, ...), custom_call_target="tpu_custom_call" | custom-call | flops 7549747200 | bytes 33554432 | tf_op jit(solution)/shard_map/mix_forward/pallas_call | solution.py:415
  132.1 4.3 all-to-all-start.2
  144.8 21.2 %collective-permute-done.14 = bf16[96,1536]{1,0:T(8,128)(2,1)S(1)} collective-permute-done((bf16[96,1536]{1,0:T(8,128)(2,1)S(1)}, bf16[96,1536]{1,0:T(8,128)(2,1)S(1)}, u32[]{:S(2)}, u32[]{:S(2)}) %collective-permute-start.14) | collective-permute-done | bytes 294944 | tf_op jit(solution)/shard_map/ppermute | solution.py:28
  182.0 4.3 attend.1
  195.7 25.0 %collective-permute-done.20.refs_1_ = bf16[384,1536]{1,0:T(8,128)(2,1)S(1)} collective-permute-done((bf16[384,1536]{1,0:T(8,128)(2,1)S(1)}, bf16[384,1536]{1,0:T(8,128)(2,1)S(1)}, u32[]{:S(2)}, u32[]{:S(2)}) %collective-permute-start.20) | collective-permute-done | bytes 1179680 | tf_op jit(solution)/shard_map/ppermute | solution.py:28
  225.5 7.5 %stack.107.refs_1_ = bf16[8,384,1536]{2,1,0:T(8,128)(2,1)} custom-call(bf16[384,1536]{1,0:T(8,128)(2,1)} %copy-done.11, bf16[384,1536]{1,0:T(8,128)(2,1)} %copy-done.39, bf16[384,1536]{1,0:T(8,128)(2,1)} %collective-permute-done.25.refs_2_, bf16[384,1536]{1,0:T(8,128)(2,1)} %copy-done.42, bf16[384,1536]{1,0:T(8,128)(2,1)} %collective-permute-done.23.refs_4_, ...), custom_call_target="tpu_custom_call" | custom-call | bytes 18874368 | tf_op jit(solution)/shard_map/stack/pallas_call | solution.py:91
  241.1 3.8 stack.108.refs_4_
  248.2 3.8 stack.109.refs_0_
  252.0 33.2 %feed.2 = (bf16[8,384,864]{2,1,0:T(8,128)(2,1)}, bf16[8,384,1792]{2,1,0:T(8,128)(2,1)}, bf16[4,384,1536]{2,1,0:T(8,128)(2,1)}, bf16[4,384,1536]{2,1,0:T(8,128)(2,1)}) custom-call(bf16[8,384,1536]{2,1,0:T(8,128)(2,1)} %stack.109.refs_0_, bf16[8,384,1536]{2,1,0:T(8,128)(2,1)} %stack.107.refs_1_, bf16[1536,1792]{1,0:T(8,128)(2,1)} %bitcast.163, ...), custom_call_target="tpu_custom_call" | custom-call | flops 24461180928 | bytes 41943040 | tf_op jit(solution)/shard_map/feed/pallas_call | solution.py:713
  285.7 33.1 %feed.3 = (bf16[8,384,864]{2,1,0:T(8,128)(2,1)}, bf16[8,384,1792]{2,1,0:T(8,128)(2,1)}, bf16[4,384,1536]{2,1,0:T(8,128)(2,1)}, bf16[4,384,1536]{2,1,0:T(8,128)(2,1)}) custom-call(bf16[8,384,1536]{2,1,0:T(8,128)(2,1)} %stack.109.refs_0_, bf16[8,384,1536]{2,1,0:T(8,128)(2,1)} %stack.107.refs_1_, ...), custom_call_target="tpu_custom_call", output_to_operand_aliasing={{0}: (4, {}), {1}: (5, {})} | custom-call | flops 24461180928 | bytes 41943040 | tf_op jit(solution)/shard_map/feed/pallas_call | solution.py:713
  325.3 12.4 %bitcast_convert_fusion.1 = bf16[864,1536]{1,0:T(8,128)(2,1)} fusion(bf16[8,384,864]{2,1,0:T(8,128)(2,1)S(1)} %copy-done.62, bf16[8,384,1536]{2,1,0:T(8,128)(2,1)} %stack.107.refs_1_), kind=kOutput, calls=%fused_computation.2 | convolution fusion | flops 8155054080 | bytes 17399808 | tf_op jit(solution)/shard_map/dot_general | solution.py:233
  347.8 23.3 %bitcast_convert_fusion = bf16[1536,1792]{1,0:T(8,128)(2,1)} fusion(bf16[8,384,1536]{2,1,0:T(8,128)(2,1)S(1)} %bitcast.137, bf16[8,384,1792]{2,1,0:T(8,128)(2,1)} %get-tuple-element.192), kind=kOutput, calls=%fused_computation | convolution fusion | flops 16914186240 | bytes 25952256 | tf_op jit(solution)/shard_map/dot_general | solution.py:233
  379.4 9.1 %turn.1 = (f32[384,1536]{1,0:T(8,128)S(1)}, bf16[384,1536]{1,0:T(8,128)(2,1)S(1)}, bf16[8,384,256]{2,1,0:T(8,128)(2,1)S(1)}) custom-call(bf16[4,384,1536]{2,1,0:T(8,128)(2,1)} %get-tuple-element.181.refs_0_, bf16[4,384,1536]{2,1,0:T(8,128)(2,1)} %collective-permute-done.36.refs_1_, bf16[1,384,1536]{2,1,0:T(8,128)(2,1)S(1)} %bitcast.134, ...), custom_call_target="tpu_custom_call" | custom-call | flops 2415919104 | bytes 20971520 | tf_op jit(solution)/shard_map/turn/pallas_call | solution.py:637
  391.2 3.7 convolution_convert_fusion
  398.5 4.4 all-to-all-start.3
  410.7 12.4 %all-to-all-done.3.refs_1_.refs_2_ = bf16[8,384,256]{2,1,0:T(8,128)(2,1)} async-done(((bf16[8,384,256]{2,1,0:T(8,128)(2,1)}), bf16[8,384,256]{2,1,0:T(8,128)(2,1)}, u32[]{:S(2)}, u32[]{:S(2)}) %all-to-all-start.3) | async-done | bytes 1572896 | tf_op jit(solution)/shard_map/all_to_all | solution.py:880
  437.2 28.6 %mix_backward.1 = (bf16[1536,576]{1,0:T(8,128)(2,1)}, bf16[2,2,384,1536]{3,2,1,0:T(8,128)(2,1)}, bf16[2,2,384,1536]{3,2,1,0:T(8,128)(2,1)}, f32[8,256]{1,0:T(8,128)}) custom-call(s32[8]{0:T(128)} %stack.102.refs_0_, bf16[8,384,256]{2,1,0:T(8,128)(2,1)} %all-to-all-done.3.refs_1_.refs_2_, bf16[8,384,256]{2,1,0:T(8,128)(2,1)} %all-to-all-done.3.refs_1_.refs_2_, ...), custom_call_target="tpu_custom_call" | custom-call | flops 14495514624 | bytes 41943040 | tf_op jit(solution)/shard_map/mix_backward/pallas_call | solution.py:537
  469.8 4.3 all-to-all-start.4
  485.6 19.6 %collective-permute-done.51.refs_2_ = bf16[192,1536]{1,0:T(8,128)(2,1)S(1)} collective-permute-done((bf16[192,1536]{1,0:T(8,128)(2,1)S(1)}, bf16[192,1536]{1,0:T(8,128)(2,1)S(1)}, u32[]{:S(2)}, u32[]{:S(2)}) %collective-permute-start.51) | collective-permute-done | bytes 589856 | tf_op jit(solution)/shard_map/ppermute | solution.py:28
  508.8 8.4 %collective-permute-done.53 = bf16[192,1536]{1,0:T(8,128)(2,1)S(1)} collective-permute-done((bf16[192,1536]{1,0:T(8,128)(2,1)S(1)}, bf16[192,1536]{1,0:T(8,128)(2,1)S(1)}, u32[]{:S(2)}, u32[]{:S(2)}) %collective-permute-start.53) | collective-permute-done | bytes 589856 | tf_op jit(solution)/shard_map/ppermute | solution.py:28
  532.7 3.8 all-to-all-start.5
  540.6 8.8 %collective-permute-done.62 = bf16[48,1536]{1,0:T(8,128)(2,1)} collective-permute-done((bf16[48,1536]{1,0:T(8,128)(2,1)}, bf16[48,1536]{1,0:T(8,128)(2,1)}, u32[]{:S(2)}, u32[]{:S(2)}) %collective-permute-start.62) | collective-permute-done | bytes 147488 | tf_op jit(solution)/shard_map/ppermute | solution.py:220
  557.8 5.8 finish.1
  563.7 4.2 fusion.3
  567.9 11.8 %reduce-scatter.8.cloned.1.call-done = bf16[216,1536]{1,0:T(8,128)(2,1)} async-done(((bf16[864,1536]{1,0:T(8,128)(2,1)}), bf16[216,1536]{1,0:T(8,128)(2,1)}) %reduce-scatter.8.cloned.1.call-update) | async-done | bytes 663568 | tf_op jit(solution)/shard_map/reduce_scatter | solution.py:918
  (376 shorter events, 193.1 us)
Async XLA Ops:
  15.5 98.2 %all-gather.4.cloned.1.call-start = ((), (), s32[]{:S(2)}) async-start(), calls=%async_computation.9 | async-start | bytes 2949120 | tf_op jit(solution)/shard_map/all_gather | solution.py:810
  34.1 43.5 %collective-permute-start.1 = (bf16[400,1536]{1,0:T(8,128)(2,1)}, bf16[400,1536]{1,0:T(8,128)(2,1)}, u32[]{:S(2)}, u32[]{:S(2)}) collective-permute-start(bf16[400,1536]{1,0:T(8,128)(2,1)} %constant_dynamic-update-slice_fusion.refs_0_), channel_id=1, source_target_pairs={{0,1},{1,0},{8,9},{9,8},{16,17},{17,16},{24,25},{25,24},{2,3},{3,2... | collective-permute-start | bytes 3686408 | tf_op jit(solution)/shard_map/ppermute | solution.py:28
  35.1 42.5 %collective-permute-start.2 = (bf16[400,1536]{1,0:T(8,128)(2,1)}, bf16[400,1536]{1,0:T(8,128)(2,1)}, u32[]{:S(2)}, u32[]{:S(2)}) collective-permute-start(bf16[400,1536]{1,0:T(8,128)(2,1)} %constant_dynamic-update-slice_fusion.refs_0_), channel_id=1, source_target_pairs={{0,16},{1,17},{8,24},{9,25},{16,0},{17,1},{24,8},{25,9},{2,18},{3,... | collective-permute-start | bytes 3686408 | tf_op jit(solution)/shard_map/ppermute | solution.py:28
  37.7 39.9 %all-to-all-start.1 = ((bf16[8,48,1792]{2,1,0:T(8,128)(2,1)}), bf16[8,48,1792]{2,1,0:T(8,128)(2,1)S(1)}, u32[]{:S(2)}, u32[]{:S(2)}) async-start(bf16[8,48,1792]{2,1,0:T(8,128)(2,1)} %cut_columns.3), calls=%async_computation.1 | async-start | bytes 2752512 | tf_op jit(solution)/shard_map/all_to_all | solution.py:817
  41.2 147.6 %all-gather.6.cloned.1.call-start = ((), (), s32[]{:S(2)}) async-start(), calls=%async_computation.10 | async-start | bytes 6881280 | tf_op jit(solution)/shard_map/all_gather | solution.py:820
  101.5 30.6 %collective-permute-start.12 = (bf16[192,1536]{1,0:T(8,128)(2,1)}, bf16[192,1536]{1,0:T(8,128)(2,1)}, u32[]{:S(2)}, u32[]{:S(2)}) collective-permute-start(bf16[192,1536]{1,0:T(8,128)(2,1)} %slice.116), channel_id=1, source_target_pairs={{0,1},{1,0},{8,9},{9,8},{16,17},{17,16},{24,25},{25,24},{2,3},{3,2... | collective-permute-start | bytes 1769480 | tf_op jit(solution)/shard_map/ppermute | solution.py:28
  103.3 28.8 %collective-permute-start.13 = (bf16[192,1536]{1,0:T(8,128)(2,1)}, bf16[192,1536]{1,0:T(8,128)(2,1)}, u32[]{:S(2)}, u32[]{:S(2)}) collective-permute-start(bf16[192,1536]{1,0:T(8,128)(2,1)} %slice.116), channel_id=1, source_target_pairs={{0,16},{1,17},{8,24},{9,25},{16,0},{17,1},{24,8},{25,9},{2,18},{3,... | collective-permute-start | bytes 1769480 | tf_op jit(solution)/shard_map/ppermute | solution.py:28
  105.0 68.9 %collective-permute-start.22 = (bf16[384,1536]{1,0:T(8,128)(2,1)S(1)}, bf16[384,1536]{1,0:T(8,128)(2,1)S(1)}, u32[]{:S(2)}, u32[]{:S(2)}) collective-permute-start(bf16[384,1536]{1,0:T(8,128)(2,1)S(1)} %fusion.4.refs_0_.refs_4_), channel_id=1, source_target_pairs={{0,1},{1,0},{8,9},{9,8},{16,17},{17,16},{24,25},{25,24},{2,3},{3,2... | collective-permute-start | bytes 3538952 | tf_op jit(solution)/shard_map/ppermute | solution.py:28
  105.3 87.7 %collective-permute-start.23 = (bf16[384,1536]{1,0:T(8,128)(2,1)S(1)}, bf16[384,1536]{1,0:T(8,128)(2,1)}, u32[]{:S(2)}, u32[]{:S(2)}) collective-permute-start(bf16[384,1536]{1,0:T(8,128)(2,1)S(1)} %fusion.4.refs_0_.refs_4_), channel_id=1, source_target_pairs={{0,8},{1,9},{8,0},{9,1},{16,24},{17,25},{24,16},{25,17},{2,10},{3,... | collective-permute-start | bytes 3538952 | tf_op jit(solution)/shard_map/ppermute | solution.py:28
  105.3 65.3 %collective-permute-start.25 = (bf16[384,1536]{1,0:T(8,128)(2,1)S(1)}, bf16[384,1536]{1,0:T(8,128)(2,1)}, u32[]{:S(2)}, u32[]{:S(2)}) collective-permute-start(bf16[384,1536]{1,0:T(8,128)(2,1)S(1)} %fusion.4.refs_0_.refs_4_), channel_id=1, source_target_pairs={{0,16},{1,17},{8,24},{9,25},{16,0},{17,1},{24,8},{25,9},{2,18},{3,... | collective-permute-start | bytes 3538952 | tf_op jit(solution)/shard_map/ppermute | solution.py:28
  132.1 47.1 %all-to-all-start.2 = ((bf16[8,384,256]{2,1,0:T(8,128)(2,1)}), bf16[8,384,256]{2,1,0:T(8,128)(2,1)}, u32[]{:S(2)}, u32[]{:S(2)}) async-start(bf16[8,384,256]{2,1,0:T(8,128)(2,1)} %bitcast.151), calls=%async_computation.2 | async-start | bytes 3145728 | tf_op jit(solution)/shard_map/all_to_all | solution.py:833
  136.4 115.5 %all-gather.8.cloned.1.call-start = ((), (), s32[]{:S(2)}) async-start(), calls=%async_computation.11 | async-start | bytes 3317760 | tf_op jit(solution)/shard_map/all_gather | solution.py:845
  137.5 28.5 %collective-permute-start.14 = (bf16[96,1536]{1,0:T(8,128)(2,1)S(1)}, bf16[96,1536]{1,0:T(8,128)(2,1)S(1)}, u32[]{:S(2)}, u32[]{:S(2)}) collective-permute-start(bf16[96,1536]{1,0:T(8,128)(2,1)S(1)} %slice.94), channel_id=1, source_target_pairs={{0,1},{1,0},{8,9},{9,8},{16,17},{17,16},{24,25},{25,24},{2,3},{3,2... | collective-permute-start | bytes 884744 | tf_op jit(solution)/shard_map/ppermute | solution.py:28
  140.4 27.2 %collective-permute-start.15 = (bf16[96,1536]{1,0:T(8,128)(2,1)S(1)}, bf16[96,1536]{1,0:T(8,128)(2,1)S(1)}, u32[]{:S(2)}, u32[]{:S(2)}) collective-permute-start(bf16[96,1536]{1,0:T(8,128)(2,1)S(1)} %slice.95), channel_id=1, source_target_pairs={{0,16},{1,17},{8,24},{9,25},{16,0},{17,1},{24,8},{25,9},{2,18},{3,... | collective-permute-start | bytes 884744 | tf_op jit(solution)/shard_map/ppermute | solution.py:28
  188.9 280.9 %reduce-scatter.4.cloned.1.call-start = ((), (), s32[]{:S(2)}) async-start(), calls=%async_computation.12 | async-start | bytes 6881280 | tf_op jit(solution)/shard_map/reduce_scatter | solution.py:870
  192.4 28.3 %collective-permute-start.20 = (bf16[384,1536]{1,0:T(8,128)(2,1)S(1)}, bf16[384,1536]{1,0:T(8,128)(2,1)S(1)}, u32[]{:S(2)}, u32[]{:S(2)}) collective-permute-start(bf16[384,1536]{1,0:T(8,128)(2,1)S(1)} %get-tuple-element.170.refs_0_), channel_id=1, source_target_pairs={{0,1},{1,0},{8,9},{9,8},{16,17},{17,16},{24,25},{25,24},{2,3},{3,2... | collective-permute-start | bytes 3538952 | tf_op jit(solution)/shard_map/ppermute | solution.py:28
  193.1 28.1 %collective-permute-start.21 = (bf16[384,1536]{1,0:T(8,128)(2,1)S(1)}, bf16[384,1536]{1,0:T(8,128)(2,1)}, u32[]{:S(2)}, u32[]{:S(2)}) collective-permute-start(bf16[384,1536]{1,0:T(8,128)(2,1)S(1)} %get-tuple-element.170.refs_0_), channel_id=1, source_target_pairs={{0,16},{1,17},{8,24},{9,25},{16,0},{17,1},{24,8},{25,9},{2,18},{3,... | collective-permute-start | bytes 3538952 | tf_op jit(solution)/shard_map/ppermute | solution.py:28
  285.2 33.6 %collective-permute-start.36 = (bf16[4,384,1536]{2,1,0:T(8,128)(2,1)}, bf16[4,384,1536]{2,1,0:T(8,128)(2,1)}, u32[]{:S(2)}, u32[]{:S(2)}) collective-permute-start(bf16[4,384,1536]{2,1,0:T(8,128)(2,1)} %get-tuple-element.182), channel_id=1, source_target_pairs={{0,8},{1,9},{8,0},{9,1},{16,24},{17,25},{24,16},{25,17},{2,10},{3,... | collective-permute-start | bytes 14155784 | tf_op jit(solution)/shard_map/ppermute | solution.py:28
  285.3 52.4 %collective-permute-start.39 = (bf16[4,384,1536]{2,1,0:T(8,128)(2,1)}, bf16[4,384,1536]{2,1,0:T(8,128)(2,1)}, u32[]{:S(2)}, u32[]{:S(2)}) collective-permute-start(bf16[4,384,1536]{2,1,0:T(8,128)(2,1)} %get-tuple-element.185), channel_id=1, source_target_pairs={{0,8},{1,9},{8,0},{9,1},{16,24},{17,25},{24,16},{25,17},{2,10},{3,... | collective-permute-start | bytes 14155784 | tf_op jit(solution)/shard_map/ppermute | solution.py:28
  345.5 26.9 %collective-permute-start.40 = (bf16[384,1536]{1,0:T(8,128)(2,1)S(1)}, bf16[384,1536]{1,0:T(8,128)(2,1)S(1)}, u32[]{:S(2)}, u32[]{:S(2)}) collective-permute-start(bf16[384,1536]{1,0:T(8,128)(2,1)S(1)} %merge.13), channel_id=1, source_target_pairs={{0,1},{1,0},{8,9},{9,8},{16,17},{17,16},{24,25},{25,24},{2,3},{3,2... | collective-permute-start | bytes 3538952 | tf_op jit(solution)/shard_map/ppermute | solution.py:28
  346.9 26.6 %collective-permute-start.41 = (bf16[384,1536]{1,0:T(8,128)(2,1)S(1)}, bf16[384,1536]{1,0:T(8,128)(2,1)S(1)}, u32[]{:S(2)}, u32[]{:S(2)}) collective-permute-start(bf16[384,1536]{1,0:T(8,128)(2,1)S(1)} %merge.14), channel_id=1, source_target_pairs={{0,16},{1,17},{8,24},{9,25},{16,0},{17,1},{24,8},{25,9},{2,18},{3,... | collective-permute-start | bytes 3538952 | tf_op jit(solution)/shard_map/ppermute | solution.py:28
  402.9 115.1 %reduce-scatter.6.cloned.1.call-start = ((), (), s32[]{:S(2)}) async-start(), calls=%async_computation.13 | async-start | bytes 2457600 | tf_op jit(solution)/shard_map/reduce_scatter | solution.py:904
  432.3 36.0 %collective-permute-start.46 = (bf16[384,1536]{1,0:T(8,128)(2,1)}, bf16[384,1536]{1,0:T(8,128)(2,1)}, u32[]{:S(2)}, u32[]{:S(2)}) collective-permute-start(bf16[384,1536]{1,0:T(8,128)(2,1)} %merge.16), channel_id=1, source_target_pairs={{0,1},{1,0},{8,9},{9,8},{16,17},{17,16},{24,25},{25,24},{2,3},{3,2... | collective-permute-start | bytes 3538952 | tf_op jit(solution)/shard_map/ppermute | solution.py:28
  433.8 34.4 %collective-permute-start.47 = (bf16[384,1536]{1,0:T(8,128)(2,1)}, bf16[384,1536]{1,0:T(8,128)(2,1)}, u32[]{:S(2)}, u32[]{:S(2)}) collective-permute-start(bf16[384,1536]{1,0:T(8,128)(2,1)} %merge.17), channel_id=1, source_target_pairs={{0,16},{1,17},{8,24},{9,25},{16,0},{17,1},{24,8},{25,9},{2,18},{3,... | collective-permute-start | bytes 3538952 | tf_op jit(solution)/shard_map/ppermute | solution.py:28
  435.1 31.7 %collective-permute-start.48 = (bf16[96,1536]{1,0:T(8,128)(2,1)}, bf16[96,1536]{1,0:T(8,128)(2,1)S(1)}, u32[]{:S(2)}, u32[]{:S(2)}) collective-permute-start(bf16[96,1536]{1,0:T(8,128)(2,1)} %get-tuple-element.274), channel_id=1, source_target_pairs={{0,16},{1,17},{8,24},{9,25},{16,0},{17,1},{24,8},{25,9},{2,18},{3,... | collective-permute-start | bytes 884744 | tf_op jit(solution)/shard_map/ppermute | solution.py:28
  436.7 30.8 %collective-permute-start.49 = (bf16[96,1536]{1,0:T(8,128)(2,1)}, bf16[96,1536]{1,0:T(8,128)(2,1)S(1)}, u32[]{:S(2)}, u32[]{:S(2)}) collective-permute-start(bf16[96,1536]{1,0:T(8,128)(2,1)} %get-tuple-element.273), channel_id=1, source_target_pairs={{0,1},{1,0},{8,9},{9,8},{16,17},{17,16},{24,25},{25,24},{2,3},{3,2... | collective-permute-start | bytes 884744 | tf_op jit(solution)/shard_map/ppermute | solution.py:28
  469.8 48.2 %all-to-all-start.4 = ((bf16[8,48,1792]{2,1,0:T(8,128)(2,1)}), bf16[8,48,1792]{2,1,0:T(8,128)(2,1)}, u32[]{:S(2)}, u32[]{:S(2)}) async-start(bf16[8,48,1792]{2,1,0:T(8,128)(2,1)} %bitcast.152), calls=%async_computation.6 | async-start | bytes 2752512 | tf_op jit(solution)/shard_map/all_to_all | solution.py:907
  474.1 105.7 %reduce-scatter.8.cloned.1.call-start = ((), (), s32[]{:S(2)}) async-start(), calls=%async_computation.14 | async-start | bytes 3317760 | tf_op jit(solution)/shard_map/reduce_scatter | solution.py:918
  483.4 33.8 %collective-permute-start.53 = (bf16[192,1536]{1,0:T(8,128)(2,1)S(1)}, bf16[192,1536]{1,0:T(8,128)(2,1)S(1)}, u32[]{:S(2)}, u32[]{:S(2)}) collective-permute-start(bf16[192,1536]{1,0:T(8,128)(2,1)S(1)} %merge.22), channel_id=1, source_target_pairs={{0,1},{1,0},{8,9},{9,8},{16,17},{17,16},{24,25},{25,24},{2,3},{3,2... | collective-permute-start | bytes 1769480 | tf_op jit(solution)/shard_map/ppermute | solution.py:28
  484.5 33.5 %collective-permute-start.54 = (bf16[192,1536]{1,0:T(8,128)(2,1)S(1)}, bf16[192,1536]{1,0:T(8,128)(2,1)}, u32[]{:S(2)}, u32[]{:S(2)}) collective-permute-start(bf16[192,1536]{1,0:T(8,128)(2,1)S(1)} %merge.23), channel_id=1, source_target_pairs={{0,16},{1,17},{8,24},{9,25},{16,0},{17,1},{24,8},{25,9},{2,18},{3,... | collective-permute-start | bytes 1769480 | tf_op jit(solution)/shard_map/ppermute | solution.py:28
  522.8 29.8 %collective-permute-start.55 = (bf16[384,1536]{1,0:T(8,128)(2,1)}, bf16[384,1536]{1,0:T(8,128)(2,1)}, u32[]{:S(2)}, u32[]{:S(2)}) collective-permute-start(bf16[384,1536]{1,0:T(8,128)(2,1)} %copy-done.24), channel_id=1, source_target_pairs={{0,1},{1,0},{8,9},{9,8},{16,17},{17,16},{24,25},{25,24},{2,3},{3,2... | collective-permute-start | bytes 3538952 | tf_op jit(solution)/shard_map/ppermute | solution.py:28
  523.8 29.0 %collective-permute-start.56 = (bf16[384,1536]{1,0:T(8,128)(2,1)S(1)}, bf16[384,1536]{1,0:T(8,128)(2,1)}, u32[]{:S(2)}, u32[]{:S(2)}) collective-permute-start(bf16[384,1536]{1,0:T(8,128)(2,1)S(1)} %merge.21), channel_id=1, source_target_pairs={{0,16},{1,17},{8,24},{9,25},{16,0},{17,1},{24,8},{25,9},{2,18},{3,... | collective-permute-start | bytes 3538952 | tf_op jit(solution)/shard_map/ppermute | solution.py:28
  (111 other events, 1126.2 us)
Sparse Core Ops, SparseCore 0:
  26.1 56.5 all-gather.3
  84.2 102.8 all-gather.5
  189.0 53.3 all-gather.7
  373.7 96.0 reduce-scatter.3
  471.9 41.9 reduce-scatter.5
  518.2 61.5 reduce-scatter.7
